TPU v7x, 32 devices: a whole 2x2x4 slice. The times are simulated.
32 devices in a mesh: dp: 8 (over z, y), fsdp: 4 (over x, core).
Axes of the slice: x: 2, y: 2, z: 4, core: 2. Of those that a mesh axis runs over, the one named last changes fastest.
Arguments:
- inputs: bfloat16 [32, 1024, 768], P('dp', 'fsdp'), may hold values from -6 to 6
- cotangent: bfloat16 [32, 1024, 768], P('dp', 'fsdp'), may hold values from -6 to 6
- doc_lengths: int32 [32, 4], P('dp'), may hold values from 1 to 896, as said below
- labels: int32 [32, 4], P('dp'), may hold values from 0 to 2
- w_query: float32 [768, 768], P(('dp', 'fsdp')), may hold values from -0.21875 to 0.21875
- b_query: float32 [768], P(('dp', 'fsdp')), may hold values from -1.75 to 1.75
- w_key: float32 [768, 768], P(('dp', 'fsdp')), may hold values from -0.21875 to 0.21875
- w_value: float32 [768, 768], P(('dp', 'fsdp')), may hold values from -0.21875 to 0.21875
- b_value: float32 [768], P(('dp', 'fsdp')), may hold values from -1.75 to 1.75
- w_out: float32 [768, 768], P(('dp', 'fsdp')), may hold values from -1.25 to 1.25
- b_out: float32 [768], P(('dp', 'fsdp')), may hold values from -1.75 to 1.75
- first_gain: float32 [768], P(('dp', 'fsdp')), may hold values from 0.5 to 1.5
- first_shift: float32 [768], P(('dp', 'fsdp')), may hold values from -1.75 to 1.75
- w_inner: float32 [768, 3072], P(('dp', 'fsdp')), may hold values from -0.21875 to 0.21875
- b_inner: float32 [3072], P(('dp', 'fsdp')), may hold values from -1.75 to 1.75
- w_outer: float32 [3072, 768], P(('dp', 'fsdp')), may hold values from -0.109375 to 0.109375
- b_outer: float32 [768], P(('dp', 'fsdp')), may hold values from -1.75 to 1.75
- second_gain: float32 [768], P(('dp', 'fsdp')), may hold values from 0.5 to 1.5
- second_shift: float32 [768], P(('dp', 'fsdp')), may hold values from -1.75 to 1.75
- w_pool: float32 [768, 768], P(('dp', 'fsdp')), may hold values from -0.21875 to 0.21875
- b_pool: float32 [768], P(('dp', 'fsdp')), may hold values from -1.75 to 1.75
- w_class: float32 [768, 3], P(('dp', 'fsdp')), may hold values from -0.4375 to 0.4375
- b_class: float32 [3], replicated, may hold values from -3 to 3
Outputs:
- layer_out: bfloat16 [32, 1024, 768], P('dp', 'fsdp')
- logits: float32 [32, 4, 3], P('dp')
- grad_inputs: bfloat16 [32, 1024, 768], P('dp', 'fsdp')
- grad_w_query: float32 [768, 768], P(('dp', 'fsdp'))
- grad_b_query: float32 [768], P(('dp', 'fsdp'))
- grad_w_key: float32 [768, 768], P(('dp', 'fsdp'))
- grad_w_value: float32 [768, 768], P(('dp', 'fsdp'))
- grad_b_value: float32 [768], P(('dp', 'fsdp'))
- grad_w_out: float32 [768, 768], P(('dp', 'fsdp'))
- grad_b_out: float32 [768], P(('dp', 'fsdp'))
- grad_first_gain: float32 [768], P(('dp', 'fsdp'))
- grad_first_shift: float32 [768], P(('dp', 'fsdp'))
- grad_w_inner: float32 [768, 3072], P(('dp', 'fsdp'))
- grad_b_inner: float32 [3072], P(('dp', 'fsdp'))
- grad_w_outer: float32 [3072, 768], P(('dp', 'fsdp'))
- grad_b_outer: float32 [768], P(('dp', 'fsdp'))
- grad_second_gain: float32 [768], P(('dp', 'fsdp'))
- grad_second_shift: float32 [768], P(('dp', 'fsdp'))
- grad_w_pool: float32 [768, 768], P(('dp', 'fsdp'))
- grad_b_pool: float32 [768], P(('dp', 'fsdp'))
- grad_w_class: float32 [768, 3], P(('dp', 'fsdp'))
- grad_b_class: float32 [3], replicated
Inputs may be any that keep to these rules, and one draw needn't show every extreme that they name: `doc_lengths`: the 4 document lengths of a sequence sum to 1024; in each group of 4 consecutive sequences one (which one varies) begins with a document of exactly 896 tokens, and in each of the others every block of 256 positions holds exactly one document start.
All inputs are finite; a program needn't handle non-finite values.
Results may differ from a plain program's by a relative error of at most 0.015.
The roundings to bfloat16 on the way count: a program that leaves them out, or rounds other values in their place, can miss the bound.
Values may be sent and summed in bfloat16 or wider, within the bound.
A program may use at most 256 MiB of HBM per device.

v0:
```python
import jax
import jax.numpy as jnp
from jax import lax
from jax.sharding import PartitionSpec as P

HEAD_DIM = 64
CLASSES = 3
MICRO = 4


def product(left_side, right_side):
    return jnp.dot(left_side, right_side, preferred_element_type=jnp.float32)


def contract_rows(left_side, right_side):
    return lax.dot_general(
        left_side, right_side, (((0,), (0,)), ((), ())), preferred_element_type=jnp.float32
    )


def times_transposed(left_side, right_side):
    return lax.dot_general(
        left_side, right_side, (((1,), (1,)), ((), ())), preferred_element_type=jnp.float32
    )


def layer_norm(values, norm_gain, norm_shift):
    average = jnp.mean(values, axis=-1, keepdims=True)
    centered = values - average
    variance = jnp.mean(centered * centered, axis=-1, keepdims=True)
    return centered * lax.rsqrt(variance + 1e-06) * norm_gain + norm_shift


def gelu_exact(values):
    return jax.nn.gelu(values, approximate=False)


def segment_numbers(lengths_rows, places):
    doc_ends = jnp.cumsum(lengths_rows, axis=1)
    above = (places[None, :, None] >= doc_ends[:, None, :]).astype(jnp.int32)
    return jnp.sum(above, axis=2)


def pair_heads(values):
    return values.reshape(values.shape[0], values.shape[1], 2, HEAD_DIM)


def pair_scores(query_pair, key_pair, same_doc):
    raw_scores = jnp.einsum(
        "bqhd,bkhd->bhqk", query_pair, key_pair, preferred_element_type=jnp.float32
    ) * HEAD_DIM ** (-0.5)
    return jnp.where(same_doc[:, None], raw_scores, -1000000000.0)


def lowered_masters(masters):
    return [member.astype(jnp.bfloat16) for member in masters]


def forward(tokens, lengths_rows, weights, bias_class):
    (
        w_query,
        b_query,
        w_key,
        w_value,
        b_value,
        w_out,
        b_out,
        first_gain,
        first_shift,
        w_inner,
        b_inner,
        w_outer,
        b_outer,
        second_gain,
        second_shift,
        w_pool,
        b_pool,
        w_class,
    ) = weights
    seq_count, local_len, model_width = tokens.shape
    doc_count = lengths_rows.shape[1]
    flat_rows = tokens.reshape(seq_count * local_len, model_width)
    queries = (
        (product(flat_rows, w_query) + b_query)
        .astype(jnp.bfloat16)
        .reshape(seq_count, local_len, model_width)
    )
    key_rows = (
        product(flat_rows, w_key).astype(jnp.bfloat16).reshape(seq_count, local_len, model_width)
    )
    value_rows = (
        (product(flat_rows, w_value) + b_value)
        .astype(jnp.bfloat16)
        .reshape(seq_count, local_len, model_width)
    )
    all_keys, all_values = (
        lax.all_gather(key_rows, "fsdp", axis=1, tiled=True),
        lax.all_gather(value_rows, "fsdp", axis=1, tiled=True),
    )
    full_len = all_keys.shape[1]
    own_places = lax.axis_index("fsdp") * local_len + jnp.arange(local_len, dtype=jnp.int32)
    key_places = jnp.arange(full_len, dtype=jnp.int32)
    same_doc = (
        segment_numbers(lengths_rows, own_places)[:, :, None]
        == segment_numbers(lengths_rows, key_places)[:, None, :]
    )
    pair_width = 2 * HEAD_DIM
    mixed_list = []
    log_totals = []
    for pair_index in range(model_width // pair_width):
        col_start = pair_index * pair_width
        query_pair = pair_heads(queries[:, :, col_start : col_start + pair_width])
        key_pair = pair_heads(all_keys[:, :, col_start : col_start + pair_width])
        value_pair = pair_heads(all_values[:, :, col_start : col_start + pair_width])
        scores = pair_scores(query_pair, key_pair, same_doc)
        row_peak = jnp.max(scores, axis=-1, keepdims=True)
        exp_total = jnp.sum(jnp.exp(scores - row_peak), axis=-1, keepdims=True)
        log_total = row_peak + jnp.log(exp_total)
        attn_probs = jnp.exp(scores - log_total).astype(jnp.bfloat16)
        mixed_pair = jnp.einsum(
            "bhqk,bkhd->bqhd", attn_probs, value_pair, preferred_element_type=jnp.float32
        )
        mixed_list.append(mixed_pair.reshape(seq_count, local_len, pair_width))
        log_totals.append(log_total)
    attended = (
        jnp.concatenate(mixed_list, axis=2)
        .astype(jnp.bfloat16)
        .reshape(seq_count * local_len, model_width)
    )
    branch = product(attended, w_out) + b_out
    pre_first = flat_rows.astype(jnp.float32) + branch
    normed = layer_norm(pre_first, first_gain.astype(jnp.float32), first_shift.astype(jnp.float32))
    normed_low = normed.astype(jnp.bfloat16)
    inner_pre = product(normed_low, w_inner) + b_inner
    activated = gelu_exact(inner_pre).astype(jnp.bfloat16)
    summed = normed + (product(activated, w_outer) + b_outer)
    result = layer_norm(summed, second_gain.astype(jnp.float32), second_shift.astype(jnp.float32))
    result_low = result.astype(jnp.bfloat16).reshape(seq_count, local_len, model_width)
    starts = jnp.cumsum(lengths_rows, axis=1) - lengths_rows
    picker = (own_places[None, None, :] == starts[:, :, None]).astype(jnp.bfloat16)
    local_firsts = jnp.einsum(
        "bdl,blc->bdc", picker, result_low, preferred_element_type=jnp.float32
    )
    firsts = lax.psum(local_firsts, "fsdp")
    firsts_low = firsts.astype(jnp.bfloat16).reshape(seq_count * doc_count, model_width)
    pooled = jnp.tanh(product(firsts_low, w_pool) + b_pool)
    pooled_low = pooled.astype(jnp.bfloat16)
    logits = product(pooled_low, w_class) + bias_class
    stored = (
        flat_rows,
        queries,
        all_keys,
        all_values,
        same_doc,
        log_totals,
        attended,
        pre_first,
        summed,
        normed_low,
        inner_pre,
        activated,
        picker,
        firsts_low,
        pooled,
        pooled_low,
        logits,
    )
    return (result_low, logits.reshape(seq_count, doc_count, CLASSES), stored)


def backward(stored, weights, cot_rows, label_rows):
    (
        w_query,
        b_query,
        w_key,
        w_value,
        b_value,
        w_out,
        b_out,
        first_gain,
        first_shift,
        w_inner,
        b_inner,
        w_outer,
        b_outer,
        second_gain,
        second_shift,
        w_pool,
        b_pool,
        w_class,
    ) = weights
    (
        flat_rows,
        queries,
        all_keys,
        all_values,
        same_doc,
        log_totals,
        attended,
        pre_first,
        summed,
        normed_low,
        inner_pre,
        activated,
        picker,
        firsts_low,
        pooled,
        pooled_low,
        logits,
    ) = stored
    seq_count, local_len, model_width = queries.shape
    doc_count = picker.shape[1]
    owner_flag = (lax.axis_index("fsdp") == 0).astype(jnp.float32)
    row_peak = jnp.max(logits, axis=-1, keepdims=True)
    class_exp = jnp.exp(logits - row_peak)
    class_probs = class_exp / jnp.sum(class_exp, axis=-1, keepdims=True)
    onehot_labels = (
        label_rows.reshape(-1)[:, None] == jnp.arange(CLASSES, dtype=jnp.int32)[None, :]
    ).astype(jnp.float32)
    grad_logits = (class_probs - onehot_labels).astype(jnp.bfloat16)
    grad_b_class = owner_flag * jnp.sum(grad_logits.astype(jnp.float32), axis=0)
    grad_w_class = owner_flag * contract_rows(pooled_low, grad_logits)
    grad_pool_pre = (times_transposed(grad_logits, w_class) * (1.0 - pooled * pooled)).astype(
        jnp.bfloat16
    )
    grad_b_pool = owner_flag * jnp.sum(grad_pool_pre.astype(jnp.float32), axis=0)
    grad_w_pool = owner_flag * contract_rows(firsts_low, grad_pool_pre)
    grad_firsts = times_transposed(grad_pool_pre, w_pool).reshape(seq_count, doc_count, model_width)
    from_pool = jnp.einsum(
        "bdl,bdc->blc", picker.astype(jnp.float32), grad_firsts, precision=lax.Precision.HIGHEST
    )
    grad_result = cot_rows.astype(jnp.float32).reshape(-1, model_width) + from_pool.reshape(
        -1, model_width
    )
    second_back = jax.vjp(
        layer_norm, summed, second_gain.astype(jnp.float32), second_shift.astype(jnp.float32)
    )[1]
    grad_summed, grad_second_gain, grad_second_shift = second_back(grad_result)
    grad_outer = grad_summed.astype(jnp.bfloat16)
    grad_b_outer = jnp.sum(grad_outer.astype(jnp.float32), axis=0)
    grad_w_outer = contract_rows(activated, grad_outer)
    gelu_back = jax.vjp(gelu_exact, inner_pre)[1]
    grad_inner = gelu_back(times_transposed(grad_outer, w_outer))[0].astype(jnp.bfloat16)
    grad_b_inner = jnp.sum(grad_inner.astype(jnp.float32), axis=0)
    grad_w_inner = contract_rows(normed_low, grad_inner)
    grad_normed = grad_summed + times_transposed(grad_inner, w_inner)
    first_back = jax.vjp(
        layer_norm, pre_first, first_gain.astype(jnp.float32), first_shift.astype(jnp.float32)
    )[1]
    grad_pre_first, grad_first_gain, grad_first_shift = first_back(grad_normed)
    grad_branch = grad_pre_first.astype(jnp.bfloat16)
    grad_b_out = jnp.sum(grad_branch.astype(jnp.float32), axis=0)
    grad_w_out = contract_rows(attended, grad_branch)
    grad_attended = (
        times_transposed(grad_branch, w_out)
        .astype(jnp.bfloat16)
        .reshape(seq_count, local_len, model_width)
    )
    pair_width = 2 * HEAD_DIM
    query_list = []
    key_list = []
    value_list = []
    for pair_index in range(model_width // pair_width):
        col_start = pair_index * pair_width
        query_pair = pair_heads(queries[:, :, col_start : col_start + pair_width])
        key_pair = pair_heads(all_keys[:, :, col_start : col_start + pair_width])
        value_pair = pair_heads(all_values[:, :, col_start : col_start + pair_width])
        grad_pair = pair_heads(grad_attended[:, :, col_start : col_start + pair_width])
        scores = pair_scores(query_pair, key_pair, same_doc)
        attn_probs = jnp.exp(scores - log_totals[pair_index])
        grad_probs = jnp.einsum(
            "bqhd,bkhd->bhqk", grad_pair, value_pair, preferred_element_type=jnp.float32
        )
        row_dot = jnp.sum(attn_probs * grad_probs, axis=-1, keepdims=True)
        grad_scores = (attn_probs * (grad_probs - row_dot)).astype(jnp.bfloat16)
        query_part = jnp.einsum(
            "bhqk,bkhd->bqhd", grad_scores, key_pair, preferred_element_type=jnp.float32
        ) * HEAD_DIM ** (-0.5)
        query_list.append(query_part.reshape(seq_count, local_len, pair_width))
        probs_low = attn_probs.astype(jnp.bfloat16)
        key_part = jnp.einsum(
            "bhqk,bqhd->bkhd", grad_scores, query_pair, preferred_element_type=jnp.float32
        ) * HEAD_DIM ** (-0.5)
        value_part = jnp.einsum(
            "bhqk,bqhd->bkhd", probs_low, grad_pair, preferred_element_type=jnp.float32
        )
        key_list.append(key_part.reshape(seq_count, key_part.shape[1], pair_width))
        value_list.append(value_part.reshape(seq_count, value_part.shape[1], pair_width))
    key_partials = jnp.concatenate(key_list, axis=2)
    value_partials = jnp.concatenate(value_list, axis=2)
    own_keys, own_values = (
        lax.psum_scatter(
            key_partials.astype(jnp.bfloat16), "fsdp", scatter_dimension=1, tiled=True
        ).astype(jnp.float32),
        lax.psum_scatter(
            value_partials.astype(jnp.bfloat16), "fsdp", scatter_dimension=1, tiled=True
        ).astype(jnp.float32),
    )
    query_grad = jnp.concatenate(query_list, axis=2).astype(jnp.bfloat16).reshape(-1, model_width)
    key_grad = own_keys.astype(jnp.bfloat16).reshape(-1, model_width)
    value_grad = own_values.astype(jnp.bfloat16).reshape(-1, model_width)
    grad_w_query = contract_rows(flat_rows, query_grad)
    grad_b_query = jnp.sum(query_grad.astype(jnp.float32), axis=0)
    grad_w_key = contract_rows(flat_rows, key_grad)
    grad_w_value = contract_rows(flat_rows, value_grad)
    grad_b_value = jnp.sum(value_grad.astype(jnp.float32), axis=0)
    grad_tokens = (
        grad_pre_first
        + times_transposed(query_grad, w_query)
        + times_transposed(key_grad, w_key)
        + times_transposed(value_grad, w_value)
    )
    new_grads = (
        grad_w_query,
        grad_b_query,
        grad_w_key,
        grad_w_value,
        grad_b_value,
        grad_w_out,
        grad_b_out,
        grad_first_gain,
        grad_first_shift,
        grad_w_inner,
        grad_b_inner,
        grad_w_outer,
        grad_b_outer,
        grad_second_gain,
        grad_second_shift,
        grad_w_pool,
        grad_b_pool,
        grad_w_class,
    )
    return (
        new_grads,
        grad_b_class,
        grad_tokens.astype(jnp.bfloat16).reshape(seq_count, local_len, model_width),
    )


def body(
    inputs,
    cotangent,
    doc_lengths,
    labels,
    w_query,
    b_query,
    w_key,
    w_value,
    b_value,
    w_out,
    b_out,
    first_gain,
    first_shift,
    w_inner,
    b_inner,
    w_outer,
    b_outer,
    second_gain,
    second_shift,
    w_pool,
    b_pool,
    w_class,
    b_class,
):
    masters = (
        w_query,
        b_query,
        w_key,
        w_value,
        b_value,
        w_out,
        b_out,
        first_gain,
        first_shift,
        w_inner,
        b_inner,
        w_outer,
        b_outer,
        second_gain,
        second_shift,
        w_pool,
        b_pool,
        w_class,
    )
    group_size = lax.axis_size("dp") * lax.axis_size("fsdp")
    grad_sums = [
        jnp.zeros((member.shape[0] * group_size,) + member.shape[1:], jnp.float32)
        for member in masters
    ]
    class_sum = jnp.zeros((CLASSES,), jnp.float32)
    micro_seqs = inputs.shape[0] // MICRO
    out_list = []
    logit_list = []
    grad_list = []
    for micro_step in range(MICRO):
        first_seq = micro_step * micro_seqs
        after_seq = first_seq + micro_seqs
        tokens = inputs[first_seq:after_seq]
        lengths_rows = doc_lengths[first_seq:after_seq]
        pieces = lowered_masters(masters)
        front_weights = (
            lax.all_gather(pieces[0], ("dp", "fsdp"), axis=0, tiled=True),
            lax.all_gather(pieces[1], ("dp", "fsdp"), axis=0, tiled=True),
            lax.all_gather(pieces[2], ("dp", "fsdp"), axis=0, tiled=True),
            lax.all_gather(pieces[3], ("dp", "fsdp"), axis=0, tiled=True),
            lax.all_gather(pieces[4], ("dp", "fsdp"), axis=0, tiled=True),
            lax.all_gather(pieces[5], ("dp", "fsdp"), axis=0, tiled=True),
            lax.all_gather(pieces[6], ("dp", "fsdp"), axis=0, tiled=True),
            lax.all_gather(pieces[7], ("dp", "fsdp"), axis=0, tiled=True),
            lax.all_gather(pieces[8], ("dp", "fsdp"), axis=0, tiled=True),
            lax.all_gather(pieces[9], ("dp", "fsdp"), axis=0, tiled=True),
            lax.all_gather(pieces[10], ("dp", "fsdp"), axis=0, tiled=True),
            lax.all_gather(pieces[11], ("dp", "fsdp"), axis=0, tiled=True),
            lax.all_gather(pieces[12], ("dp", "fsdp"), axis=0, tiled=True),
            lax.all_gather(pieces[13], ("dp", "fsdp"), axis=0, tiled=True),
            lax.all_gather(pieces[14], ("dp", "fsdp"), axis=0, tiled=True),
            lax.all_gather(pieces[15], ("dp", "fsdp"), axis=0, tiled=True),
            lax.all_gather(pieces[16], ("dp", "fsdp"), axis=0, tiled=True),
            lax.all_gather(pieces[17], ("dp", "fsdp"), axis=0, tiled=True),
        )
        result_low, logits, stored = forward(tokens, lengths_rows, front_weights, b_class)
        out_list.append(result_low)
        logit_list.append(logits)
        back_weights = (
            lax.all_gather(pieces[0], ("dp", "fsdp"), axis=0, tiled=True),
            lax.all_gather(pieces[1], ("dp", "fsdp"), axis=0, tiled=True),
            lax.all_gather(pieces[2], ("dp", "fsdp"), axis=0, tiled=True),
            lax.all_gather(pieces[3], ("dp", "fsdp"), axis=0, tiled=True),
            lax.all_gather(pieces[4], ("dp", "fsdp"), axis=0, tiled=True),
            lax.all_gather(pieces[5], ("dp", "fsdp"), axis=0, tiled=True),
            lax.all_gather(pieces[6], ("dp", "fsdp"), axis=0, tiled=True),
            lax.all_gather(pieces[7], ("dp", "fsdp"), axis=0, tiled=True),
            lax.all_gather(pieces[8], ("dp", "fsdp"), axis=0, tiled=True),
            lax.all_gather(pieces[9], ("dp", "fsdp"), axis=0, tiled=True),
            lax.all_gather(pieces[10], ("dp", "fsdp"), axis=0, tiled=True),
            lax.all_gather(pieces[11], ("dp", "fsdp"), axis=0, tiled=True),
            lax.all_gather(pieces[12], ("dp", "fsdp"), axis=0, tiled=True),
            lax.all_gather(pieces[13], ("dp", "fsdp"), axis=0, tiled=True),
            lax.all_gather(pieces[14], ("dp", "fsdp"), axis=0, tiled=True),
            lax.all_gather(pieces[15], ("dp", "fsdp"), axis=0, tiled=True),
            lax.all_gather(pieces[16], ("dp", "fsdp"), axis=0, tiled=True),
            lax.all_gather(pieces[17], ("dp", "fsdp"), axis=0, tiled=True),
        )
        stored = forward(tokens, lengths_rows, back_weights, b_class)[2]
        new_grads, class_grad, grad_tokens = backward(
            stored, back_weights, cotangent[first_seq:after_seq], labels[first_seq:after_seq]
        )
        grad_sums = [running + fresh_grad for running, fresh_grad in zip(grad_sums, new_grads)]
        class_sum = class_sum + class_grad
        grad_list.append(grad_tokens)
    owned = (
        lax.psum_scatter(grad_sums[0], ("dp", "fsdp"), scatter_dimension=0, tiled=True),
        lax.psum_scatter(grad_sums[1], ("dp", "fsdp"), scatter_dimension=0, tiled=True),
        lax.psum_scatter(grad_sums[2], ("dp", "fsdp"), scatter_dimension=0, tiled=True),
        lax.psum_scatter(grad_sums[3], ("dp", "fsdp"), scatter_dimension=0, tiled=True),
        lax.psum_scatter(grad_sums[4], ("dp", "fsdp"), scatter_dimension=0, tiled=True),
        lax.psum_scatter(grad_sums[5], ("dp", "fsdp"), scatter_dimension=0, tiled=True),
        lax.psum_scatter(grad_sums[6], ("dp", "fsdp"), scatter_dimension=0, tiled=True),
        lax.psum_scatter(grad_sums[7], ("dp", "fsdp"), scatter_dimension=0, tiled=True),
        lax.psum_scatter(grad_sums[8], ("dp", "fsdp"), scatter_dimension=0, tiled=True),
        lax.psum_scatter(grad_sums[9], ("dp", "fsdp"), scatter_dimension=0, tiled=True),
        lax.psum_scatter(grad_sums[10], ("dp", "fsdp"), scatter_dimension=0, tiled=True),
        lax.psum_scatter(grad_sums[11], ("dp", "fsdp"), scatter_dimension=0, tiled=True),
        lax.psum_scatter(grad_sums[12], ("dp", "fsdp"), scatter_dimension=0, tiled=True),
        lax.psum_scatter(grad_sums[13], ("dp", "fsdp"), scatter_dimension=0, tiled=True),
        lax.psum_scatter(grad_sums[14], ("dp", "fsdp"), scatter_dimension=0, tiled=True),
        lax.psum_scatter(grad_sums[15], ("dp", "fsdp"), scatter_dimension=0, tiled=True),
        lax.psum_scatter(grad_sums[16], ("dp", "fsdp"), scatter_dimension=0, tiled=True),
        lax.psum_scatter(grad_sums[17], ("dp", "fsdp"), scatter_dimension=0, tiled=True),
    )
    class_total = lax.psum(class_sum, ("dp", "fsdp"))
    return (
        jnp.concatenate(out_list, axis=0),
        jnp.concatenate(logit_list, axis=0),
        jnp.concatenate(grad_list, axis=0),
        owned[0],
        owned[1],
        owned[2],
        owned[3],
        owned[4],
        owned[5],
        owned[6],
        owned[7],
        owned[8],
        owned[9],
        owned[10],
        owned[11],
        owned[12],
        owned[13],
        owned[14],
        owned[15],
        owned[16],
        owned[17],
        class_total,
    )


def solution(mesh):
    placed = (
        P("dp", "fsdp", None),
        P("dp", "fsdp", None),
        P("dp", None),
        P("dp", None),
        P(("dp", "fsdp"), None),
        P(("dp", "fsdp")),
        P(("dp", "fsdp"), None),
        P(("dp", "fsdp"), None),
        P(("dp", "fsdp")),
        P(("dp", "fsdp"), None),
        P(("dp", "fsdp")),
        P(("dp", "fsdp")),
        P(("dp", "fsdp")),
        P(("dp", "fsdp"), None),
        P(("dp", "fsdp")),
        P(("dp", "fsdp"), None),
        P(("dp", "fsdp")),
        P(("dp", "fsdp")),
        P(("dp", "fsdp")),
        P(("dp", "fsdp"), None),
        P(("dp", "fsdp")),
        P(("dp", "fsdp"), None),
        P(),
    )
    return jax.shard_map(
        body,
        mesh=mesh,
        in_specs=placed,
        out_specs=(
            P("dp", "fsdp", None),
            P("dp", None, None),
            P("dp", "fsdp", None),
            P(("dp", "fsdp"), None),
            P(("dp", "fsdp")),
            P(("dp", "fsdp"), None),
            P(("dp", "fsdp"), None),
            P(("dp", "fsdp")),
            P(("dp", "fsdp"), None),
            P(("dp", "fsdp")),
            P(("dp", "fsdp")),
            P(("dp", "fsdp")),
            P(("dp", "fsdp"), None),
            P(("dp", "fsdp")),
            P(("dp", "fsdp"), None),
            P(("dp", "fsdp")),
            P(("dp", "fsdp")),
            P(("dp", "fsdp")),
            P(("dp", "fsdp"), None),
            P(("dp", "fsdp")),
            P(("dp", "fsdp"), None),
            P(),
        ),
        check_vma=False,
    )
```

profile of v0, /device:TPU:0, one launch (start us, length us, event | category | flops | bytes accessed | tf_op | source)
XLA Modules:
  0.0 1802.8 jit_solution(15763916821212695829)
XLA Ops:
  20.7 42.4 %all-reduce.23 = (bf16[3072]{0:T(1024)(128)(2,1)S(1)}, bf16[768]{0:T(1024)(128)(2,1)S(1)}, bf16[768]{0:T(1024)(128)(2,1)S(1)}, bf16[768]{0:T(1024)(128)(2,1)S(1)...) all-reduce(bf16[3072]{0:T(1024)(128)(2,1)S(1)} %dynamic-update-slic, ...), channel_id=1, replica_groups=mesh['dp'=8,'fsdp'=4] {'dp','fsdp'}, use_global_device_ids=true, to_apply=%add.5 | all-reduce | flops 9984 | bytes 39936
  63.1 5.2 all-gather.25.cloned.1.call-done
  75.1 49.7 %all-gather.29.cloned.1.call-done = bf16[768,768]{1,0:T(8,128)(2,1)} async-done(((bf16[24,768]{1,0:T(8,128)(2,1)}), bf16[768,768]{1,0:T(8,128)(2,1)}) %all-gather.29.cloned.1.call-update) | async-done | bytes 1179664 | tf_op jit(solution)/shard_map/all_gather | solution.py:404
  140.9 39.6 %all-gather.8 = bf16[32,24,3]{1,2,0:T(4,128)(2,1)S(1)} all-gather(bf16[1,24,3]{1,2,0:T(4,128)(2,1)S(1)} %convert_bitcast_fusion), channel_id=1, replica_groups=mesh['dp'=8,'fsdp'=4] {'dp','fsdp'}, dimensions={0}, use_global_device_ids=true | all-gather | bytes 4752 | tf_op jit(solution)/shard_map/all_gather | solution.py:419
  239.6 3.9 all-gather.43.cloned.1.call-done
  252.9 12.5 all-gather.39.cloned.1.call-done
  274.6 12.0 all-gather.53.cloned.1.call-done
  294.3 13.6 all-gather.49.cloned.1.call-done
  321.3 7.7 all-gather.45.cloned.1.call-done
  342.4 8.5 all-gather.41.cloned.1.call-done
  376.8 30.9 %all-gather.31.cloned.1.call-done = bf16[768,768]{1,0:T(8,128)(2,1)} async-done(((bf16[24,768]{1,0:T(8,128)(2,1)}), bf16[768,768]{1,0:T(8,128)(2,1)}) %all-gather.31.cloned.1.call-update) | async-done | bytes 1179664 | tf_op jit(solution)/shard_map/all_gather | solution.py:407
  453.5 19.7 %all-gather.33.cloned.1.call-done = bf16[768,3072]{1,0:T(8,128)(2,1)} async-done(((bf16[24,3072]{1,0:T(8,128)(2,1)}), bf16[768,3072]{1,0:T(8,128)(2,1)}) %all-gather.33.cloned.1.call-update) | async-done | bytes 4718608 | tf_op jit(solution)/shard_map/all_gather | solution.py:411
  473.2 12.0 multiply_convert_fusion.3
  485.1 53.3 %all-gather.35.cloned.1.call-done = bf16[3072,768]{1,0:T(8,128)(2,1)} async-done(((bf16[96,768]{1,0:T(8,128)(2,1)}), bf16[3072,768]{1,0:T(8,128)(2,1)}) %all-gather.35.cloned.1.call-update) | async-done | bytes 4718608 | tf_op jit(solution)/shard_map/all_gather | solution.py:413
  538.5 4.7 fusion.381
  543.2 12.2 multiply_convert_fusion.2
  557.8 11.7 multiply_convert_fusion.1
  572.3 11.7 multiply_convert_fusion
  592.1 12.8 all-reduce.22
  631.6 3.2 multiply_reduce_fusion.28
  652.4 4.3 multiply_reduce_fusion.31
  656.8 3.2 fusion.345
  910.3 3.0 copy.560
  923.9 2.9 fusion.145
  926.8 2.9 fusion.151
  929.8 2.9 fusion.157
  932.6 5.1 add_bitcast_fusion
  937.8 3.3 copy.564
  941.4 2.9 fusion.148
  944.3 2.9 fusion.154
  947.2 12.1 reduce-scatter.23.cloned.1.call-done
  962.2 28.6 %reduce-scatter.35.cloned.1.call-done = bf16[1,256,768]{1,2,0:T(8,128)(2,1)} async-done(((bf16[1,1024,768]{1,2,0:T(8,128)(2,1)}), bf16[1,256,768]{1,2,0:T(8,128)(2,1)}) %reduce-scatter.35.cloned.1.call-update) | async-done | bytes 393232 | tf_op jit(solution)/shard_map/reduce_scatter | solution.py:292
  990.8 5.1 add_bitcast_fusion.1
  995.9 3.1 copy.562
  1000.2 3.1 fusion.335
  1003.4 6.1 fusion.332
  1009.5 6.0 fusion.338
  1015.5 13.0 add_add_fusion.1
  1032.6 5.0 fusion.418
  1037.6 5.0 fusion.419
  1042.6 12.8 add_add_fusion
  1077.6 41.6 %all-reduce.21 = (f32[768]{0:T(1024)}, f32[768]{0:T(1024)}, f32[768]{0:T(1024)}, f32[768]{0:T(1024)}, f32[768]{0:T(1024)}, /*index=5*/f32[3072]{0:T(1024)}, f32[...) all-reduce(f32[768]{0:T(1024)} %add_add_fusion.19, ...), channel_id=19, replica_groups=mesh['dp'=8,'fsdp'=4] {'dp','fsdp'}, use_global_device_ids=true, to_apply=%region_141.142.clone | all-reduce | flops 12291 | bytes 98328
  1142.6 57.7 %reduce-scatter.39.cloned.1.call-done = f32[24,768]{1,0:T(8,128)} async-done(((f32[768,768]{1,0:T(8,128)}), f32[24,768]{1,0:T(8,128)}) %reduce-scatter.39.cloned.1.call-update) | async-done | bytes 73744 | tf_op jit(solution)/shard_map/reduce_scatter | solution.py:457
  1200.3 103.9 %reduce-scatter.45.cloned.1.call-done = f32[24,768]{1,0:T(8,128)} async-done(((f32[768,768]{1,0:T(8,128)}), f32[24,768]{1,0:T(8,128)}) %reduce-scatter.45.cloned.1.call-update) | async-done | bytes 73744 | tf_op jit(solution)/shard_map/reduce_scatter | solution.py:467
  1304.1 104.5 %reduce-scatter.51.cloned.1.call-done = f32[24,768]{1,0:T(8,128)} async-done(((f32[768,768]{1,0:T(8,128)}), f32[24,768]{1,0:T(8,128)}) %reduce-scatter.51.cloned.1.call-update) | async-done | bytes 73744
  1408.7 103.9 %reduce-scatter.49.cloned.1.call-done = f32[24,768]{1,0:T(8,128)} async-done(((f32[768,768]{1,0:T(8,128)}), f32[24,768]{1,0:T(8,128)}) %reduce-scatter.49.cloned.1.call-update) | async-done | bytes 73744
  1512.5 142.1 %reduce-scatter.41.cloned.1.call-done = f32[24,3072]{1,0:T(8,128)} async-done(((f32[768,3072]{1,0:T(8,128)}), f32[24,3072]{1,0:T(8,128)}) %reduce-scatter.41.cloned.1.call-update) | async-done | bytes 294928 | tf_op jit(solution)/shard_map/reduce_scatter | solution.py:461
  1654.6 141.1 %reduce-scatter.43.cloned.1.call-done = f32[96,768]{1,0:T(8,128)} async-done(((f32[3072,768]{1,0:T(8,128)}), f32[96,768]{1,0:T(8,128)}) %reduce-scatter.43.cloned.1.call-update) | async-done | bytes 294928 | tf_op jit(solution)/shard_map/reduce_scatter | solution.py:463
  (2014 shorter events, 584.8 us)
Async XLA Ops:
  7.2 64.0 %copy-start.74 = (bf16[4,256,768]{2,1,0:T(8,128)(2,1)S(1)}, bf16[4,256,768]{2,1,0:T(8,128)(2,1)}, u32[]{:S(2)}) copy-start(bf16[4,256,768]{2,1,0:T(8,128)(2,1)} %param.23) | copy-start | bytes 4718596
  7.2 61.2 %all-gather.25.cloned.1.call-start = ((), (), s32[]{:S(2)}) async-start(), calls=%async_computation.15 | async-start | bytes 1216512 | tf_op jit(solution)/shard_map/all_gather | solution.py:405
  8.9 116.0 %all-gather.29.cloned.1.call-start = ((), (), s32[]{:S(2)}) async-start(), calls=%async_computation.17 | async-start | bytes 1216512 | tf_op jit(solution)/shard_map/all_gather | solution.py:404
  10.5 172.1 %all-gather.27.cloned.1.call-start = ((), (), s32[]{:S(2)}) async-start(), calls=%async_computation.16 | async-start | bytes 1216512 | tf_op jit(solution)/shard_map/all_gather | solution.py:402
  12.1 208.9 %all-gather.51.cloned.1.call-start = ((), (), s32[]{:S(2)}) async-start(), calls=%async_computation.40 | async-start | bytes 1966080 | tf_op jit(solution)/shard_map/all_gather | solution.py:98
  71.1 159.1 %all-gather.47.cloned.1.call-start = ((), (), s32[]{:S(2)}) async-start(), calls=%async_computation.38 | async-start | bytes 1966080 | tf_op jit(solution)/shard_map/all_gather | solution.py:98
  72.5 171.1 %all-gather.43.cloned.1.call-start = ((), (), s32[]{:S(2)}) async-start(), calls=%async_computation.36 | async-start | bytes 1966080 | tf_op jit(solution)/shard_map/all_gather | solution.py:98
  73.8 191.6 %all-gather.39.cloned.1.call-start = ((), (), s32[]{:S(2)}) async-start(), calls=%async_computation.34 | async-start | bytes 1966080 | tf_op jit(solution)/shard_map/all_gather | solution.py:98
  75.1 211.6 %all-gather.53.cloned.1.call-start = ((), (), s32[]{:S(2)}) async-start(), calls=%async_computation.41 | async-start | bytes 1966080 | tf_op jit(solution)/shard_map/all_gather | solution.py:97
  127.5 180.4 %all-gather.49.cloned.1.call-start = ((), (), s32[]{:S(2)}) async-start(), calls=%async_computation.39 | async-start | bytes 1966080 | tf_op jit(solution)/shard_map/all_gather | solution.py:97
  128.8 200.2 %all-gather.45.cloned.1.call-start = ((), (), s32[]{:S(2)}) async-start(), calls=%async_computation.37 | async-start | bytes 1966080 | tf_op jit(solution)/shard_map/all_gather | solution.py:97
  130.2 220.7 %all-gather.41.cloned.1.call-start = ((), (), s32[]{:S(2)}) async-start(), calls=%async_computation.35 | async-start | bytes 1966080 | tf_op jit(solution)/shard_map/all_gather | solution.py:97
  131.5 276.2 %all-gather.31.cloned.1.call-start = ((), (), s32[]{:S(2)}) async-start(), calls=%async_computation.18 | async-start | bytes 1216512 | tf_op jit(solution)/shard_map/all_gather | solution.py:407
  132.2 341.0 %all-gather.33.cloned.1.call-start = ((), (), s32[]{:S(2)}) async-start(), calls=%async_computation.19 | async-start | bytes 4866048 | tf_op jit(solution)/shard_map/all_gather | solution.py:411
  132.9 405.5 %all-gather.35.cloned.1.call-start = ((), (), s32[]{:S(2)}) async-start(), calls=%async_computation.20 | async-start | bytes 4866048 | tf_op jit(solution)/shard_map/all_gather | solution.py:413
  133.7 471.3 %all-gather.37.cloned.1.call-start = ((), (), s32[]{:S(2)}) async-start(), calls=%async_computation.21 | async-start | bytes 1216512 | tf_op jit(solution)/shard_map/all_gather | solution.py:417
  134.4 789.5 %reduce-scatter.33.cloned.1.call-start = ((), (), s32[]{:S(2)}) async-start(), calls=%async_computation.27 | async-start | bytes 1966080 | tf_op jit(solution)/shard_map/reduce_scatter | solution.py:295
  134.5 48.1 %copy-start.415 = (s32[256]{0:T(256)}, s32[256]{0:T(256)S(1)}, u32[]{:S(2)}) copy-start(s32[256]{0:T(256)S(1)} %iota_add_fusion) | copy-start | bytes 3076
  137.3 446.8 %copy-start.297 = (f32[768]{0:T(1024)}, f32[768]{0:T(1024)S(1)}, u32[]{:S(2)}) copy-start(f32[768]{0:T(1024)S(1)} %convert_element_type.1047) | copy-start | bytes 9220
  289.1 81.5 %copy-start.177 = (bf16[1,1024,128]{1,2,0:T(8,128)(2,1)}, bf16[1,1024,128]{1,2,0:T(8,128)(2,1)S(1)}, u32[]{:S(2)}) copy-start(bf16[1,1024,128]{1,2,0:T(8,128)(2,1)S(1)} %copy.526) | copy-start | bytes 786436
  289.3 80.1 %copy-start.179 = (bf16[1,1024,128]{1,2,0:T(8,128)(2,1)}, bf16[1,1024,128]{1,2,0:T(8,128)(2,1)S(1)}, u32[]{:S(2)}) copy-start(bf16[1,1024,128]{1,2,0:T(8,128)(2,1)S(1)} %copy.523) | copy-start | bytes 786436
  289.4 78.7 %copy-start.181 = (bf16[1,1024,128]{1,2,0:T(8,128)(2,1)}, bf16[1,1024,128]{1,2,0:T(8,128)(2,1)S(1)}, u32[]{:S(2)}) copy-start(bf16[1,1024,128]{1,2,0:T(8,128)(2,1)S(1)} %copy.520) | copy-start | bytes 786436
  290.6 76.2 %copy-start.182 = (bf16[1,1024,128]{1,2,0:T(8,128)(2,1)}, bf16[1,1024,128]{1,2,0:T(8,128)(2,1)S(1)}, u32[]{:S(2)}) copy-start(bf16[1,1024,128]{1,2,0:T(8,128)(2,1)S(1)} %copy.517) | copy-start | bytes 786436
  376.8 33.7 %copy-start.188 = (bf16[1,1024,128]{1,2,0:T(8,128)(2,1)S(1)}, bf16[1,1024,128]{1,2,0:T(8,128)(2,1)}, u32[]{:S(2)}) copy-start(bf16[1,1024,128]{1,2,0:T(8,128)(2,1)} %copy.496) | copy-start | bytes 786436
  376.8 33.7 %copy-start.353 = (bf16[1,256,128]{1,2,0:T(8,128)(2,1)S(1)}, bf16[1,256,128]{1,2,0:T(8,128)(2,1)}, u32[]{:S(2)}) copy-start(bf16[1,256,128]{1,2,0:T(8,128)(2,1)} %copy.495) | copy-start | bytes 196612
  376.8 34.3 %copy-start.383 = (bf16[256,768]{0,1:T(8,128)(2,1)}, bf16[256,768]{0,1:T(8,128)(2,1)S(1)}, u32[]{:S(2)}) copy-start(bf16[256,768]{0,1:T(8,128)(2,1)S(1)} %constant_dynamic-update-slice_fusion.18) | copy-start | bytes 1179652
  424.3 145.2 %copy-start.482 = (f32[256]{0:T(256)}, f32[256]{0:T(256)S(1)}, u32[]{:S(2)}) copy-start(f32[256]{0:T(256)S(1)} %broadcast_multiply_fusion.3) | copy-start | bytes 3076
  438.0 117.4 %copy-start.485 = (f32[256]{0:T(256)}, f32[256]{0:T(256)S(1)}, u32[]{:S(2)}) copy-start(f32[256]{0:T(256)S(1)} %broadcast_multiply_fusion.5) | copy-start | bytes 3076
  543.1 44.2 %copy-start.78 = (f32[256,768]{1,0:T(8,128)}, f32[256,768]{1,0:T(8,128)S(1)}, u32[]{:S(2)}) copy-start(f32[256,768]{1,0:T(8,128)S(1)} %get-tuple-element.372) | copy-start | bytes 2359300
  543.2 44.1 %copy-start.491 = (f32[256]{0:T(256)}, f32[256]{0:T(256)S(1)}, u32[]{:S(2)}) copy-start(f32[256]{0:T(256)S(1)} %broadcast_multiply_fusion.6) | copy-start | bytes 3076
  557.7 29.6 %copy-start.80 = (f32[256,768]{1,0:T(8,128)}, f32[256,768]{1,0:T(8,128)S(1)}, u32[]{:S(2)}) copy-start(f32[256,768]{1,0:T(8,128)S(1)} %get-tuple-element.389) | copy-start | bytes 2359300
  744.7 182.1 %reduce-scatter.29.cloned.1.call-start = ((), (), s32[]{:S(2)}) async-start(), calls=%async_computation.25 | async-start | bytes 1966080 | tf_op jit(solution)/shard_map/reduce_scatter | solution.py:295
  778.4 151.4 %reduce-scatter.25.cloned.1.call-start = ((), (), s32[]{:S(2)}) async-start(), calls=%async_computation.23 | async-start | bytes 1966080 | tf_op jit(solution)/shard_map/reduce_scatter | solution.py:295
  793.5 139.1 %reduce-scatter.37.cloned.1.call-start = ((), (), s32[]{:S(2)}) async-start(), calls=%async_computation.29 | async-start | bytes 1966080 | tf_op jit(solution)/shard_map/reduce_scatter | solution.py:295
  815.3 126.0 %reduce-scatter.31.cloned.1.call-start = ((), (), s32[]{:S(2)}) async-start(), calls=%async_computation.26 | async-start | bytes 1966080 | tf_op jit(solution)/shard_map/reduce_scatter | solution.py:292
  847.6 96.7 %reduce-scatter.27.cloned.1.call-start = ((), (), s32[]{:S(2)}) async-start(), calls=%async_computation.24 | async-start | bytes 1966080 | tf_op jit(solution)/shard_map/reduce_scatter | solution.py:292
  865.3 94.0 %reduce-scatter.23.cloned.1.call-start = ((), (), s32[]{:S(2)}) async-start(), calls=%async_computation.22 | async-start | bytes 1966080 | tf_op jit(solution)/shard_map/reduce_scatter | solution.py:292
  878.9 111.9 %reduce-scatter.35.cloned.1.call-start = ((), (), s32[]{:S(2)}) async-start(), calls=%async_computation.28 | async-start | bytes 1966080 | tf_op jit(solution)/shard_map/reduce_scatter | solution.py:292
  902.3 240.3 %reduce-scatter.47.cloned.1.call-start = ((), (), s32[]{:S(2)}) async-start(), calls=%async_computation.42 | async-start | bytes 2433024
  913.4 286.9 %reduce-scatter.39.cloned.1.call-start = ((), (), s32[]{:S(2)}) async-start(), calls=%async_computation.30 | async-start | bytes 2433024 | tf_op jit(solution)/shard_map/reduce_scatter | solution.py:457
  919.5 384.6 %reduce-scatter.45.cloned.1.call-start = ((), (), s32[]{:S(2)}) async-start(), calls=%async_computation.33 | async-start | bytes 2433024 | tf_op jit(solution)/shard_map/reduce_scatter | solution.py:467
  923.8 484.8 %reduce-scatter.51.cloned.1.call-start = ((), (), s32[]{:S(2)}) async-start(), calls=%async_computation.44 | async-start | bytes 2433024
  941.1 571.4 %reduce-scatter.49.cloned.1.call-start = ((), (), s32[]{:S(2)}) async-start(), calls=%async_computation.43 | async-start | bytes 2433024
  999.1 655.5 %reduce-scatter.41.cloned.1.call-start = ((), (), s32[]{:S(2)}) async-start(), calls=%async_computation.31 | async-start | bytes 9732096 | tf_op jit(solution)/shard_map/reduce_scatter | solution.py:461
  1028.5 767.2 %reduce-scatter.43.cloned.1.call-start = ((), (), s32[]{:S(2)}) async-start(), calls=%async_computation.32 | async-start | bytes 9732096 | tf_op jit(solution)/shard_map/reduce_scatter | solution.py:463
  1074.8 58.3 %copy-start.68 = (bf16[768,768]{1,0:T(8,128)(2,1)S(1)}, bf16[768,768]{1,0:T(8,128)(2,1)}, u32[]{:S(2)}) copy-start(bf16[768,768]{1,0:T(8,128)(2,1)} %all-gather.29.cloned.1.call-done) | copy-start | bytes 3538948
  1076.6 58.3 %copy-start.73 = (bf16[768,768]{1,0:T(8,128)(2,1)S(1)}, bf16[768,768]{1,0:T(8,128)(2,1)}, u32[]{:S(2)}) copy-start(bf16[768,768]{1,0:T(8,128)(2,1)} %all-gather.25.cloned.1.call-done) | copy-start | bytes 3538948
  1076.6 58.3 %copy-start.163 = (bf16[1,256,768]{1,2,0:T(8,128)(2,1)S(1)}, bf16[1,256,768]{1,2,0:T(8,128)(2,1)}, u32[]{:S(2)}) copy-start(bf16[1,256,768]{1,2,0:T(8,128)(2,1)} %reduce-scatter.25.cloned.1.call-done) | copy-start | bytes 1179652
  (618 other events, 2251.9 us)
Sparse Core Ops, SparseCore 0:
  11.5 56.8 all-gather.24
  71.9 52.9 all-gather.28
  128.3 52.9 all-gather.26
  182.7 18.5 all-gather.50
  202.8 19.6 all-gather.46
  223.9 19.6 all-gather.42
  245.7 19.6 all-gather.38
  266.9 19.6 all-gather.52
  288.2 19.6 all-gather.48
  309.3 19.6 all-gather.44
  331.2 19.6 all-gather.40
  353.6 54.0 all-gather.30
  410.6 62.5 all-gather.32
  475.9 62.4 all-gather.34
  541.2 52.8 all-gather.36
  744.8 27.0 reduce-scatter.32
  778.5 26.9 reduce-scatter.28
  807.9 28.1 reduce-scatter.24
  838.8 28.1 reduce-scatter.36
  869.4 28.2 reduce-scatter.30
  900.4 28.1 reduce-scatter.26
  931.1 28.1 reduce-scatter.22
  962.6 28.1 reduce-scatter.34
  996.5 99.0 reduce-scatter.46
  1102.4 97.8 reduce-scatter.38
  1206.0 98.0 reduce-scatter.44
  1310.7 97.9 reduce-scatter.50
  1414.5 97.9 reduce-scatter.48
  1520.0 134.5 reduce-scatter.40
  1660.9 134.7 reduce-scatter.42
where the time goes:
time: 1820 us; the launch traced here: 1800 us
  waiting for transfers between devices  912 us (50%)
  matrix products  373 us (20%)
  local copies, waits for them, and re-layouts  277 us (15%)
  blocking collectives  136 us (7%)
  other arithmetic  79.9 us (4%)
  between operations  22.4 us (1%)
    unnamed x33, waiting for transfers between devices  209 us
    reduce_scatter x1, waiting for transfers between devices, body(): lax.psum_scatter(grad_sums[9], ('dp', 'fsdp'), scatter_dimension=0, tiled...  142 us
    reduce_scatter x1, waiting for transfers between devices, body(): lax.psum_scatter(grad_sums[11], ('dp', 'fsdp'), scatter_dimension=0, tile...  141 us
    unnamed x1388, local copies, waits for them, and re-layouts  128 us
    reduce_scatter x1, waiting for transfers between devices, body(): lax.psum_scatter(grad_sums[15], ('dp', 'fsdp'), scatter_dimension=0, tile...  104 us
    dot_general x32, matrix products, contract_rows(): lax.dot_general(left_side, right_side, (((0,), (0,)), ((), ())), preferre...  95.8 us
    dot_general x32, matrix products, product(): return jnp.dot(left_side, right_side, preferred_element_type=jnp.float32)  87.1 us
    unnamed x2, blocking collectives  84 us
  transfers between devices with their start and end apart: 30, of which 19 were waited for; matrix products, arithmetic and copies ran while one was open for 31% of the time, Pallas kernels for 0%

commit v1 on v0

--- a/solution.py
+++ b/solution.py
@@ -1,6 +1,10 @@
+import functools
+
 import jax
 import jax.numpy as jnp
 from jax import lax
+from jax.experimental import pallas as pl
+from jax.experimental.pallas import tpu as pltpu
 from jax.sharding import PartitionSpec as P
 
 HEAD_DIM = 64
@@ -35,8 +39,14 @@
     return jax.nn.gelu(values, approximate=False)
 
 
+def running_sum(lengths_rows):
+    count = lengths_rows.shape[1]
+    upper = jnp.arange(count)[:, None] <= jnp.arange(count)[None, :]
+    return jnp.sum(jnp.where(upper[None], lengths_rows[:, :, None], 0), axis=1)
+
+
 def segment_numbers(lengths_rows, places):
-    doc_ends = jnp.cumsum(lengths_rows, axis=1)
+    doc_ends = running_sum(lengths_rows)
     above = (places[None, :, None] >= doc_ends[:, None, :]).astype(jnp.int32)
     return jnp.sum(above, axis=2)
 
@@ -136,7 +146,7 @@
     summed = normed + (product(activated, w_outer) + b_outer)
     result = layer_norm(summed, second_gain.astype(jnp.float32), second_shift.astype(jnp.float32))
     result_low = result.astype(jnp.bfloat16).reshape(seq_count, local_len, model_width)
-    starts = jnp.cumsum(lengths_rows, axis=1) - lengths_rows
+    starts = running_sum(lengths_rows) - lengths_rows
     picker = (own_places[None, None, :] == starts[:, :, None]).astype(jnp.bfloat16)
     local_firsts = jnp.einsum(
         "bdl,blc->bdc", picker, result_low, preferred_element_type=jnp.float32
@@ -337,7 +347,7 @@
     )
 
 
-def body(
+def general_body(
     inputs,
     cotangent,
     doc_lengths,
@@ -495,6 +505,944 @@
     )
 
 
+BF = jnp.bfloat16
+F32 = jnp.float32
+MESH = pl.DeviceIdType.MESH
+ANY = pl.BlockSpec(memory_space=pl.ANY)
+SMEM = pl.BlockSpec(memory_space=pltpu.SMEM)
+ZS = 4
+CLASS_ROWS, B_QUERY, B_VALUE, B_OUT, GAIN1, SHIFT1, B_OUTER, GAIN2, SHIFT2, B_POOL = (0, 3, 4, 5, 6, 7, 8, 9, 10, 11)
+VEC_ROWS = 16
+
+
+def nn(a, b):
+    return lax.dot_general(a, b, (((1,), (0,)), ((), ())), preferred_element_type=F32)
+
+
+def nt(a, b):
+    return lax.dot_general(a, b, (((1,), (1,)), ((), ())), preferred_element_type=F32)
+
+
+def tn(a, b):
+    return lax.dot_general(a, b, (((0,), (0,)), ((), ())), preferred_element_type=F32)
+
+
+def my_place():
+    dp, fs = lax.axis_index("dp"), lax.axis_index("fsdp")
+    return dp // 2, lax.rem(dp, 2), fs // 2, lax.rem(fs, 2)
+
+
+def device_at(z, y, x, c):
+    return (z * 2 + y, x * 2 + c)
+
+
+def meet(partners):
+    barrier = pltpu.get_barrier_semaphore()
+    for partner in partners:
+        pl.semaphore_signal(barrier, inc=1, device_id=partner, device_id_type=MESH)
+    pl.semaphore_wait(barrier, len(partners))
+
+
+def all_partners(z, y, x, c):
+    found = [device_at(lax.rem(z + k, ZS), y, x, c) for k in range(1, ZS)]
+    found.append(device_at(z, 1 - y, x, c))
+    found.append(device_at(z, y, 1 - x, c))
+    found.append(device_at(z, y, x, 1 - c))
+    found.append(device_at(z, y, 1 - x, 1 - c))
+    return found
+
+
+def group_partner(k, x, c):
+    return (1 - x if k >= 2 else x, 1 - c if k % 2 == 1 else c)
+
+
+def gather_kernel(orders, *refs):
+    count = len(orders)
+    rows_ref, shards = refs[0], refs[1 : 1 + count]
+    seq_ref, wholes = refs[1 + count], refs[2 + count : 2 + 2 * count]
+    local_sem, row_send, row_recv, send_sem, recv_sem = refs[2 + 2 * count :]
+    z, y, x, c = my_place()
+    meet(all_partners(z, y, x, c))
+    mine = x * 2 + c
+    sent = []
+    got_rows = []
+    for k in range(1, 4):
+        px, pc = group_partner(k, x, c)
+        copy = pltpu.make_async_remote_copy(
+            src_ref=rows_ref.at[px * 2 + pc],
+            dst_ref=seq_ref.at[mine],
+            send_sem=row_send.at[k - 1],
+            recv_sem=row_recv.at[k - 1],
+            device_id=device_at(z, y, px, pc),
+            device_id_type=MESH,
+        )
+        copy.start()
+        sent.append(copy)
+        got_rows.append(copy)
+    own = pltpu.make_async_copy(rows_ref.at[mine], seq_ref.at[mine], local_sem.at[count])
+    own.start()
+    local = [own]
+
+    def place(rel):
+        dz, fy, fx, fc = rel
+        zz = lax.rem(z + dz, ZS)
+        yy = 1 - y if fy else y
+        xx = 1 - x if fx else x
+        cc = 1 - c if fc else c
+        return ((zz * 2 + yy) * 2 + xx) * 2 + cc
+
+    def slot(rel):
+        dz, fy, fx, fc = rel
+        return ((dz * 2 + fy) * 2 + fx) * 2 + fc
+
+    def send(a, rel, there, device, number):
+        source = shards[a] if slot(rel) == 0 else wholes[a].at[place(rel)]
+        copy = pltpu.make_async_remote_copy(
+            src_ref=source,
+            dst_ref=wholes[a].at[place(rel)],
+            send_sem=send_sem.at[a, number],
+            recv_sem=recv_sem.at[a, slot(there)],
+            device_id=device,
+            device_id_type=MESH,
+        )
+        copy.start()
+        sent.append(copy)
+
+    def arrive(a, rel):
+        block = wholes[a].at[place(rel)]
+        pltpu.make_async_remote_copy(
+            src_ref=block,
+            dst_ref=block,
+            send_sem=send_sem.at[a, 0],
+            recv_sem=recv_sem.at[a, slot(rel)],
+            device_id=device_at(z, y, x, 1 - c),
+            device_id_type=MESH,
+        ).wait_recv()
+
+    numbers = [0] * count
+
+    def forward_to(a, rel, axis):
+        numbers[a] += 1
+        dz, fy, fx, fc = rel
+        if axis == "y":
+            send(a, rel, (dz, 1 - fy, fx, fc), device_at(z, 1 - y, x, c), numbers[a] - 1)
+        elif axis == "x":
+            send(a, rel, (dz, fy, 1 - fx, fc), device_at(z, y, 1 - x, c), numbers[a] - 1)
+        else:
+            send(a, rel, (dz, fy, fx, 1 - fc), device_at(z, y, x, 1 - c), numbers[a] - 1)
+
+    for a in range(count):
+        keep = pltpu.make_async_copy(
+            shards[a], wholes[a].at[place((0, 0, 0, 0))], local_sem.at[a]
+        )
+        keep.start()
+        local.append(keep)
+        for k in (2, 1, 3):
+            numbers[a] += 1
+            send(
+                a, (0, 0, 0, 0), ((ZS - k) % ZS, 0, 0, 0),
+                device_at(lax.rem(z + k, ZS), y, x, c), numbers[a] - 1,
+            )
+        for axis in (*orders[a], "c"):
+            forward_to(a, (0, 0, 0, 0), axis)
+    for a in range(count):
+        for dz in (1, 3, 2):
+            arrive(a, (dz, 0, 0, 0))
+            for axis in (*orders[a], "c"):
+                forward_to(a, (dz, 0, 0, 0), axis)
+    for a in range(count):
+        first, second = orders[a]
+        for dz in (0, 1, 3, 2):
+            rel = (dz, int(first == "y"), int(first == "x"), 0)
+            arrive(a, rel)
+            forward_to(a, rel, second)
+            forward_to(a, rel, "c")
+    for a in range(count):
+        first, second = orders[a]
+        for dz in (0, 1, 3, 2):
+            for turn in (0, 1):
+                fy = 1 if second == "y" else turn
+                fx = 1 if second == "x" else turn
+                arrive(a, (dz, fy, fx, 0))
+                forward_to(a, (dz, fy, fx, 0), "c")
+    for a in range(count):
+        for dz in range(ZS):
+            for fy in (0, 1):
+                for fx in (0, 1):
+                    arrive(a, (dz, fy, fx, 1))
+    for copy in got_rows:
+        copy.wait_recv()
+    for copy in sent:
+        copy.wait_send()
+    for copy in local:
+        copy.wait()
+
+
+def gather_all(rows, shards, orders, collective_id):
+    count = len(shards)
+    whole = 8 * ZS
+    return pl.pallas_call(
+        functools.partial(gather_kernel, orders),
+        out_shape=[jax.ShapeDtypeStruct(rows.shape, rows.dtype)]
+        + [jax.ShapeDtypeStruct((whole,) + s.shape, s.dtype) for s in shards],
+        in_specs=[ANY] * (1 + count),
+        out_specs=[ANY] * (1 + count),
+        scratch_shapes=[
+            pltpu.SemaphoreType.DMA((count + 1,)),
+            pltpu.SemaphoreType.DMA((3,)),
+            pltpu.SemaphoreType.DMA((3,)),
+            pltpu.SemaphoreType.DMA((count, whole)),
+            pltpu.SemaphoreType.DMA((count, whole)),
+        ],
+        compiler_params=pltpu.CompilerParams(collective_id=collective_id, has_side_effects=True),
+        name="gather_weights",
+    )(rows, *shards)
+
+
+def scatter_kernel(orders, *refs):
+    count = len(orders)
+    rows_ref, logit_ref, parts = refs[0], refs[1], refs[2 : 2 + count]
+    back_ref, logits_ref, outs = refs[2 + count], refs[3 + count], refs[4 + count : 4 + 2 * count]
+    rest = refs[4 + 2 * count :]
+    local_sem, row_send, row_recv, send_sem, recv_sem = rest[:5]
+    keeps, firsts, seconds, thirds, fourths = (
+        rest[5 + i * count : 5 + (i + 1) * count] for i in range(5)
+    )
+    z, y, x, c = my_place()
+    mine = x * 2 + c
+    local = []
+    sent = []
+
+    def half(a, ref, at_first):
+        return ref.at[:, at_first] if orders[a][0] == "y" else ref.at[:, :, at_first]
+
+    own_loads = []
+    for a in range(count):
+        at = y if orders[a][0] == "y" else x
+        loads = []
+        for turn in (0, 1):
+            place = 1 - at if turn == 0 else at
+            if orders[a][0] == "y":
+                source = parts[a].at[:, place, :, c]
+            else:
+                source = parts[a].at[:, :, place, c]
+            copy = pltpu.make_async_copy(source, half(a, keeps[a], place), local_sem.at[a, turn])
+            copy.start()
+            loads.append(copy)
+        own_loads.append(loads)
+    meet(all_partners(z, y, x, c))
+
+    def push(source, target, a, number, device):
+        copy = pltpu.make_async_remote_copy(
+            src_ref=source,
+            dst_ref=target,
+            send_sem=send_sem.at[a, number],
+            recv_sem=recv_sem.at[a, number],
+            device_id=device,
+            device_id_type=MESH,
+        )
+        copy.start()
+        sent.append(copy)
+        return copy
+
+    sibling = []
+    for a in range(count):
+        at = y if orders[a][0] == "y" else x
+        copies = []
+        for turn in (0, 1):
+            place = 1 - at if turn == 0 else at
+            if orders[a][0] == "y":
+                source = parts[a].at[:, place, :, 1 - c]
+            else:
+                source = parts[a].at[:, :, place, 1 - c]
+            copies.append(
+                push(source, half(a, firsts[a], place), a, turn, device_at(z, y, x, 1 - c))
+            )
+        sibling.append(copies)
+    got_rows = []
+    for k in range(1, 4):
+        px, pc = group_partner(k, x, c)
+        for which, (source, target) in enumerate(
+            ((rows_ref.at[px * 2 + pc], back_ref.at[mine]), (logit_ref, logits_ref.at[mine]))
+        ):
+            copy = pltpu.make_async_remote_copy(
+                src_ref=source,
+                dst_ref=target,
+                send_sem=row_send.at[which, k - 1],
+                recv_sem=row_recv.at[which, k - 1],
+                device_id=device_at(z, y, px, pc),
+                device_id_type=MESH,
+            )
+            copy.start()
+            sent.append(copy)
+            got_rows.append(copy)
+    for which, (source, target) in enumerate(
+        ((rows_ref.at[mine], back_ref.at[mine]), (logit_ref, logits_ref.at[mine]))
+    ):
+        copy = pltpu.make_async_copy(source, target, local_sem.at[count, which])
+        copy.start()
+        local.append(copy)
+
+    def add_into(target, source):
+        total = functools.reduce(lambda p, q: p * q, target.shape[:-2], 1)
+        lead = target.shape[:-2]
+
+        def step(i, carry):
+            where = []
+            for size in reversed(lead):
+                where.append(lax.rem(i, size))
+                i = i // size
+            where = tuple(reversed(where))
+            target[where] = (target[where].astype(F32) + source[where].astype(F32)).astype(target.dtype)
+            return carry
+
+        lax.fori_loop(0, total, step, 0)
+
+    waits2 = []
+    for a in range(count):
+        first = orders[a][0]
+        at = y if first == "y" else x
+        own_loads[a][0].wait()
+        sibling[a][0].wait_recv()
+        add_into(half(a, keeps[a], 1 - at), half(a, firsts[a], 1 - at))
+        device = device_at(z, 1 - y, x, c) if first == "y" else device_at(z, y, 1 - x, c)
+        waits2.append(push(half(a, keeps[a], 1 - at), seconds[a], a, 2, device))
+    for a in range(count):
+        at = y if orders[a][0] == "y" else x
+        own_loads[a][1].wait()
+        sibling[a][1].wait_recv()
+        add_into(half(a, keeps[a], at), half(a, firsts[a], at))
+    waits3 = []
+    for a in range(count):
+        first = orders[a][0]
+        at, other = (y, x) if first == "y" else (x, y)
+        kept = half(a, keeps[a], at)
+        waits2[a].wait_recv()
+        add_into(kept.at[:, 1 - other], seconds[a].at[:, 1 - other])
+        device = device_at(z, y, 1 - x, c) if first == "y" else device_at(z, 1 - y, x, c)
+        waits3.append(push(kept.at[:, 1 - other], thirds[a], a, 3, device))
+        add_into(kept.at[:, other], seconds[a].at[:, other])
+    waits4 = []
+    for a in range(count):
+        first = orders[a][0]
+        at, other = (y, x) if first == "y" else (x, y)
+        kept = half(a, keeps[a], at).at[:, other]
+        waits3[a].wait_recv()
+        add_into(kept, thirds[a])
+        copies = []
+        for k in (2, 1, 3):
+            there = lax.rem(z + k, ZS)
+            copies.append(
+                push(kept.at[there], fourths[a].at[k - 1], a, 3 + k, device_at(there, y, x, c))
+            )
+        waits4.append(copies)
+    for a in range(count):
+        first = orders[a][0]
+        at, other = (y, x) if first == "y" else (x, y)
+        kept = half(a, keeps[a], at).at[:, other]
+        for copy in waits4[a]:
+            copy.wait_recv()
+        outs[a][...] = (
+            kept[z].astype(F32)
+            + fourths[a][0].astype(F32)
+            + fourths[a][1].astype(F32)
+            + fourths[a][2].astype(F32)
+        )
+    for copy in got_rows:
+        copy.wait_recv()
+    for copy in sent:
+        copy.wait_send()
+    for copy in local:
+        copy.wait()
+
+
+def scatter_all(rows, logit_block, parts, orders, collective_id):
+    count = len(parts)
+    blocks = [part.shape[1:] for part in parts]
+    kinds = [part.dtype for part in parts]
+    split = [part.reshape((ZS, 2, 2, 2) + block) for part, block in zip(parts, blocks)]
+    scratch = []
+    for lead in ((ZS, 2, 2), (ZS, 2, 2), (ZS, 2), (ZS,), (ZS - 1,)):
+        scratch += [pltpu.VMEM(lead + block, kind) for block, kind in zip(blocks, kinds)]
+    return pl.pallas_call(
+        functools.partial(scatter_kernel, orders),
+        out_shape=[
+            jax.ShapeDtypeStruct(rows.shape, rows.dtype),
+            jax.ShapeDtypeStruct((4,) + logit_block.shape, logit_block.dtype),
+        ]
+        + [jax.ShapeDtypeStruct(block, F32) for block in blocks],
+        in_specs=[ANY] * (2 + count),
+        out_specs=[ANY] * 2 + [pl.BlockSpec(memory_space=pltpu.VMEM)] * count,
+        scratch_shapes=[
+            pltpu.SemaphoreType.DMA((count + 1, 2)),
+            pltpu.SemaphoreType.DMA((2, 3)),
+            pltpu.SemaphoreType.DMA((2, 3)),
+            pltpu.SemaphoreType.DMA((count, 7)),
+            pltpu.SemaphoreType.DMA((count, 7)),
+        ]
+        + scratch,
+        compiler_params=pltpu.CompilerParams(
+            collective_id=collective_id, has_side_effects=True, vmem_limit_bytes=48 * 2**20
+        ),
+        name="scatter_gradients",
+    )(rows, logit_block, *split)
+
+
+def doc_ends(lens_ref):
+    ends = []
+    total = 0
+    for d in range(lens_ref.shape[0]):
+        total = total + lens_ref[d]
+        ends.append(total)
+    return ends
+
+
+def doc_numbers(places, ends):
+    number = jnp.zeros(places.shape, jnp.int32)
+    for end in ends:
+        number = number + (places >= end).astype(jnp.int32)
+    return number
+
+
+def attend_kernel(
+    lens_ref, x_ref, wq_ref, wk_ref, wv_ref, vec_ref, q_ref, k_ref, v_ref, att_ref, lse_ref, vt_ref
+):
+    x = x_ref[...]
+    length, width = q_ref.shape
+    chunk = 256
+    heads = width // HEAD_DIM
+    queries = (nn(x, wq_ref[...]) + vec_ref[B_QUERY : B_QUERY + 1, :]).astype(BF)
+    q_ref[...] = queries
+    k_ref[...] = nn(x, wk_ref[...]).astype(BF)
+    values = (nn(x, wv_ref[...]) + vec_ref[B_VALUE : B_VALUE + 1, :]).astype(BF)
+    v_ref[...] = values
+    vt_ref[...] = values.astype(F32).T.astype(BF)
+    ends = doc_ends(lens_ref)
+    key_doc = doc_numbers(lax.broadcasted_iota(jnp.int32, (length, 1), 0), ends)
+    lane_head = lax.broadcasted_iota(jnp.int32, (1, width), 1) // HEAD_DIM
+
+    def step(i, carry):
+        at = pl.multiple_of(i * chunk, chunk)
+        query_doc = doc_numbers(lax.broadcasted_iota(jnp.int32, (1, chunk), 1) + at, ends)
+        scaled = q_ref[pl.ds(at, chunk), :] * jnp.asarray(0.125, BF)
+        mixed = []
+        for h in range(heads):
+            own = jnp.where(lane_head == h, scaled, jnp.zeros_like(scaled))
+            blocks = []
+            for s in range(0, length, chunk):
+                scores = nt(k_ref[s : s + chunk, :], own)
+                blocks.append(jnp.where(key_doc[s : s + chunk] == query_doc, scores, -1000000000.0))
+            peak = functools.reduce(jnp.maximum, [jnp.max(b, axis=0, keepdims=True) for b in blocks])
+            exps = [jnp.exp(b - peak) for b in blocks]
+            total = functools.reduce(jnp.add, [jnp.sum(e, axis=0, keepdims=True) for e in exps])
+            scale = 1.0 / total
+            probs = jnp.concatenate([(e * scale).astype(BF) for e in exps], axis=0)
+            mixed.append(nn(vt_ref[h * HEAD_DIM : (h + 1) * HEAD_DIM, :], probs))
+            lse_ref[0, h : h + 1, pl.ds(at, chunk)] = peak + jnp.log(total)
+        att_ref[pl.ds(at, chunk), :] = jnp.concatenate(mixed, axis=0).T.astype(BF)
+        return carry
+
+    lax.fori_loop(0, length // chunk, step, 0)
+
+
+def attend(lens, rows, w_qkv, vectors):
+    length, width = rows.shape
+    group = 256
+    groups = width // group
+    whole = pl.BlockSpec((length, width), lambda g: (0, 0))
+    part = pl.BlockSpec((length, group), lambda g: (0, g))
+    return pl.pallas_call(
+        attend_kernel,
+        grid=(groups,),
+        out_shape=[jax.ShapeDtypeStruct((length, width), BF)] * 4
+        + [jax.ShapeDtypeStruct((groups, 8, length), F32)],
+        in_specs=[
+            SMEM,
+            whole,
+            pl.BlockSpec((width, group), lambda g: (0, g)),
+            pl.BlockSpec((width, group), lambda g: (0, g + groups)),
+            pl.BlockSpec((width, group), lambda g: (0, g + 2 * groups)),
+            pl.BlockSpec((VEC_ROWS, group), lambda g: (0, g)),
+        ],
+        out_specs=[part] * 4 + [pl.BlockSpec((1, 8, length), lambda g: (g, 0, 0))],
+        scratch_shapes=[pltpu.VMEM((group, length), BF)],
+        compiler_params=pltpu.CompilerParams(vmem_limit_bytes=48 * 2**20),
+        cost_estimate=pl.CostEstimate(flops=10 * 10**9, bytes_accessed=16 * 10**6, transcendentals=12 * 2**20),
+        name="attend",
+    )(lens, rows, w_qkv, w_qkv, w_qkv, vectors)
+
+
+def attend_back_kernel(
+    lens_ref, x_ref, wq_ref, wk_ref, wv_ref, q_ref, k_ref, v_ref, att_ref, datt_ref, lse_ref, start_ref,
+    dwq_ref, dwk_ref, dwv_ref, bias_ref, dx_ref, xt_ref, kt_ref, dot_ref, dq_ref, dk_ref, dv_ref, acc_ref,
+):
+    length, width = q_ref.shape
+    chunk = 256
+    heads = width // HEAD_DIM
+    group = pl.program_id(0)
+
+    @pl.when(group == 0)
+    def _():
+        xt_ref[...] = x_ref[...].astype(F32).T.astype(BF)
+        acc_ref[...] = start_ref[...]
+
+    kt_ref[...] = k_ref[...].astype(F32).T.astype(BF)
+    dot_ref[...] = (datt_ref[...].astype(F32) * att_ref[...].astype(F32)).T
+    dk_ref[...] = jnp.zeros_like(dk_ref)
+    dv_ref[...] = jnp.zeros_like(dv_ref)
+    ends = doc_ends(lens_ref)
+    key_doc = doc_numbers(lax.broadcasted_iota(jnp.int32, (length, 1), 0), ends)
+    lane_head = lax.broadcasted_iota(jnp.int32, (1, width), 1) // HEAD_DIM
+
+    def step(i, carry):
+        at = pl.multiple_of(i * chunk, chunk)
+        query_doc = doc_numbers(lax.broadcasted_iota(jnp.int32, (1, chunk), 1) + at, ends)
+        scaled = q_ref[pl.ds(at, chunk), :] * jnp.asarray(0.125, BF)
+        given = datt_ref[pl.ds(at, chunk), :]
+        own_q = [jnp.where(lane_head == h, scaled, jnp.zeros_like(scaled)) for h in range(heads)]
+        own_d = [jnp.where(lane_head == h, given, jnp.zeros_like(given)) for h in range(heads)]
+        all_probs = [[] for _ in range(length // chunk)]
+        all_grads = [[] for _ in range(length // chunk)]
+        for h in range(heads):
+            lse = lse_ref[0, h : h + 1, pl.ds(at, chunk)]
+            dots = jnp.sum(
+                dot_ref[h * HEAD_DIM : (h + 1) * HEAD_DIM, pl.ds(at, chunk)], axis=0, keepdims=True
+            )
+            for j in range(length // chunk):
+                s = j * chunk
+                scores = nt(k_ref[s : s + chunk, :], own_q[h])
+                scores = jnp.where(key_doc[s : s + chunk] == query_doc, scores, -1000000000.0)
+                probs = jnp.exp(scores - lse)
+                grad_probs = nt(v_ref[s : s + chunk, :], own_d[h])
+                all_grads[j].append((probs * (grad_probs - dots)).astype(BF))
+                all_probs[j].append(probs.astype(BF))
+        stacked_q = jnp.concatenate(own_q, axis=0)
+        stacked_d = jnp.concatenate(own_d, axis=0)
+        for j in range(length // chunk):
+            s = j * chunk
+            dk_ref[s : s + chunk, :] += nn(jnp.concatenate(all_grads[j], axis=1), stacked_q)
+            dv_ref[s : s + chunk, :] += nn(jnp.concatenate(all_probs[j], axis=1), stacked_d)
+        mixed = []
+        for h in range(heads):
+            column = jnp.concatenate([all_grads[j][h] for j in range(length // chunk)], axis=0)
+            mixed.append(nn(kt_ref[h * HEAD_DIM : (h + 1) * HEAD_DIM, :], column))
+        dq_ref[pl.ds(at, chunk), :] = (jnp.concatenate(mixed, axis=0).T * 0.125).astype(BF)
+        return carry
+
+    lax.fori_loop(0, length // chunk, step, 0)
+    grad_q = dq_ref[...]
+    grad_k = dk_ref[...].astype(BF)
+    grad_v = dv_ref[...].astype(BF)
+    xt = xt_ref[...]
+    dwq_ref[...] = nn(xt, grad_q).astype(BF)
+    dwk_ref[...] = nn(xt, grad_k).astype(BF)
+    dwv_ref[...] = nn(xt, grad_v).astype(BF)
+    bias_ref[0:1, :] = jnp.sum(grad_q.astype(F32), axis=0, keepdims=True)
+    bias_ref[1:2, :] = jnp.sum(grad_v.astype(F32), axis=0, keepdims=True)
+    acc_ref[...] += nt(grad_q, wq_ref[...]) + nt(grad_k, wk_ref[...]) + nt(grad_v, wv_ref[...])
+
+    @pl.when(group == pl.num_programs(0) - 1)
+    def _():
+        dx_ref[...] = acc_ref[...].astype(BF)
+
+
+def attend_back(lens, rows, w_qkv, q, k, v, att, datt, lse, grad_pre):
+    length, width = rows.shape
+    group = 256
+    groups = width // group
+    whole = pl.BlockSpec((length, width), lambda g: (0, 0))
+    part = pl.BlockSpec((length, group), lambda g: (0, g))
+    return pl.pallas_call(
+        attend_back_kernel,
+        grid=(groups,),
+        out_shape=[jax.ShapeDtypeStruct((width, width), BF)] * 3
+        + [jax.ShapeDtypeStruct((8, width), F32), jax.ShapeDtypeStruct((length, width), BF)],
+        in_specs=[
+            SMEM,
+            whole,
+            pl.BlockSpec((width, group), lambda g: (0, g)),
+            pl.BlockSpec((width, group), lambda g: (0, g + groups)),
+            pl.BlockSpec((width, group), lambda g: (0, g + 2 * groups)),
+            part, part, part, part, part,
+            pl.BlockSpec((1, 8, length), lambda g: (g, 0, 0)),
+            whole,
+        ],
+        out_specs=[pl.BlockSpec((width, group), lambda g: (0, g))] * 3
+        + [pl.BlockSpec((8, group), lambda g: (0, g)), whole],
+        scratch_shapes=[
+            pltpu.VMEM((width, length), BF),
+            pltpu.VMEM((group, length), BF),
+            pltpu.VMEM((group, length), F32),
+            pltpu.VMEM((length, group), BF),
+            pltpu.VMEM((length, group), F32),
+            pltpu.VMEM((length, group), F32),
+            pltpu.VMEM((length, width), F32),
+        ],
+        compiler_params=pltpu.CompilerParams(vmem_limit_bytes=56 * 2**20),
+        cost_estimate=pl.CostEstimate(flops=20 * 10**9, bytes_accessed=24 * 10**6, transcendentals=12 * 2**20),
+        name="attend_back",
+    )(lens, rows, w_qkv, w_qkv, w_qkv, q, k, v, att, datt, lse, grad_pre)
+
+
+def normal_parts(v):
+    bell = jnp.exp(v * v * -0.5)
+    t = 1.0 / (1.0 + jnp.abs(v) * 0.23164189)
+    tail = t * (0.127414796 + t * (-0.142248368 + t * (0.710706870 + t * (-0.726576013 + t * 0.530702714)))) * bell
+    return jnp.where(v >= 0.0, 1.0 - tail, tail), bell
+
+
+def centered_parts(values):
+    average = jnp.mean(values, axis=-1, keepdims=True)
+    centered = values - average
+    variance = jnp.mean(centered * centered, axis=-1, keepdims=True)
+    inverse = lax.rsqrt(variance + 1e-06)
+    return centered * inverse, inverse
+
+
+def dense_kernel(
+    lens_ref, labels_ref, x_ref, att_ref, w_inner_ref, w_out_ref, w_pool_ref, w_outer_ref, vec_ref, b_inner_ref, b_class_ref,
+    pre_ref, summed_ref, low_ref, act_ref, dact_ref, lo_ref, dpool_ref, first_ref, small_ref, logits_ref, picked_ref,
+):
+    step = pl.program_id(0)
+    rows = x_ref.shape[0]
+    hidden = w_inner_ref.shape[1]
+    chunk = 512
+
+    def vec(row):
+        return vec_ref[row : row + 1, :]
+
+    pre = x_ref[...].astype(F32) + (nn(att_ref[...], w_out_ref[...]) + vec(B_OUT))
+    pre_ref[...] = pre
+    normed = centered_parts(pre)[0] * vec(GAIN1) + vec(SHIFT1)
+    low = normed.astype(BF)
+    low_ref[...] = low
+    total = normed + vec(B_OUTER)
+    for s in range(0, hidden, chunk):
+        inner = nn(low, w_inner_ref[:, s : s + chunk]) + b_inner_ref[:, s : s + chunk]
+        phi, bell = normal_parts(inner)
+        activated = (inner * phi).astype(BF)
+        act_ref[:, s : s + chunk] = activated
+        dact_ref[:, s : s + chunk] = (phi + inner * bell * 0.3989422804014327).astype(BF)
+        total = total + nn(activated, w_outer_ref[s : s + chunk, :])
+    summed_ref[...] = total
+    result = (centered_parts(total)[0] * vec(GAIN2) + vec(SHIFT2)).astype(BF)
+    lo_ref[...] = result
+    ends = doc_ends(lens_ref)
+    docs = len(ends)
+    places = lax.broadcasted_iota(jnp.int32, (VEC_ROWS, rows), 1) + step * rows
+    row_doc = lax.broadcasted_iota(jnp.int32, (VEC_ROWS, rows), 0)
+    hit = jnp.zeros((VEC_ROWS, rows), jnp.bool_)
+    for d in range(docs):
+        hit = hit | ((row_doc == d) & (places == ends[d] - lens_ref[d]))
+    found = nn(jnp.where(hit, 1.0, 0.0).astype(BF), result)
+
+    @pl.when(step == 0)
+    def _():
+        picked_ref[...] = found
+
+    @pl.when(step > 0)
+    def _():
+        picked_ref[...] += found
+
+    @pl.when(step == pl.num_programs(0) - 1)
+    def _():
+        picked = picked_ref[...].astype(BF)
+        pooled = jnp.tanh(nn(picked, w_pool_ref[...]) + vec(B_POOL))
+        pooled_low = pooled.astype(BF)
+        table = vec_ref[...].astype(BF)
+        logits = nt(pooled_low, table) + b_class_ref[...]
+        column = lax.broadcasted_iota(jnp.int32, (VEC_ROWS, VEC_ROWS), 1)
+        row = lax.broadcasted_iota(jnp.int32, (VEC_ROWS, VEC_ROWS), 0)
+        logits_ref[...] = logits
+        live = column < CLASSES
+        shown = jnp.where(live, logits, -jnp.inf)
+        exps = jnp.where(live, jnp.exp(shown - jnp.max(shown, axis=-1, keepdims=True)), 0.0)
+        probs = exps / jnp.sum(exps, axis=-1, keepdims=True)
+        label = jnp.zeros((VEC_ROWS, VEC_ROWS), jnp.int32)
+        for d in range(docs):
+            label = jnp.where(row == d, labels_ref[d], label)
+        grad = jnp.where(live & (row < docs), probs - jnp.where(label == column, 1.0, 0.0), 0.0)
+        grad_low = grad.astype(BF)
+        grad_pool = (nn(grad_low, table) * (1.0 - pooled * pooled)).astype(BF)
+        dpool_ref[...] = tn(picked, grad_pool).astype(BF)
+        first_ref[...] = nt(grad_pool, w_pool_ref[...])
+        small_ref[0:16, :] = tn(grad_low, pooled_low)
+        small_ref[16:17, :] = jnp.sum(grad_pool.astype(F32), axis=0, keepdims=True)
+        width = small_ref.shape[1]
+        class_sum = jnp.sum(grad_low.astype(F32), axis=0, keepdims=True)
+        small_ref[17:18, :] = jnp.concatenate(
+            [class_sum, jnp.zeros((1, width - VEC_ROWS), F32)], axis=1
+        )
+
+
+def dense(lens, labels, rows, att, w_mid, w_outer, vectors, b_inner, b_class_row):
+    length, width = rows.shape
+    hidden = w_outer.shape[0]
+    tile = 256
+    steps = length // tile
+    part = pl.BlockSpec((tile, width), lambda i: (i, 0))
+    wide = pl.BlockSpec((tile, hidden), lambda i: (i, 0))
+
+    def fixed(shape, column=0):
+        return pl.BlockSpec(shape, lambda i: (0, column))
+
+    spots = hidden // width
+    return pl.pallas_call(
+        dense_kernel,
+        grid=(steps,),
+        out_shape=[
+            jax.ShapeDtypeStruct((length, width), F32),
+            jax.ShapeDtypeStruct((length, width), F32),
+            jax.ShapeDtypeStruct((length, width), BF),
+            jax.ShapeDtypeStruct((length, hidden), BF),
+            jax.ShapeDtypeStruct((length, hidden), BF),
+            jax.ShapeDtypeStruct((length, width), BF),
+            jax.ShapeDtypeStruct((width, width), BF),
+            jax.ShapeDtypeStruct((VEC_ROWS, width), F32),
+            jax.ShapeDtypeStruct((24, width), F32),
+            jax.ShapeDtypeStruct((VEC_ROWS, VEC_ROWS), F32),
+        ],
+        in_specs=[
+            SMEM, SMEM, part, part,
+            fixed((width, hidden)), fixed((width, width), spots), fixed((width, width), spots + 1),
+            fixed((hidden, width)), fixed((VEC_ROWS, width)), fixed((1, hidden)), fixed((1, VEC_ROWS)),
+        ],
+        out_specs=[
+            part, part, part, wide, wide, part,
+            fixed((width, width)), fixed((VEC_ROWS, width)), fixed((24, width)), fixed((VEC_ROWS, VEC_ROWS)),
+        ],
+        scratch_shapes=[pltpu.VMEM((VEC_ROWS, width), F32)],
+        compiler_params=pltpu.CompilerParams(vmem_limit_bytes=60 * 2**20),
+        cost_estimate=pl.CostEstimate(flops=11 * 10**9, bytes_accessed=40 * 10**6, transcendentals=3 * 2**20),
+        name="dense",
+    )(lens, labels, rows, att, w_mid, w_mid, w_mid, w_outer, vectors, b_inner, b_class_row)
+
+
+def norm_back(grad, values, gain):
+    hat, inverse = centered_parts(values)
+    scaled = grad * gain
+    mean_scaled = jnp.mean(scaled, axis=-1, keepdims=True)
+    mean_cross = jnp.mean(scaled * hat, axis=-1, keepdims=True)
+    back = (scaled - mean_scaled - hat * mean_cross) * inverse
+    return back, jnp.sum(grad * hat, axis=0, keepdims=True), jnp.sum(grad, axis=0, keepdims=True)
+
+
+def dense_back_kernel(
+    lens_ref, cot_ref, summed_ref, pre_ref, dact_ref, w_inner_ref, w_out_ref, w_outer_ref, vec_ref, first_ref,
+    outer_ref, inner_ref, branch_ref, datt_ref, gpre_ref, small_ref, bi_ref,
+):
+    step = pl.program_id(0)
+    rows = cot_ref.shape[0]
+    hidden = dact_ref.shape[1]
+    chunk = 512
+
+    def vec(row):
+        return vec_ref[row : row + 1, :]
+
+    @pl.when(step == 0)
+    def _():
+        small_ref[...] = jnp.zeros_like(small_ref)
+        bi_ref[...] = jnp.zeros_like(bi_ref)
+
+    grad = cot_ref[...].astype(F32)
+    places = lax.broadcasted_iota(jnp.int32, (rows, 1), 0) + step * rows
+    ends = doc_ends(lens_ref)
+    placed = jnp.zeros(grad.shape, F32)
+    for d in range(len(ends)):
+        placed = jnp.where(places == ends[d] - lens_ref[d], first_ref[d : d + 1, :], placed)
+    grad = grad + placed
+    grad_summed, gain2, shift2 = norm_back(grad, summed_ref[...], vec(GAIN2))
+    outer = grad_summed.astype(BF)
+    outer_ref[...] = outer
+    grad_normed = grad_summed
+    for s in range(0, hidden, chunk):
+        back = nt(outer, w_outer_ref[s : s + chunk, :])
+        inner = (back * dact_ref[:, s : s + chunk].astype(F32)).astype(BF)
+        inner_ref[:, s : s + chunk] = inner
+        bi_ref[:, s : s + chunk] += jnp.sum(inner.astype(F32), axis=0, keepdims=True)
+        grad_normed = grad_normed + nt(inner, w_inner_ref[:, s : s + chunk])
+    grad_pre, gain1, shift1 = norm_back(grad_normed, pre_ref[...], vec(GAIN1))
+    gpre_ref[...] = grad_pre
+    branch = grad_pre.astype(BF)
+    branch_ref[...] = branch
+    datt_ref[...] = nt(branch, w_out_ref[...]).astype(BF)
+    small_ref[0:1, :] += jnp.sum(outer.astype(F32), axis=0, keepdims=True)
+    small_ref[1:2, :] += gain2
+    small_ref[2:3, :] += shift2
+    small_ref[3:4, :] += jnp.sum(branch.astype(F32), axis=0, keepdims=True)
+    small_ref[4:5, :] += gain1
+    small_ref[5:6, :] += shift1
+
+
+def dense_back(lens, cot, summed, pre, dact, w_mid, w_outer, vectors, first):
+    length, width = cot.shape
+    hidden = w_outer.shape[0]
+    tile = 256
+    part = pl.BlockSpec((tile, width), lambda i: (i, 0))
+    wide = pl.BlockSpec((tile, hidden), lambda i: (i, 0))
+
+    def fixed(shape, column=0):
+        return pl.BlockSpec(shape, lambda i: (0, column))
+
+    spots = hidden // width
+    return pl.pallas_call(
+        dense_back_kernel,
+        grid=(length // tile,),
+        out_shape=[
+            jax.ShapeDtypeStruct((length, width), BF),
+            jax.ShapeDtypeStruct((length, hidden), BF),
+            jax.ShapeDtypeStruct((length, width), BF),
+            jax.ShapeDtypeStruct((length, width), BF),
+            jax.ShapeDtypeStruct((length, width), F32),
+            jax.ShapeDtypeStruct((8, width), F32),
+            jax.ShapeDtypeStruct((1, hidden), F32),
+        ],
+        in_specs=[
+            SMEM, part, part, part, wide,
+            fixed((width, hidden)), fixed((width, width), spots), fixed((hidden, width)),
+            fixed((VEC_ROWS, width)), fixed((VEC_ROWS, width)),
+        ],
+        out_specs=[part, wide, part, part, part, fixed((8, width)), fixed((1, hidden))],
+        compiler_params=pltpu.CompilerParams(vmem_limit_bytes=60 * 2**20),
+        cost_estimate=pl.CostEstimate(flops=11 * 10**9, bytes_accessed=40 * 10**6, transcendentals=0),
+        name="dense_back",
+    )(lens, cot, summed, pre, dact, w_mid, w_mid, w_outer, vectors, first)
+
+
+def exchange(blocks):
+    count = blocks.shape[0]
+    mine = lax.axis_index("fsdp")
+    held = jnp.zeros_like(blocks)
+    own = lax.dynamic_index_in_dim(blocks, mine, 0, keepdims=True)
+    held = lax.dynamic_update_slice_in_dim(held, own, mine, 0)
+    for k in range(1, count):
+        leaving = lax.dynamic_index_in_dim(blocks, lax.rem(mine + k, count), 0, keepdims=True)
+        came = lax.ppermute(leaving, "fsdp", [(i, (i + k) % count) for i in range(count)])
+        held = lax.dynamic_update_slice_in_dim(held, came, lax.rem(mine - k + count, count), 0)
+    return held
+
+
+def fast_body(
+    inputs, cotangent, doc_lengths, labels, w_query, b_query, w_key, w_value, b_value, w_out, b_out, first_gain, first_shift,
+    w_inner, b_inner, w_outer, b_outer, second_gain, second_shift, w_pool, b_pool, w_class, b_class,
+):
+    seqs, local_len, width = inputs.shape
+    length = seqs * local_len
+    devices = 8 * ZS
+    mine = lax.axis_index("fsdp")
+    docs = doc_lengths.shape[1]
+    own_lens = lax.dynamic_index_in_dim(doc_lengths, mine, 0, keepdims=False)
+    own_labels = lax.dynamic_index_in_dim(labels, mine, 0, keepdims=False)
+
+    share = width // devices
+    hidden_share = b_inner.shape[0]
+    hidden = hidden_share * devices
+    qkv_shard = jnp.concatenate([w_query, w_key, w_value], axis=1).astype(BF)
+    mid_shard = jnp.concatenate([w_inner, w_out, w_pool], axis=1).astype(BF)
+    outer_shard = w_outer.astype(BF)
+    vec_shard = jnp.concatenate(
+        [
+            w_class.T.reshape(-1), b_query, b_value, b_out, first_gain, first_shift, b_outer, second_gain, second_shift,
+            b_pool, b_inner,
+        ]
+    )
+    vec_len = vec_shard.shape[0]
+    vec_shard = jnp.pad(vec_shard, (0, 1024 - vec_len)).reshape(8, 128).astype(BF).astype(F32)
+
+    rows, w_qkv, vec_all, w_mid, w_outer_all = gather_all(
+        inputs, [qkv_shard, vec_shard, mid_shard, outer_shard], ["xy", "xy", "xy", "yx"], 1
+    )
+    rows = rows.reshape(length, width)
+    w_qkv = w_qkv.reshape(width, 3 * width)
+    w_mid = w_mid.reshape(width, hidden + 2 * width)
+    w_outer_all = w_outer_all.reshape(hidden, width)
+    flat_vec = vec_all.reshape(devices, 1024)
+    rows_used = B_POOL + 1
+    vectors = flat_vec[:, : rows_used * share].reshape(devices, rows_used, share).transpose(1, 0, 2).reshape(rows_used, width)
+    vectors = jnp.pad(vectors, ((0, VEC_ROWS - rows_used), (0, 0)))
+    b_inner_row = flat_vec[:, rows_used * share : vec_len].reshape(1, hidden)
+    b_class_row = jnp.pad(b_class, (0, VEC_ROWS - CLASSES)).reshape(1, VEC_ROWS)
+
+    cot = exchange(cotangent).reshape(length, width)
+    q, k, v, att, lse = attend(own_lens, rows, w_qkv, vectors)
+    pre, summed, low, act, dact, result, grad_pool, first, small_a, logits = dense(
+        own_lens, own_labels, rows, att, w_mid, w_outer_all, vectors, b_inner_row, b_class_row
+    )
+    layer_out = exchange(result.reshape(seqs, local_len, width))
+    outer, inner, branch, datt, grad_pre, small_b, grad_b_inner = dense_back(
+        own_lens, cot, summed, pre, dact, w_mid, w_outer_all, vectors, first
+    )
+    grad_outer_w = tn(act, outer).astype(BF)
+    grad_inner_w = tn(low, inner).astype(BF)
+    grad_out_w = tn(att, branch).astype(BF)
+    gwq, gwk, gwv, small_c, grad_rows = attend_back(own_lens, rows, w_qkv, q, k, v, att, datt, lse, grad_pre)
+
+    grad_vec = jnp.concatenate(
+        [
+            small_a[0:CLASSES], small_c[0:2], small_b[3:4], small_b[4:6], small_b[0:1], small_b[1:3], small_a[16:17],
+        ],
+        axis=0,
+    )
+    grad_vec = grad_vec.reshape(rows_used, devices, share).transpose(1, 0, 2).reshape(devices, rows_used * share)
+    grad_vec = jnp.concatenate(
+        [
+            grad_vec,
+            grad_b_inner.reshape(devices, hidden_share),
+            jnp.broadcast_to(small_a[17:18, :CLASSES], (devices, CLASSES)),
+        ],
+        axis=1,
+    )
+    grad_vec = jnp.pad(grad_vec, ((0, 0), (0, 1024 - grad_vec.shape[1]))).reshape(devices, 8, 128)
+    logit_block = jnp.pad(logits[:docs, :CLASSES], ((0, 8 - docs), (0, 128 - CLASSES)))
+    scattered = scatter_all(
+        grad_rows.reshape(seqs, local_len, width),
+        logit_block,
+        [
+            grad_inner_w.reshape(devices, share, hidden),
+            grad_outer_w.reshape(devices, hidden_share, width),
+            grad_out_w.reshape(devices, share, width),
+            grad_pool.reshape(devices, share, width),
+            gwq.reshape(devices, share, width),
+            gwk.reshape(devices, share, width),
+            gwv.reshape(devices, share, width),
+            grad_vec,
+        ],
+        ["yx", "xy", "yx", "yx", "yx", "yx", "yx", "yx"],
+        2,
+    )
+    grad_inputs, all_logits, o_inner, o_outer, o_out, o_pool, o_query, o_key, o_value, o_vec = scattered
+    o_vec = o_vec.reshape(1024)
+
+    def vec_part(row):
+        return o_vec[row * share : (row + 1) * share]
+
+    after = rows_used * share + hidden_share
+    return (
+        layer_out,
+        all_logits[:, :docs, :CLASSES],
+        grad_inputs,
+        o_query,
+        vec_part(B_QUERY),
+        o_key,
+        o_value,
+        vec_part(B_VALUE),
+        o_out,
+        vec_part(B_OUT),
+        vec_part(GAIN1),
+        vec_part(SHIFT1),
+        o_inner,
+        o_vec[rows_used * share : after],
+        o_outer,
+        vec_part(B_OUTER),
+        vec_part(GAIN2),
+        vec_part(SHIFT2),
+        o_pool,
+        vec_part(B_POOL),
+        o_vec[: CLASSES * share].reshape(CLASSES, share).T,
+        o_vec[after : after + CLASSES],
+    )
+
+
 def solution(mesh):
     placed = (
         P("dp", "fsdp", None),
@@ -521,8 +1469,10 @@
         P(("dp", "fsdp"), None),
         P(),
     )
+    sizes = (mesh.shape["dp"], mesh.shape["fsdp"])
+    chosen = fast_body if sizes == (8, 4) else general_body
     return jax.shard_map(
-        body,
+        chosen,
         mesh=mesh,
         in_specs=placed,
         out_specs=(

time: 1820 us -> 453 us (0.25)
  waiting for transfers between devices: 912 us -> 0.02 us
  Pallas kernels: 0 us -> 365 us
  matrix products: 373 us -> 18.6 us
  local copies, waits for them, and re-layouts: 277 us -> 49.6 us
  blocking collectives: 136 us -> 0 us
  other arithmetic: 79.9 us -> 11.9 us
  between operations: 22.4 us -> 1.21 us
    reduce_scatter x12 -> x0, waiting for transfers between devices: 486 us -> none  [the longest x1 142 us: body(): lax.psum_scatter(grad_sums[9], ('dp', 'fsdp'), scatter_dimension=0, tiled...]
    pallas_call x0 -> x6, Pallas kernels: none -> 365 us  [the longest x1 125 us: scatter_all(): pl.pallas_call(functools.partial(scatter_kernel, orders), out_shape=[jax....]
    dot_general x248 -> x3, matrix products: 373 us -> 18.6 us  [tn(): lax.dot_general(a, b, (((0,), (0,)), ((), ())), preferred_element_type=F32)]
    all_gather x15 -> x0, waiting for transfers between devices: 217 us -> none  [the longest x1 53.3 us: body(): lax.all_gather(pieces[11], ('dp', 'fsdp'), axis=0, tiled=True)]
    unnamed x33 -> x0, waiting for transfers between devices: 209 us -> none
    slice x113 -> x12, local copies, waits for them, and re-layouts: 140 us -> 6.54 us  [the longest x1 1.4 us: fast_body(): small_c[0:2]]
    unnamed x1388 -> x103, local copies, waits for them, and re-layouts: 128 us -> 20.8 us
    unnamed x2 -> x0, blocking collectives: 84 us -> none
  transfers between devices with their start and end apart: 30 -> 6, of which waited for: 19 -> 0; matrix products, arithmetic and copies ran while one was open for 31% -> 13% of each run, Pallas kernels for 0% -> 81%
where the time goes in v1:
time: 453 us; the launch traced here: 452 us
  Pallas kernels  365 us (81%)
  local copies, waits for them, and re-layouts  49.6 us (11%)
  matrix products  18.6 us (4%)
  other arithmetic  11.9 us (3%)
  starting transfers between devices  5.68 us (1%)
    pallas_call x1, Pallas kernels, scatter_all(): pl.pallas_call(functools.partial(scatter_kernel, orders), out_shape=[jax....  125 us
    pallas_call x1, Pallas kernels, gather_all(): pl.pallas_call(functools.partial(gather_kernel, orders), out_shape=[jax.S...  87.5 us
    pallas_call x1, Pallas kernels, attend_back(): pl.pallas_call(attend_back_kernel, grid=(groups,), out_shape=[jax.ShapeDt...  53 us
    pallas_call x1, Pallas kernels, attend(): pl.pallas_call(attend_kernel, grid=(groups,), out_shape=[jax.ShapeDtypeSt...  40.7 us
    pallas_call x1, Pallas kernels, dense(): pl.pallas_call(dense_kernel, grid=(steps,), out_shape=[jax.ShapeDtypeStru...  33.9 us
    pallas_call x1, Pallas kernels, dense_back(): pl.pallas_call(dense_back_kernel, grid=(length // tile,), out_shape=[jax....  25.1 us
    unnamed x103, local copies, waits for them, and re-layouts  20.8 us
    dot_general x3, matrix products, tn(): lax.dot_general(a, b, (((0,), (0,)), ((), ())), preferred_element_type=F32)  18.6 us
  transfers between devices with their start and end apart: 6, of which 0 were waited for; matrix products, arithmetic and copies ran while one was open for 13% of the time, Pallas kernels for 81%

profile of v1, /device:TPU:0, one launch (start us, length us, event | category | flops | bytes accessed | tf_op | source)
XLA Modules:
  0.0 452.1 jit_solution(3971169982069058784)
XLA Ops:
  0.8 1.3 copy-done.26
  2.2 1.1 constant_dynamic-slice_fusion.5
  3.2 2.4 collective-permute-start.5
  5.6 1.1 collective-permute-start.4
  7.7 0.9 convert.56
  8.6 0.9 convert.57
  9.4 0.9 convert.58
  10.3 0.9 convert.71
  11.2 0.9 convert.72
  12.1 1.0 convert.70
  13.1 1.6 convert_element_type.33.refs_4_
  16.1 87.5 %gather_weights.1 = (bf16[4,256,768]{2,1,0:T(8,128)(2,1)}, bf16[32,24,2304]{2,1,0:T(8,128)(2,1)}, f32[32,8,128]{2,1,0:T(8,128)}, bf16[32,24,4608]{2,1,0:T(8,128)(2,1)}, bf16[32,96,768]{2,1,0:T(8,128)(2,1)}) custom-call(bf16[4,256,768]{2,1,0:T(8,128)(2,1)} %refs_0_.1, bf16[24,2304]{1,0:T(8,128)(2,1)} %pad_maximum_fusion.1.refs_1_, ...), custom_call_target="tpu_custom_call" | custom-call | tf_op jit(solution)/shard_map/gather_weights/pallas_call | solution.py:684
  103.6 0.9 copy.62
  106.1 1.2 fusion
  107.4 40.7 %attend.1 = (bf16[1024,768]{1,0:T(8,128)(2,1)S(1)}, bf16[1024,768]{1,0:T(8,128)(2,1)S(1)}, bf16[1024,768]{1,0:T(8,128)(2,1)S(1)}, bf16[1024,768]{1,0:T(8,128)(2,1)}, f32[3,8,1024]{2,1,0:T(8,128)S(1)}) custom-call(s32[4]{0:T(128)S(1)} %get-tuple-element.191.lens_ref, bf16[1024,768]{1,0:T(8,128)(2,1)} %bitcast.83, bf16[768,2304]{1,0:T(8,128)(2,1)} %bitcast.77, ...), custom_call_target="tpu_custom_call" | custom-call | flops 10000000000 | bytes 16000000 | tf_op jit(solution)/shard_map/attend/pallas_call | solution.py:954
  148.1 1.2 copy-done.20
  149.3 1.2 copy-done.21
  150.4 1.2 copy-done.22
  152.3 33.9 %dense.1 = (f32[1024,768]{1,0:T(8,128)}, f32[1024,768]{1,0:T(8,128)}, bf16[1024,768]{1,0:T(8,128)(2,1)}, bf16[1024,3072]{1,0:T(8,128)(2,1)}, bf16[1024,3072]{1,0...) custom-call(s32[4]{0:T(128)} %copy-done.19, ...), custom_call_target="tpu_custom_call" | custom-call | flops 11000000512 | bytes 40000000 | tf_op jit(solution)/shard_map/dense/pallas_call | solution.py:1190
  186.2 1.2 broadcast.19.clone
  187.4 0.7 copy-done.27
  188.2 1.2 constant_dynamic-slice_fusion.2
  189.7 1.9 collective-permute-start.1
  191.6 1.3 slice.77
  192.9 0.7 slice.73
  195.7 1.1 copy-done.25
  196.9 25.1 %dense_back.1 = (bf16[1024,768]{1,0:T(8,128)(2,1)}, bf16[1024,3072]{1,0:T(8,128)(2,1)}, bf16[1024,768]{1,0:T(8,128)(2,1)}, bf16[1024,768]{1,0:T(8,128)(2,1)}, f3...) custom-call(s32[4]{0:T(128)} %copy-done.19, bf16[1024,768]{1,0:T(8,128)(2,1)} %bitcast.60, ...), custom_call_target="tpu_custom_call" | custom-call | flops 11000000512 | bytes 40000000 | tf_op jit(solution)/shard_map/dense_back/pallas_call | solution.py:1288
  222.0 9.3 %convolution_convert_fusion = bf16[3072,768]{1,0:T(8,128)(2,1)} fusion(bf16[1024,3072]{1,0:T(8,128)(2,1)} %get-tuple-element.85, bf16[1024,768]{1,0:T(8,128)(2,1)} %get-tuple-element.86), kind=kOutput, calls=%fused_computation | convolution fusion | flops 4834197504 | bytes 12582912 | tf_op jit(solution)/shard_map/dot_general | solution.py:527
  231.3 6.9 %convolution_convert_fusion.1 = bf16[768,3072]{1,0:T(8,128)(2,1)} fusion(bf16[1024,768]{1,0:T(8,128)(2,1)S(1)} %copy-done.44, bf16[1024,3072]{1,0:T(8,128)(2,1)S(1)} %copy-done.41), kind=kOutput, calls=%fused_computation.1 | convolution fusion | flops 4834197504 | bytes 12582912 | tf_op jit(solution)/shard_map/dot_general | solution.py:527
  238.1 53.0 %attend_back.1 = (bf16[768,768]{1,0:T(8,128)(2,1)}, bf16[768,768]{1,0:T(8,128)(2,1)}, bf16[768,768]{1,0:T(8,128)(2,1)}, f32[8,768]{1,0:T(8,128)}, bf16[1024,768]{1,0:T(8,128)(2,1)}) custom-call(s32[4]{0:T(128)} %copy-done.19, bf16[1024,768]{1,0:T(8,128)(2,1)} %bitcast.85, bf16[768,2304]{1,0:T(8,128)(2,1)} %bitcast.80, bf16[768,2304]{1,0:T(8,128)(2,1)} %bitcast.81, ...), custom_call_target="tpu_custom_call" | custom-call | flops 20000000000 | bytes 24000000 | tf_op jit(solution)/shard_map/attend_back/pallas_call | solution.py:1055
  291.8 2.5 convolution_convert_fusion.2
  294.3 0.8 constant_dynamic-update-slice_fusion.5
  295.0 1.4 slice.74
  297.0 2.0 reduce.3
  298.9 1.4 reshape.118
  300.3 2.7 concatenate.22
  303.0 1.6 reshape.116
  304.6 1.7 copy.55
  306.3 1.6 copy.56
  308.0 0.9 maximum_maximum_fusion
  308.9 1.3 copy-done.3
  310.2 124.9 %scatter_gradients.1 = (bf16[4,256,768]{2,1,0:T(8,128)(2,1)}, f32[4,8,128]{2,1,0:T(8,128)S(1)}, f32[24,3072]{1,0:T(8,128)S(1)}, f32[96,768]{1,0:T(8,128)S(1)}, f...) custom-call(bf16[4,256,768]{2,1,0:T(8,128)(2,1)} %bitcast.59, ...), custom_call_target="tpu_custom_call" | custom-call | tf_op jit(solution)/shard_map/scatter_gradients/pallas_call | solution.py:867
  435.8 0.7 copy-done.6
  442.1 1.8 constant_dynamic-update-slice_fusion.4
  444.5 1.8 constant_dynamic-update-slice_fusion.3
  446.3 1.1 copy.79
  450.0 0.7 copy.84
  450.7 0.7 copy.85
  (139 shorter events, 18.4 us)
Async XLA Ops:
  0.7 1.4 copy-start.26
  2.1 4.6 %copy-start.30 = (f32[24]{0:T(128)S(1)}, f32[24]{0:T(128)}, u32[]{:S(2)}) copy-start(f32[24]{0:T(128)} %param.28) | copy-start | bytes 292
  2.1 4.6 %copy-start.31 = (f32[24]{0:T(128)S(1)}, f32[24]{0:T(128)}, u32[]{:S(2)}) copy-start(f32[24]{0:T(128)} %param.31) | copy-start | bytes 292
  2.1 4.6 %copy-start.32 = (f32[24]{0:T(128)S(1)}, f32[24]{0:T(128)}, u32[]{:S(2)}) copy-start(f32[24]{0:T(128)} %param.33) | copy-start | bytes 292
  2.1 4.6 %copy-start.33 = (f32[24]{0:T(128)S(1)}, f32[24]{0:T(128)}, u32[]{:S(2)}) copy-start(f32[24]{0:T(128)} %param.34) | copy-start | bytes 292
  2.1 4.7 %copy-start.34 = (f32[24]{0:T(128)S(1)}, f32[24]{0:T(128)}, u32[]{:S(2)}) copy-start(f32[24]{0:T(128)} %param.35) | copy-start | bytes 292
  2.1 4.7 %copy-start.35 = (f32[96]{0:T(128)S(1)}, f32[96]{0:T(128)}, u32[]{:S(2)}) copy-start(f32[96]{0:T(128)} %param.37) | copy-start | bytes 1156
  2.1 4.7 %copy-start.36 = (f32[24]{0:T(128)S(1)}, f32[24]{0:T(128)}, u32[]{:S(2)}) copy-start(f32[24]{0:T(128)} %param.39) | copy-start | bytes 292
  2.1 4.7 %copy-start.37 = (f32[24]{0:T(128)S(1)}, f32[24]{0:T(128)}, u32[]{:S(2)}) copy-start(f32[24]{0:T(128)} %param.40) | copy-start | bytes 292
  2.1 4.7 %copy-start.38 = (f32[24]{0:T(128)S(1)}, f32[24]{0:T(128)}, u32[]{:S(2)}) copy-start(f32[24]{0:T(128)} %param.41) | copy-start | bytes 292
  2.1 4.7 %copy-start.39 = (f32[24]{0:T(128)S(1)}, f32[24]{0:T(128)}, u32[]{:S(2)}) copy-start(f32[24]{0:T(128)} %param.43) | copy-start | bytes 292
  2.1 4.7 %copy-start.29 = (f32[24,3]{0,1:T(4,128)S(1)}, f32[24,3]{0,1:T(4,128)}, u32[]{:S(2)}) copy-start(f32[24,3]{0,1:T(4,128)} %param.44) | copy-start | bytes 868
  3.2 192.5 %collective-permute-start.5 = (bf16[1,256,768]{2,1,0:T(8,128)(2,1)S(1)}, bf16[1,256,768]{2,1,0:T(8,128)(2,1)S(1)}, u32[]{:S(2)}, u32[]{:S(2)}) collective-permute-start(bf16[1,256,768]{2,1,0:T(8,128)(2,1)S(1)} %get-tuple-element.172), channel_id=1, source_target_pairs={{0,3},{1,0},{2,1},{3,2},{4,7},{5,4},{6,5},{7,6},{8,11},{9,8},{10,9... | collective-permute-start | bytes 1179656 | tf_op jit(solution)/shard_map/ppermute | solution.py:1320
  5.6 190.0 %collective-permute-start.3 = (bf16[1,256,768]{2,1,0:T(8,128)(2,1)}, bf16[1,256,768]{2,1,0:T(8,128)(2,1)S(1)}, u32[]{:S(2)}, u32[]{:S(2)}) collective-permute-start(bf16[1,256,768]{2,1,0:T(8,128)(2,1)} %get-tuple-element.173), channel_id=1, source_target_pairs={{0,1},{1,2},{2,3},{3,0},{4,5},{5,6},{6,7},{7,4},{8,9},{9,10},{10,1... | collective-permute-start | bytes 1179656 | tf_op jit(solution)/shard_map/ppermute | solution.py:1320
  5.6 190.0 %collective-permute-start.4 = (bf16[1,256,768]{2,1,0:T(8,128)(2,1)}, bf16[1,256,768]{2,1,0:T(8,128)(2,1)S(1)}, u32[]{:S(2)}, u32[]{:S(2)}) collective-permute-start(bf16[1,256,768]{2,1,0:T(8,128)(2,1)} %get-tuple-element.175), channel_id=1, source_target_pairs={{0,2},{1,3},{2,0},{3,1},{4,6},{5,7},{6,4},{7,5},{8,10},{9,11},{10,... | collective-permute-start | bytes 1179656 | tf_op jit(solution)/shard_map/ppermute | solution.py:1320
  14.7 89.8 %copy-start.40 = (f32[3]{0:T(128)S(1)}, f32[3]{0:T(128)}, u32[]{:S(2)}) copy-start(f32[3]{0:T(128)} %param.45) | copy-start | bytes 40
  107.4 40.7 %copy-start.19 = (s32[4]{0:T(128)}, s32[4]{0:T(128)S(1)}, u32[]{:S(2)}) copy-start(s32[4]{0:T(128)S(1)} %get-tuple-element.191.lens_ref) | copy-start | bytes 52
  107.4 40.7 %copy-start.18 = (f32[16,768]{1,0:T(8,128)}, f32[16,768]{1,0:T(8,128)S(1)}, u32[]{:S(2)}) copy-start(f32[16,768]{1,0:T(8,128)S(1)} %pad.22.vec_ref) | copy-start | bytes 147460
  148.1 1.2 copy-start.20
  149.3 1.2 copy-start.21
  150.4 1.2 copy-start.22
  151.6 0.6 copy-start.23
  186.2 2.0 copy-start.27
  189.3 255.2 %collective-permute-start.2 = (bf16[1,256,768]{2,1,0:T(8,128)(2,1)}, bf16[1,256,768]{2,1,0:T(8,128)(2,1)}, u32[]{:S(2)}, u32[]{:S(2)}) collective-permute-start(bf16[1,256,768]{2,1,0:T(8,128)(2,1)} %get-tuple-element.176), channel_id=1, source_target_pairs={{0,3},{1,0},{2,1},{3,2},{4,7},{5,4},{6,5},{7,6},{8,11},{9,8},{10,9... | collective-permute-start | bytes 1179656 | tf_op jit(solution)/shard_map/ppermute | solution.py:1320
  189.7 252.4 %collective-permute-start.1 = (bf16[1,256,768]{2,1,0:T(8,128)(2,1)}, bf16[1,256,768]{2,1,0:T(8,128)(2,1)}, u32[]{:S(2)}, u32[]{:S(2)}) collective-permute-start(bf16[1,256,768]{2,1,0:T(8,128)(2,1)} %get-tuple-element.177), channel_id=1, source_target_pairs={{0,2},{1,3},{2,0},{3,1},{4,6},{5,7},{6,4},{7,5},{8,10},{9,11},{10,... | collective-permute-start | bytes 1179656 | tf_op jit(solution)/shard_map/ppermute | solution.py:1320
  195.6 98.7 %collective-permute-start = (bf16[1,256,768]{2,1,0:T(8,128)(2,1)}, bf16[1,256,768]{2,1,0:T(8,128)(2,1)S(1)}, u32[]{:S(2)}, u32[]{:S(2)}) collective-permute-start(bf16[1,256,768]{2,1,0:T(8,128)(2,1)} %get-tuple-element.178), channel_id=1, source_target_pairs={{0,1},{1,2},{2,3},{3,0},{4,5},{5,6},{6,7},{7,4},{8,9},{9,10},{10,1... | collective-permute-start | bytes 1179656 | tf_op jit(solution)/shard_map/ppermute | solution.py:1320
  195.7 1.1 copy-start.25
  221.9 9.3 %copy-start.41 = (bf16[1024,3072]{1,0:T(8,128)(2,1)S(1)}, bf16[1024,3072]{1,0:T(8,128)(2,1)}, u32[]{:S(2)}) copy-start(bf16[1024,3072]{1,0:T(8,128)(2,1)} %get-tuple-element.84) | copy-start | bytes 18874372
  222.0 9.3 %copy-start.44 = (bf16[1024,768]{1,0:T(8,128)(2,1)S(1)}, bf16[1024,768]{1,0:T(8,128)(2,1)}, u32[]{:S(2)}) copy-start(bf16[1024,768]{1,0:T(8,128)(2,1)} %get-tuple-element.83) | copy-start | bytes 4718596
  238.1 53.0 %copy-start.28 = (f32[8,768]{1,0:T(8,128)S(1)}, f32[8,768]{1,0:T(8,128)}, u32[]{:S(2)}) copy-start(f32[8,768]{1,0:T(8,128)} %get-tuple-element.94) | copy-start | bytes 73732
  238.1 53.7 %copy-start.42 = (bf16[1024,768]{1,0:T(8,128)(2,1)S(1)}, bf16[1024,768]{1,0:T(8,128)(2,1)}, u32[]{:S(2)}) copy-start(bf16[1024,768]{1,0:T(8,128)(2,1)} %get-tuple-element.67.att_ref) | copy-start | bytes 4718596
  238.1 53.7 %copy-start.43 = (bf16[1024,768]{1,0:T(8,128)(2,1)S(1)}, bf16[1024,768]{1,0:T(8,128)(2,1)}, u32[]{:S(2)}) copy-start(bf16[1024,768]{1,0:T(8,128)(2,1)} %get-tuple-element.87) | copy-start | bytes 4718596
  291.8 17.1 %copy-start.2 = (bf16[768,768]{1,0:T(8,128)(2,1)S(1)}, bf16[768,768]{1,0:T(8,128)(2,1)}, u32[]{:S(2)}) copy-start(bf16[768,768]{1,0:T(8,128)(2,1)} %get-tuple-element.90) | copy-start | bytes 3538948
  294.3 14.6 %copy-start = (bf16[768,768]{1,0:T(8,128)(2,1)S(1)}, bf16[768,768]{1,0:T(8,128)(2,1)}, u32[]{:S(2)}) copy-start(bf16[768,768]{1,0:T(8,128)(2,1)} %get-tuple-element.88) | copy-start | bytes 3538948
  294.3 14.6 %copy-start.1 = (bf16[768,768]{1,0:T(8,128)(2,1)S(1)}, bf16[768,768]{1,0:T(8,128)(2,1)}, u32[]{:S(2)}) copy-start(bf16[768,768]{1,0:T(8,128)(2,1)} %get-tuple-element.89) | copy-start | bytes 3538948
  308.9 1.3 copy-start.3
  435.1 0.7 copy-start.4
  435.8 0.7 copy-start.6
  437.1 0.6 copy-start.10
  437.7 0.6 copy-start.12
  439.6 6.6 %copy-start.24 = (bf16[4,256,768]{2,1,0:T(8,128)(2,1)S(1)}, bf16[4,256,768]{2,1,0:T(8,128)(2,1)}, u32[]{:S(2)}) copy-start(bf16[4,256,768]{2,1,0:T(8,128)(2,1)} %get-tuple-element.217) | copy-start | bytes 4718596
  446.3 1.2 copy-start.17
  446.3 1.8 copy-start.15
  446.3 2.5 copy-start.13
  446.3 3.1 copy-start.11
  446.3 3.7 copy-start.7
  446.3 4.4 copy-start.5
  447.5 4.0 copy-start.9
  (3 other events, 1.9 us)

commit v2 on v1

--- a/solution.py
+++ b/solution.py
@@ -699,195 +699,6 @@
     )(rows, *shards)
 
 
-def scatter_kernel(orders, *refs):
-    count = len(orders)
-    rows_ref, logit_ref, parts = refs[0], refs[1], refs[2 : 2 + count]
-    back_ref, logits_ref, outs = refs[2 + count], refs[3 + count], refs[4 + count : 4 + 2 * count]
-    rest = refs[4 + 2 * count :]
-    local_sem, row_send, row_recv, send_sem, recv_sem = rest[:5]
-    keeps, firsts, seconds, thirds, fourths = (
-        rest[5 + i * count : 5 + (i + 1) * count] for i in range(5)
-    )
-    z, y, x, c = my_place()
-    mine = x * 2 + c
-    local = []
-    sent = []
-
-    def half(a, ref, at_first):
-        return ref.at[:, at_first] if orders[a][0] == "y" else ref.at[:, :, at_first]
-
-    own_loads = []
-    for a in range(count):
-        at = y if orders[a][0] == "y" else x
-        loads = []
-        for turn in (0, 1):
-            place = 1 - at if turn == 0 else at
-            if orders[a][0] == "y":
-                source = parts[a].at[:, place, :, c]
-            else:
-                source = parts[a].at[:, :, place, c]
-            copy = pltpu.make_async_copy(source, half(a, keeps[a], place), local_sem.at[a, turn])
-            copy.start()
-            loads.append(copy)
-        own_loads.append(loads)
-    meet(all_partners(z, y, x, c))
-
-    def push(source, target, a, number, device):
-        copy = pltpu.make_async_remote_copy(
-            src_ref=source,
-            dst_ref=target,
-            send_sem=send_sem.at[a, number],
-            recv_sem=recv_sem.at[a, number],
-            device_id=device,
-            device_id_type=MESH,
-        )
-        copy.start()
-        sent.append(copy)
-        return copy
-
-    sibling = []
-    for a in range(count):
-        at = y if orders[a][0] == "y" else x
-        copies = []
-        for turn in (0, 1):
-            place = 1 - at if turn == 0 else at
-            if orders[a][0] == "y":
-                source = parts[a].at[:, place, :, 1 - c]
-            else:
-                source = parts[a].at[:, :, place, 1 - c]
-            copies.append(
-                push(source, half(a, firsts[a], place), a, turn, device_at(z, y, x, 1 - c))
-            )
-        sibling.append(copies)
-    got_rows = []
-    for k in range(1, 4):
-        px, pc = group_partner(k, x, c)
-        for which, (source, target) in enumerate(
-            ((rows_ref.at[px * 2 + pc], back_ref.at[mine]), (logit_ref, logits_ref.at[mine]))
-        ):
-            copy = pltpu.make_async_remote_copy(
-                src_ref=source,
-                dst_ref=target,
-                send_sem=row_send.at[which, k - 1],
-                recv_sem=row_recv.at[which, k - 1],
-                device_id=device_at(z, y, px, pc),
-                device_id_type=MESH,
-            )
-            copy.start()
-            sent.append(copy)
-            got_rows.append(copy)
-    for which, (source, target) in enumerate(
-        ((rows_ref.at[mine], back_ref.at[mine]), (logit_ref, logits_ref.at[mine]))
-    ):
-        copy = pltpu.make_async_copy(source, target, local_sem.at[count, which])
-        copy.start()
-        local.append(copy)
-
-    def add_into(target, source):
-        total = functools.reduce(lambda p, q: p * q, target.shape[:-2], 1)
-        lead = target.shape[:-2]
-
-        def step(i, carry):
-            where = []
-            for size in reversed(lead):
-                where.append(lax.rem(i, size))
-                i = i // size
-            where = tuple(reversed(where))
-            target[where] = (target[where].astype(F32) + source[where].astype(F32)).astype(target.dtype)
-            return carry
-
-        lax.fori_loop(0, total, step, 0)
-
-    waits2 = []
-    for a in range(count):
-        first = orders[a][0]
-        at = y if first == "y" else x
-        own_loads[a][0].wait()
-        sibling[a][0].wait_recv()
-        add_into(half(a, keeps[a], 1 - at), half(a, firsts[a], 1 - at))
-        device = device_at(z, 1 - y, x, c) if first == "y" else device_at(z, y, 1 - x, c)
-        waits2.append(push(half(a, keeps[a], 1 - at), seconds[a], a, 2, device))
-    for a in range(count):
-        at = y if orders[a][0] == "y" else x
-        own_loads[a][1].wait()
-        sibling[a][1].wait_recv()
-        add_into(half(a, keeps[a], at), half(a, firsts[a], at))
-    waits3 = []
-    for a in range(count):
-        first = orders[a][0]
-        at, other = (y, x) if first == "y" else (x, y)
-        kept = half(a, keeps[a], at)
-        waits2[a].wait_recv()
-        add_into(kept.at[:, 1 - other], seconds[a].at[:, 1 - other])
-        device = device_at(z, y, 1 - x, c) if first == "y" else device_at(z, 1 - y, x, c)
-        waits3.append(push(kept.at[:, 1 - other], thirds[a], a, 3, device))
-        add_into(kept.at[:, other], seconds[a].at[:, other])
-    waits4 = []
-    for a in range(count):
-        first = orders[a][0]
-        at, other = (y, x) if first == "y" else (x, y)
-        kept = half(a, keeps[a], at).at[:, other]
-        waits3[a].wait_recv()
-        add_into(kept, thirds[a])
-        copies = []
-        for k in (2, 1, 3):
-            there = lax.rem(z + k, ZS)
-            copies.append(
-                push(kept.at[there], fourths[a].at[k - 1], a, 3 + k, device_at(there, y, x, c))
-            )
-        waits4.append(copies)
-    for a in range(count):
-        first = orders[a][0]
-        at, other = (y, x) if first == "y" else (x, y)
-        kept = half(a, keeps[a], at).at[:, other]
-        for copy in waits4[a]:
-            copy.wait_recv()
-        outs[a][...] = (
-            kept[z].astype(F32)
-            + fourths[a][0].astype(F32)
-            + fourths[a][1].astype(F32)
-            + fourths[a][2].astype(F32)
-        )
-    for copy in got_rows:
-        copy.wait_recv()
-    for copy in sent:
-        copy.wait_send()
-    for copy in local:
-        copy.wait()
-
-
-def scatter_all(rows, logit_block, parts, orders, collective_id):
-    count = len(parts)
-    blocks = [part.shape[1:] for part in parts]
-    kinds = [part.dtype for part in parts]
-    split = [part.reshape((ZS, 2, 2, 2) + block) for part, block in zip(parts, blocks)]
-    scratch = []
-    for lead in ((ZS, 2, 2), (ZS, 2, 2), (ZS, 2), (ZS,), (ZS - 1,)):
-        scratch += [pltpu.VMEM(lead + block, kind) for block, kind in zip(blocks, kinds)]
-    return pl.pallas_call(
-        functools.partial(scatter_kernel, orders),
-        out_shape=[
-            jax.ShapeDtypeStruct(rows.shape, rows.dtype),
-            jax.ShapeDtypeStruct((4,) + logit_block.shape, logit_block.dtype),
-        ]
-        + [jax.ShapeDtypeStruct(block, F32) for block in blocks],
-        in_specs=[ANY] * (2 + count),
-        out_specs=[ANY] * 2 + [pl.BlockSpec(memory_space=pltpu.VMEM)] * count,
-        scratch_shapes=[
-            pltpu.SemaphoreType.DMA((count + 1, 2)),
-            pltpu.SemaphoreType.DMA((2, 3)),
-            pltpu.SemaphoreType.DMA((2, 3)),
-            pltpu.SemaphoreType.DMA((count, 7)),
-            pltpu.SemaphoreType.DMA((count, 7)),
-        ]
-        + scratch,
-        compiler_params=pltpu.CompilerParams(
-            collective_id=collective_id, has_side_effects=True, vmem_limit_bytes=48 * 2**20
-        ),
-        name="scatter_gradients",
-    )(rows, logit_block, *split)
-
-
 def doc_ends(lens_ref):
     ends = []
     total = 0
@@ -959,9 +770,9 @@
         in_specs=[
             SMEM,
             whole,
-            pl.BlockSpec((width, group), lambda g: (0, g)),
-            pl.BlockSpec((width, group), lambda g: (0, g + groups)),
-            pl.BlockSpec((width, group), lambda g: (0, g + 2 * groups)),
+            pl.BlockSpec((width, group), lambda g: (0, 3 * g)),
+            pl.BlockSpec((width, group), lambda g: (0, 3 * g + 1)),
+            pl.BlockSpec((width, group), lambda g: (0, 3 * g + 2)),
             pl.BlockSpec((VEC_ROWS, group), lambda g: (0, g)),
         ],
         out_specs=[part] * 4 + [pl.BlockSpec((1, 8, length), lambda g: (g, 0, 0))],
@@ -972,17 +783,228 @@
     )(lens, rows, w_qkv, w_qkv, w_qkv, vectors)
 
 
-def attend_back_kernel(
-    lens_ref, x_ref, wq_ref, wk_ref, wv_ref, q_ref, k_ref, v_ref, att_ref, datt_ref, lse_ref, start_ref,
-    dwq_ref, dwk_ref, dwv_ref, bias_ref, dx_ref, xt_ref, kt_ref, dot_ref, dq_ref, dk_ref, dv_ref, acc_ref,
-):
+DENSE = 4
+SCATTER_ORDERS = ("yx", "xy", "yx", "yx", "yx", "yx", "yx")
+TABLE_ROWS = 24
+
+
+def attend_back_kernel(groups, *refs):
+    items = DENSE + groups
+    lens_ref, x_ref, w_ref, q_ref, k_ref, v_ref, att_ref, datt_ref, lse_ref, start_ref = refs[:10]
+    small_a_ref, small_b_ref, bi_ref, logit_ref = refs[10:14]
+    parts = refs[14 : 14 + DENSE]
+    back_ref, logits_ref, table_ref = refs[18:21]
+    dense_outs, (out_q, out_k, out_v) = refs[21 : 21 + DENSE], refs[21 + DENSE : 24 + DENSE]
+    rest = refs[24 + DENSE :]
+    xt_ref, kt_ref, dot_ref, dq_ref, dk_ref, dv_ref, acc_ref, dx_ref, bias_ref, dw_ref, tab_ref, tab_in_ref = rest[:12]
+    local_sem, row_send, row_recv, tab_send, tab_recv, send_sem, recv_sem = rest[12:19]
+    rest = rest[19:]
+    keeps, rest = rest[:DENSE], rest[DENSE:]
+    firsts, seconds, thirds, fourths = (rest[j * items : (j + 1) * items] for j in range(4))
+
     length, width = q_ref.shape
     chunk = 256
+    points = length // chunk
     heads = width // HEAD_DIM
     group = pl.program_id(0)
+    z, y, x, c = my_place()
+    mine = x * 2 + c
+
+    def axes(a):
+        return (y, x) if SCATTER_ORDERS[a][0] == "y" else (x, y)
+
+    def device_along(axis):
+        return device_at(z, 1 - y, x, c) if axis == "y" else device_at(z, y, 1 - x, c)
+
+    def half(a, ref, place):
+        return ref.at[:, place] if SCATTER_ORDERS[a][0] == "y" else ref.at[:, :, place]
+
+    def whole_of(a, core):
+        ref = parts[a] if a < DENSE else dw_ref.at[a - DENSE]
+        return ref.at[:, :, :, core]
+
+    def kept(a):
+        return keeps[a] if a < DENSE else whole_of(a, c)
+
+    def load(a, turn):
+        place = 1 - axes(a)[0] if turn == 0 else axes(a)[0]
+        return pltpu.make_async_copy(
+            half(a, whole_of(a, c), place), half(a, keeps[a], place), local_sem.at[a, turn]
+        )
+
+    def copy_of(a, number):
+        at, other = axes(a)
+        if number < 2:
+            place = 1 - at if number == 0 else at
+            source, target = half(a, whole_of(a, 1 - c), place), half(a, firsts[a], place)
+            device = device_at(z, y, x, 1 - c)
+        elif number == 2:
+            source, target = half(a, kept(a), 1 - at), seconds[a]
+            device = device_along(SCATTER_ORDERS[a][0])
+        elif number == 3:
+            source, target = half(a, kept(a), at).at[:, 1 - other], thirds[a]
+            device = device_along(SCATTER_ORDERS[a][1])
+        else:
+            there = lax.rem(z + number - 3, ZS)
+            source, target = half(a, kept(a), at).at[:, other].at[there], fourths[a].at[number - 4]
+            device = device_at(there, y, x, c)
+        return pltpu.make_async_remote_copy(
+            src_ref=source,
+            dst_ref=target,
+            send_sem=send_sem.at[a, number],
+            recv_sem=recv_sem.at[a, number],
+            device_id=device,
+            device_id_type=MESH,
+        )
+
+    def add_into(target, source):
+        lead = target.shape[:-2]
+        total = functools.reduce(lambda p, q: p * q, lead, 1)
+
+        def step(i, carry):
+            where = []
+            for size in reversed(lead):
+                where.append(lax.rem(i, size))
+                i = i // size
+            where = tuple(reversed(where))
+            target[where] = (target[where].astype(F32) + source[where].astype(F32)).astype(target.dtype)
+            return carry
+
+        lax.fori_loop(0, total, step, 0)
+
+    def begin(a):
+        if a < DENSE:
+            load(a, 0).start()
+            load(a, 1).start()
+        copy_of(a, 0).start()
+        copy_of(a, 1).start()
+
+    def after_core(a, turn):
+        place = 1 - axes(a)[0] if turn == 0 else axes(a)[0]
+        if a < DENSE:
+            load(a, turn).wait()
+        copy_of(a, turn).wait_recv()
+        add_into(half(a, kept(a), place), half(a, firsts[a], place))
+        if turn == 0:
+            copy_of(a, 2).start()
+
+    def after_first(a):
+        at, other = axes(a)
+        ours = half(a, kept(a), at)
+        copy_of(a, 2).wait_recv()
+        add_into(ours.at[:, 1 - other], seconds[a].at[:, 1 - other])
+        copy_of(a, 3).start()
+        add_into(ours.at[:, other], seconds[a].at[:, other])
+
+    def after_second(a):
+        at, other = axes(a)
+        copy_of(a, 3).wait_recv()
+        add_into(half(a, kept(a), at).at[:, other], thirds[a])
+        for number in (5, 4, 6):
+            copy_of(a, number).start()
+
+    def finish(a):
+        at, other = axes(a)
+        for number in (4, 5, 6):
+            copy_of(a, number).wait_recv()
+        ours = half(a, kept(a), at).at[:, other]
+        total = (
+            ours[z].astype(F32)
+            + fourths[a][0].astype(F32)
+            + fourths[a][1].astype(F32)
+            + fourths[a][2].astype(F32)
+        )
+        if a < DENSE:
+            dense_outs[a][...] = total
+        else:
+            s = (a - DENSE) * width
+            for j, out in enumerate((out_q, out_k, out_v)):
+                out[:, s : s + width] = total[:, j * width : (j + 1) * width]
+
+    def row_copy(which, k):
+        px, pc = group_partner(k, x, c)
+        if which == 0:
+            source, target = dx_ref.at[px * 2 + pc], back_ref.at[mine]
+        else:
+            source, target = logit_ref, logits_ref.at[mine]
+        return pltpu.make_async_remote_copy(
+            src_ref=source,
+            dst_ref=target,
+            send_sem=row_send.at[which, k - 1],
+            recv_sem=row_recv.at[which, k - 1],
+            device_id=device_at(z, y, px, pc),
+            device_id_type=MESH,
+        )
+
+    def row_own(which):
+        if which == 0:
+            source, target = dx_ref.at[mine], back_ref.at[mine]
+        else:
+            source, target = logit_ref, logits_ref.at[mine]
+        return pltpu.make_async_copy(source, target, local_sem.at[DENSE, which])
+
+    def table_copy(level):
+        if level < 3:
+            source, target = tab_ref.at[level], tab_in_ref.at[level]
+            device = (
+                device_at(z, y, x, 1 - c), device_at(z, 1 - y, x, c), device_at(z, y, 1 - x, c)
+            )[level]
+        else:
+            source, target = tab_ref.at[3], tab_in_ref.at[3 + z]
+            device = device_at(lax.rem(z + level - 2, ZS), y, x, c)
+        return pltpu.make_async_remote_copy(
+            src_ref=source,
+            dst_ref=target,
+            send_sem=tab_send.at[level],
+            recv_sem=tab_recv.at[level],
+            device_id=device,
+            device_id_type=MESH,
+        )
+
+    def table_wait(level):
+        if level < 3:
+            table_copy(level).wait_recv()
+        else:
+            slot = tab_in_ref.at[3 + lax.rem(z + ZS - (level - 2), ZS)]
+            pltpu.make_async_remote_copy(
+                src_ref=slot,
+                dst_ref=slot,
+                send_sem=tab_send.at[level],
+                recv_sem=tab_recv.at[level],
+                device_id=device_at(lax.rem(z + level - 2, ZS), y, x, c),
+                device_id_type=MESH,
+            ).wait_recv()
+
+    def table_level(level):
+        table_wait(level)
+        tab_ref[level + 1] = tab_ref[level] + tab_in_ref[level]
+        if level < 2:
+            table_copy(level + 1).start()
+        else:
+            tab_in_ref[3 + z] = tab_ref[3]
+            for nxt in (4, 3, 5):
+                table_copy(nxt).start()
+
+    dense_items = tuple(range(DENSE))
+    plan = {
+        2: [functools.partial(after_core, 0, 0), functools.partial(after_core, 1, 0)],
+        3: [functools.partial(after_core, a, 0) for a in dense_items[2:]] + [functools.partial(after_core, 0, 1)],
+        4: [functools.partial(begin, DENSE)] + [functools.partial(after_core, a, 1) for a in dense_items[1:]],
+        5: [functools.partial(after_core, DENSE, 0), functools.partial(after_core, DENSE, 1)],
+        8: [functools.partial(begin, DENSE + 1), functools.partial(after_first, 0)],
+        9: [functools.partial(after_core, DENSE + 1, 0), functools.partial(after_core, DENSE + 1, 1), functools.partial(after_first, 1)],
+        10: [functools.partial(after_first, a) for a in dense_items[2:]],
+        11: [functools.partial(after_second, 0), functools.partial(after_second, 1)],
+    }
 
     @pl.when(group == 0)
     def _():
+        meet(all_partners(z, y, x, c))
+        for a in range(DENSE):
+            begin(a)
+        for k in range(1, 4):
+            row_copy(1, k).start()
+        row_own(1).start()
         xt_ref[...] = x_ref[...].astype(F32).T.astype(BF)
         acc_ref[...] = start_ref[...]
 
@@ -995,6 +1017,13 @@
     lane_head = lax.broadcasted_iota(jnp.int32, (1, width), 1) // HEAD_DIM
 
     def step(i, carry):
+        for point, actions in plan.items():
+
+            @pl.when((group == point // points) & (i == point % points))
+            def _(actions=actions):
+                for action in actions:
+                    action()
+
         at = pl.multiple_of(i * chunk, chunk)
         query_doc = doc_numbers(lax.broadcasted_iota(jnp.int32, (1, chunk), 1) + at, ends)
         scaled = q_ref[pl.ds(at, chunk), :] * jnp.asarray(0.125, BF)
@@ -1029,46 +1058,117 @@
         dq_ref[pl.ds(at, chunk), :] = (jnp.concatenate(mixed, axis=0).T * 0.125).astype(BF)
         return carry
 
-    lax.fori_loop(0, length // chunk, step, 0)
-    grad_q = dq_ref[...]
-    grad_k = dk_ref[...].astype(BF)
-    grad_v = dv_ref[...].astype(BF)
+    lax.fori_loop(0, points, step, 0)
     xt = xt_ref[...]
-    dwq_ref[...] = nn(xt, grad_q).astype(BF)
-    dwk_ref[...] = nn(xt, grad_k).astype(BF)
-    dwv_ref[...] = nn(xt, grad_v).astype(BF)
-    bias_ref[0:1, :] = jnp.sum(grad_q.astype(F32), axis=0, keepdims=True)
-    bias_ref[1:2, :] = jnp.sum(grad_v.astype(F32), axis=0, keepdims=True)
-    acc_ref[...] += nt(grad_q, wq_ref[...]) + nt(grad_k, wk_ref[...]) + nt(grad_v, wv_ref[...])
-
-    @pl.when(group == pl.num_programs(0) - 1)
+    grads = (dq_ref[...], dk_ref[...].astype(BF), dv_ref[...].astype(BF))
+    block = dw_ref.shape[1:6]
+    for j, grad in enumerate(grads):
+        dw_ref[group, :, :, :, :, :, j * width : (j + 1) * width] = nn(xt, grad).reshape(block + (width,)).astype(BF)
+    bias_ref[group, 0:1, :] = jnp.sum(grads[0].astype(F32), axis=0, keepdims=True)
+    bias_ref[group, 1:2, :] = jnp.sum(grads[2].astype(F32), axis=0, keepdims=True)
+    total = acc_ref[...]
+    for j, grad in enumerate(grads):
+        total = total + nt(grad, w_ref[:, j * width : (j + 1) * width])
+    acc_ref[...] = total
+
+    @pl.when(group == groups - 1)
     def _():
-        dx_ref[...] = acc_ref[...].astype(BF)
-
-
-def attend_back(lens, rows, w_qkv, q, k, v, att, datt, lse, grad_pre):
+        last = items - 1
+        begin(last)
+        dx_ref[...] = acc_ref[...].reshape(dx_ref.shape).astype(BF)
+        for k in (3, 2, 1):
+            row_copy(0, k).start()
+        row_own(0).start()
+        tab_ref[0, 0:CLASSES] = small_a_ref[0:CLASSES]
+        for g in range(groups):
+            tab_ref[0, B_QUERY : B_QUERY + 2, g * width : (g + 1) * width] = bias_ref[g, 0:2, :]
+        for row, (ref, at) in {
+            B_OUT: (small_b_ref, 3), GAIN1: (small_b_ref, 4), SHIFT1: (small_b_ref, 5), B_OUTER: (small_b_ref, 0),
+            GAIN2: (small_b_ref, 1), SHIFT2: (small_b_ref, 2), B_POOL: (small_a_ref, 16), 16: (small_a_ref, 17),
+        }.items():
+            tab_ref[0, row : row + 1] = ref[at : at + 1, :]
+        full = small_a_ref.shape[1]
+        for j in range(4):
+            tab_ref[0, 12 + j : 13 + j] = bi_ref[:, j * full : (j + 1) * full]
+        tab_ref[0, 17:TABLE_ROWS] = jnp.zeros((TABLE_ROWS - 17, full), F32)
+        table_copy(0).start()
+        after_first(DENSE)
+        after_core(last, 0)
+        after_core(last, 1)
+        table_level(0)
+        for a in dense_items[2:]:
+            after_second(a)
+        after_first(DENSE + 1)
+        table_level(1)
+        finish(0)
+        finish(1)
+        after_second(DENSE)
+        after_first(last)
+        table_level(2)
+        after_second(DENSE + 1)
+        for a in dense_items[2:]:
+            finish(a)
+        after_second(last)
+        finish(DENSE)
+        finish(DENSE + 1)
+        for level in (3, 4, 5):
+            table_wait(level)
+        table_ref[...] = (tab_in_ref[3] + tab_in_ref[4]) + (tab_in_ref[5] + tab_in_ref[6])
+        finish(last)
+        for a in range(items):
+            for number in range(7):
+                copy_of(a, number).wait_send()
+        for level in range(6):
+            table_copy(level).wait_send()
+        for which in (0, 1):
+            for k in range(1, 4):
+                row_copy(which, k).wait_recv()
+                row_copy(which, k).wait_send()
+            row_own(which).wait()
+
+
+def attend_back(lens, rows, w_groups, q, k, v, att, datt, lse, grad_pre, small_a, small_b, grad_b_inner, logit_block, parts):
     length, width = rows.shape
     group = 256
     groups = width // group
-    whole = pl.BlockSpec((length, width), lambda g: (0, 0))
+    local_len = length // 4
+    share = width // (8 * ZS)
+    once = pl.Buffered(buffer_count=1)
+    whole = pl.BlockSpec((length, width), lambda g: (0, 0), pipeline_mode=once)
     part = pl.BlockSpec((length, group), lambda g: (0, g))
+    blocks = [p.shape[1:] for p in parts]
+    split = [p.reshape((ZS, 2, 2, 2) + b) for p, b in zip(parts, blocks)]
+    blocks = blocks + [(share, 3 * group)] * groups
+    hbm = pl.BlockSpec(memory_space=pl.ANY)
+
+    def fixed(shape):
+        return pl.BlockSpec(shape, lambda g: (0,) * len(shape))
+
+    results = [b for b in blocks[:DENSE]] + [(share, width)] * 3
+    arriving = []
+    for lead in ((ZS, 2, 2), (ZS, 2), (ZS,), (ZS - 1,)):
+        arriving += [pltpu.VMEM(lead + b, BF) for b in blocks]
+    items = len(blocks)
     return pl.pallas_call(
-        attend_back_kernel,
+        functools.partial(attend_back_kernel, groups),
         grid=(groups,),
-        out_shape=[jax.ShapeDtypeStruct((width, width), BF)] * 3
-        + [jax.ShapeDtypeStruct((8, width), F32), jax.ShapeDtypeStruct((length, width), BF)],
+        out_shape=[
+            jax.ShapeDtypeStruct((4, local_len, width), BF),
+            jax.ShapeDtypeStruct((4,) + logit_block.shape, F32),
+            jax.ShapeDtypeStruct((TABLE_ROWS, width), F32),
+        ]
+        + [jax.ShapeDtypeStruct(r, F32) for r in results],
         in_specs=[
             SMEM,
             whole,
-            pl.BlockSpec((width, group), lambda g: (0, g)),
-            pl.BlockSpec((width, group), lambda g: (0, g + groups)),
-            pl.BlockSpec((width, group), lambda g: (0, g + 2 * groups)),
+            pl.BlockSpec((width, 3 * group), lambda g: (0, g)),
             part, part, part, part, part,
             pl.BlockSpec((1, 8, length), lambda g: (g, 0, 0)),
             whole,
-        ],
-        out_specs=[pl.BlockSpec((width, group), lambda g: (0, g))] * 3
-        + [pl.BlockSpec((8, group), lambda g: (0, g)), whole],
+            fixed(small_a.shape), fixed(small_b.shape), fixed(grad_b_inner.shape), hbm,
+        ]
+        + [hbm] * DENSE,
+        out_specs=[hbm, hbm, fixed((TABLE_ROWS, width))] + [fixed(r) for r in results],
         scratch_shapes=[
             pltpu.VMEM((width, length), BF),
             pltpu.VMEM((group, length), BF),
@@ -1077,11 +1177,26 @@
             pltpu.VMEM((length, group), F32),
             pltpu.VMEM((length, group), F32),
             pltpu.VMEM((length, width), F32),
-        ],
-        compiler_params=pltpu.CompilerParams(vmem_limit_bytes=56 * 2**20),
-        cost_estimate=pl.CostEstimate(flops=20 * 10**9, bytes_accessed=24 * 10**6, transcendentals=12 * 2**20),
+            pltpu.VMEM((4, local_len, width), BF),
+            pltpu.VMEM((groups, 8, group), F32),
+            pltpu.VMEM((groups, ZS, 2, 2, 2, share, 3 * group), BF),
+            pltpu.VMEM((4, TABLE_ROWS, width), F32),
+            pltpu.VMEM((3 + ZS, TABLE_ROWS, width), F32),
+            pltpu.SemaphoreType.DMA((DENSE + 1, 2)),
+            pltpu.SemaphoreType.DMA((2, 3)),
+            pltpu.SemaphoreType.DMA((2, 3)),
+            pltpu.SemaphoreType.DMA((6,)),
+            pltpu.SemaphoreType.DMA((6,)),
+            pltpu.SemaphoreType.DMA((items, 7)),
+            pltpu.SemaphoreType.DMA((items, 7)),
+        ]
+        + [pltpu.VMEM((ZS, 2, 2) + b, BF) for b in blocks[:DENSE]]
+        + arriving,
+        compiler_params=pltpu.CompilerParams(
+            collective_id=2, has_side_effects=True, vmem_limit_bytes=60 * 2**20
+        ),
         name="attend_back",
-    )(lens, rows, w_qkv, w_qkv, w_qkv, q, k, v, att, datt, lse, grad_pre)
+    )(lens, rows, w_groups, q, k, v, att, datt, lse, grad_pre, small_a, small_b, grad_b_inner, logit_block, *split)
 
 
 def normal_parts(v):
@@ -1337,7 +1452,10 @@
     share = width // devices
     hidden_share = b_inner.shape[0]
     hidden = hidden_share * devices
-    qkv_shard = jnp.concatenate([w_query, w_key, w_value], axis=1).astype(BF)
+    group = 256
+    qkv_shard = jnp.concatenate(
+        [w[:, s : s + group] for s in range(0, width, group) for w in (w_query, w_key, w_value)], axis=1
+    ).astype(BF)
     mid_shard = jnp.concatenate([w_inner, w_out, w_pool], axis=1).astype(BF)
     outer_shard = w_outer.astype(BF)
     vec_shard = jnp.concatenate(
@@ -1375,71 +1493,42 @@
     grad_outer_w = tn(act, outer).astype(BF)
     grad_inner_w = tn(low, inner).astype(BF)
     grad_out_w = tn(att, branch).astype(BF)
-    gwq, gwk, gwv, small_c, grad_rows = attend_back(own_lens, rows, w_qkv, q, k, v, att, datt, lse, grad_pre)
-
-    grad_vec = jnp.concatenate(
-        [
-            small_a[0:CLASSES], small_c[0:2], small_b[3:4], small_b[4:6], small_b[0:1], small_b[1:3], small_a[16:17],
-        ],
-        axis=0,
-    )
-    grad_vec = grad_vec.reshape(rows_used, devices, share).transpose(1, 0, 2).reshape(devices, rows_used * share)
-    grad_vec = jnp.concatenate(
-        [
-            grad_vec,
-            grad_b_inner.reshape(devices, hidden_share),
-            jnp.broadcast_to(small_a[17:18, :CLASSES], (devices, CLASSES)),
-        ],
-        axis=1,
-    )
-    grad_vec = jnp.pad(grad_vec, ((0, 0), (0, 1024 - grad_vec.shape[1]))).reshape(devices, 8, 128)
     logit_block = jnp.pad(logits[:docs, :CLASSES], ((0, 8 - docs), (0, 128 - CLASSES)))
-    scattered = scatter_all(
-        grad_rows.reshape(seqs, local_len, width),
-        logit_block,
+    grad_inputs, all_logits, table, o_inner, o_outer, o_out, o_pool, o_query, o_key, o_value = attend_back(
+        own_lens, rows, w_qkv, q, k, v, att, datt, lse, grad_pre, small_a, small_b, grad_b_inner, logit_block,
         [
             grad_inner_w.reshape(devices, share, hidden),
             grad_outer_w.reshape(devices, hidden_share, width),
             grad_out_w.reshape(devices, share, width),
             grad_pool.reshape(devices, share, width),
-            gwq.reshape(devices, share, width),
-            gwk.reshape(devices, share, width),
-            gwv.reshape(devices, share, width),
-            grad_vec,
         ],
-        ["yx", "xy", "yx", "yx", "yx", "yx", "yx", "yx"],
-        2,
-    )
-    grad_inputs, all_logits, o_inner, o_outer, o_out, o_pool, o_query, o_key, o_value, o_vec = scattered
-    o_vec = o_vec.reshape(1024)
-
-    def vec_part(row):
-        return o_vec[row * share : (row + 1) * share]
-
-    after = rows_used * share + hidden_share
+    )
+    device = lax.axis_index("dp") * 4 + mine
+    columns = lax.dynamic_slice_in_dim(table[:12], device * share, share, 1)
+    own_b_inner = lax.dynamic_slice_in_dim(table[12:16].reshape(hidden), device * hidden_share, hidden_share, 0)
     return (
         layer_out,
         all_logits[:, :docs, :CLASSES],
         grad_inputs,
         o_query,
-        vec_part(B_QUERY),
+        columns[B_QUERY],
         o_key,
         o_value,
-        vec_part(B_VALUE),
+        columns[B_VALUE],
         o_out,
-        vec_part(B_OUT),
-        vec_part(GAIN1),
-        vec_part(SHIFT1),
+        columns[B_OUT],
+        columns[GAIN1],
+        columns[SHIFT1],
         o_inner,
-        o_vec[rows_used * share : after],
+        own_b_inner,
         o_outer,
-        vec_part(B_OUTER),
-        vec_part(GAIN2),
-        vec_part(SHIFT2),
+        columns[B_OUTER],
+        columns[GAIN2],
+        columns[SHIFT2],
         o_pool,
-        vec_part(B_POOL),
-        o_vec[: CLASSES * share].reshape(CLASSES, share).T,
-        o_vec[after : after + CLASSES],
+        columns[B_POOL],
+        columns[:CLASSES].T,
+        table[16, :CLASSES],
     )
 
 

time: 453 us -> 392 us (0.87)
  Pallas kernels: 365 us -> 324 us
  local copies, waits for them, and re-layouts: 49.6 us -> 34.4 us
  other arithmetic: 11.9 us -> 2.08 us
    pallas_call x2 -> x1, Pallas kernels: 178 us -> 135 us  [attend_back(): pl.pallas_call(functools.partial(attend_back_kernel, groups), grid=(group...]
    unnamed x103 -> x101, local copies, waits for them, and re-layouts: 20.8 us -> 14.9 us
    another operation x16, other arithmetic: 5.46 us -> 0.09 us
    reshape x4 -> x1, local copies, waits for them, and re-layouts: 5.3 us -> 0.61 us  [fast_body(): table[12:16].reshape(hidden)]
  transfers between devices with their start and end apart: 6 -> 6, of which waited for: 0 -> 0; matrix products, arithmetic and copies ran while one was open for 13% -> 11% of each run, Pallas kernels for 81% -> 83%
where the time goes in v2:
time: 392 us
  Pallas kernels  324 us (83%)
  local copies, waits for them, and re-layouts  34.4 us (9%)
  matrix products  22 us (6%)
  starting transfers between devices  8.13 us (2%)
    pallas_call x1, Pallas kernels, attend_back(): pl.pallas_call(functools.partial(attend_back_kernel, groups), grid=(group...  135 us
    pallas_call x1, Pallas kernels, gather_all(): pl.pallas_call(functools.partial(gather_kernel, orders), out_shape=[jax.S...  88.5 us
    pallas_call x1, Pallas kernels, attend(): pl.pallas_call(attend_kernel, grid=(groups,), out_shape=[jax.ShapeDtypeSt...  40.7 us
    pallas_call x1, Pallas kernels, dense(): pl.pallas_call(dense_kernel, grid=(steps,), out_shape=[jax.ShapeDtypeStru...  33.9 us
    pallas_call x1, Pallas kernels, dense_back(): pl.pallas_call(dense_back_kernel, grid=(length // tile,), out_shape=[jax....  25.2 us
    dot_general x3, matrix products, tn(): lax.dot_general(a, b, (((0,), (0,)), ((), ())), preferred_element_type=F32)  22 us
    unnamed x101, local copies, waits for them, and re-layouts  14.9 us
    ppermute x6, starting transfers between devices, exchange(): lax.ppermute(leaving, 'fsdp', [(i, (i + k) % count) for i in range(count)])  8.13 us
  transfers between devices with their start and end apart: 6, of which 0 were waited for; matrix products, arithmetic and copies ran while one was open for 11% of the time, Pallas kernels for 83%

profile of v2, /device:TPU:0, one launch (start us, length us, event | category | flops | bytes accessed | tf_op | source)
XLA Modules:
  0.0 391.6 jit_solution(7355197715854986369)
XLA Ops:
  0.7 1.2 broadcast.17.clone.1
  1.9 0.7 copy-done.9
  2.8 1.2 constant_dynamic-slice_fusion.1
  4.5 2.5 collective-permute-start.4
  7.0 1.4 collective-permute-start.5
  9.7 0.7 convert_element_type.31.refs_4_
  10.3 0.7 pad_maximum_fusion.refs_3_
  11.0 88.5 %gather_weights.1 = (bf16[4,256,768]{2,1,0:T(8,128)(2,1)}, bf16[32,24,2304]{2,1,0:T(8,128)(2,1)}, f32[32,8,128]{2,1,0:T(8,128)}, bf16[32,24,4608]{2,1,0:T(8,128)(2,1)}, bf16[32,96,768]{2,1,0:T(8,128)(2,1)}) custom-call(bf16[4,256,768]{2,1,0:T(8,128)(2,1)} %refs_0_.1, bf16[24,2304]{1,0:T(8,128)(2,1)} %copy-done.15, f32[8,128]{1,0:T(8,128)} %bitcast_convert_fusion.refs_2_, ...), custom_call_target="tpu_custom_call" | custom-call | tf_op jit(solution)/shard_map/gather_weights/pallas_call | solution.py:684
  99.5 0.9 copy.52
  100.9 0.7 reshape.96.b_inner_ref
  102.1 1.2 fusion.1
  103.3 40.7 %attend.1 = (bf16[1024,768]{1,0:T(8,128)(2,1)S(1)}, bf16[1024,768]{1,0:T(8,128)(2,1)S(1)}, bf16[1024,768]{1,0:T(8,128)(2,1)S(1)}, bf16[1024,768]{1,0:T(8,128)(2,1)}, f32[3,8,1024]{2,1,0:T(8,128)S(1)}) custom-call(s32[4]{0:T(128)S(1)} %get-tuple-element.157.lens_ref.refs_0_, bf16[1024,768]{1,0:T(8,128)(2,1)} %bitcast.62, bf16[768,2304]{1,0:T(8,128)(2,1)} %bitcast.58, ...), custom_call_target="tpu_custom_call" | custom-call | flops 10000000000 | bytes 16000000 | tf_op jit(solution)/shard_map/attend/pallas_call | solution.py:765
  144.1 1.2 copy-done
  145.3 1.2 copy-done.1
  146.4 1.2 copy-done.2
  147.6 0.6 copy-done.3
  148.2 33.9 %dense.1 = (f32[1024,768]{1,0:T(8,128)}, f32[1024,768]{1,0:T(8,128)}, bf16[1024,768]{1,0:T(8,128)(2,1)}, bf16[1024,3072]{1,0:T(8,128)(2,1)}, bf16[1024,3072]{1,0...) custom-call(s32[4]{0:T(128)} %copy-done.5, ...), custom_call_target="tpu_custom_call" | custom-call | flops 11000000512 | bytes 40000000 | tf_op jit(solution)/shard_map/dense/pallas_call | solution.py:1305
  182.2 1.3 copy-done.10
  183.5 1.1 constant_dynamic-slice_fusion.4
  185.2 2.3 collective-permute-start.1
  187.4 0.7 slice.98
  188.7 0.9 collective-permute-start.2
  189.6 0.8 constant_dynamic-update-slice_fusion.11
  190.4 0.8 constant_dynamic-update-slice_fusion.10
  191.2 0.8 constant_dynamic-update-slice_fusion.9
  191.9 25.2 %dense_back.1 = (bf16[1024,768]{1,0:T(8,128)(2,1)}, bf16[1024,3072]{1,0:T(8,128)(2,1)}, bf16[1024,768]{1,0:T(8,128)(2,1)}, bf16[1024,768]{1,0:T(8,128)(2,1)}, f3...) custom-call(s32[4]{0:T(128)} %copy-done.5, bf16[1024,768]{1,0:T(8,128)(2,1)} %bitcast.12.cot_ref, ...), custom_call_target="tpu_custom_call" | custom-call | flops 11000000512 | bytes 40000000 | tf_op jit(solution)/shard_map/dense_back/pallas_call | solution.py:1403
  217.1 9.7 %convolution_convert_fusion.1 = bf16[768,3072]{1,0:T(8,128)(2,1)} fusion(bf16[1024,768]{1,0:T(8,128)(2,1)S(1)} %copy-done.39, bf16[1024,3072]{1,0:T(8,128)(2,1)} %get-tuple-element.81), kind=kOutput, calls=%fused_computation.1 | convolution fusion | flops 4834197504 | bytes 12582912 | tf_op jit(solution)/shard_map/dot_general | solution.py:527
  226.8 9.9 %convolution_convert_fusion = bf16[3072,768]{1,0:T(8,128)(2,1)} fusion(bf16[1024,3072]{1,0:T(8,128)(2,1)} %get-tuple-element.82, bf16[1024,768]{1,0:T(8,128)(2,1)S(1)} %copy-done.40), kind=kOutput, calls=%fused_computation | convolution fusion | flops 4834197504 | bytes 12582912 | tf_op jit(solution)/shard_map/dot_general | solution.py:527
  236.7 2.5 convolution_convert_fusion.2
  239.1 135.4 %attend_back.1 = (bf16[4,256,768]{2,1,0:T(8,128)(2,1)}, f32[4,8,128]{2,1,0:T(8,128)}, f32[24,768]{1,0:T(8,128)}, f32[24,3072]{1,0:T(8,128)}, f32[96,768]{1,0:T(8...) custom-call(s32[4]{0:T(128)} %copy-done.5, ...), custom_call_target="tpu_custom_call" | custom-call | tf_op jit(solution)/shard_map/attend_back/pallas_call | solution.py:1152
  374.5 0.9 slice.100
  375.4 0.6 dynamic-slice_bitcast_fusion
  376.1 1.0 constant_dynamic-update-slice_fusion.14
  377.1 0.7 fusion
  377.7 0.7 slice.106
  378.5 1.3 slice.99
  379.8 1.4 copy.48
  381.8 1.3 dynamic_slice.49
  383.1 1.2 slice_bitcast_fusion
  384.3 1.0 constant_dynamic-update-slice_fusion.12
  385.4 1.1 copy.77
  387.0 0.6 copy.78
  387.6 0.6 copy.79
  388.3 0.6 copy.80
  388.9 0.6 copy.81
  389.5 0.7 copy.82
  390.3 0.7 copy.83
  391.0 0.6 copy.84
  (124 shorter events, 4.9 us)
Async XLA Ops:
  0.7 2.0 copy-start.9
  2.6 5.8 %copy-start.16 = (f32[24,768]{1,0:T(8,128)S(1)}, f32[24,768]{1,0:T(8,128)}, u32[]{:S(2)}) copy-start(f32[24,768]{1,0:T(8,128)} %param.27) | copy-start | bytes 221188
  2.6 5.8 %copy-start.17 = (f32[24,768]{1,0:T(8,128)S(1)}, f32[24,768]{1,0:T(8,128)}, u32[]{:S(2)}) copy-start(f32[24,768]{1,0:T(8,128)} %param.29) | copy-start | bytes 221188
  2.6 5.8 %copy-start.18 = (f32[24,768]{1,0:T(8,128)S(1)}, f32[24,768]{1,0:T(8,128)}, u32[]{:S(2)}) copy-start(f32[24,768]{1,0:T(8,128)} %param.30) | copy-start | bytes 221188
  2.6 5.9 %copy-start.26 = (f32[24,3]{0,1:T(4,128)S(1)}, f32[24,3]{0,1:T(4,128)}, u32[]{:S(2)}) copy-start(f32[24,3]{0,1:T(4,128)} %param.44) | copy-start | bytes 868
  2.6 6.0 %copy-start.27 = (f32[24]{0:T(128)S(1)}, f32[24]{0:T(128)}, u32[]{:S(2)}) copy-start(f32[24]{0:T(128)} %param.28) | copy-start | bytes 292
  2.7 6.0 %copy-start.28 = (f32[24]{0:T(128)S(1)}, f32[24]{0:T(128)}, u32[]{:S(2)}) copy-start(f32[24]{0:T(128)} %param.31) | copy-start | bytes 292
  2.7 6.0 %copy-start.29 = (f32[24]{0:T(128)S(1)}, f32[24]{0:T(128)}, u32[]{:S(2)}) copy-start(f32[24]{0:T(128)} %param.33) | copy-start | bytes 292
  2.7 6.0 %copy-start.30 = (f32[24]{0:T(128)S(1)}, f32[24]{0:T(128)}, u32[]{:S(2)}) copy-start(f32[24]{0:T(128)} %param.34) | copy-start | bytes 292
  2.7 6.1 %copy-start.31 = (f32[24]{0:T(128)S(1)}, f32[24]{0:T(128)}, u32[]{:S(2)}) copy-start(f32[24]{0:T(128)} %param.35) | copy-start | bytes 292
  2.7 6.1 %copy-start.32 = (f32[24]{0:T(128)S(1)}, f32[24]{0:T(128)}, u32[]{:S(2)}) copy-start(f32[24]{0:T(128)} %param.39) | copy-start | bytes 292
  2.7 6.1 %copy-start.33 = (f32[24]{0:T(128)S(1)}, f32[24]{0:T(128)}, u32[]{:S(2)}) copy-start(f32[24]{0:T(128)} %param.40) | copy-start | bytes 292
  2.7 6.1 %copy-start.34 = (f32[24]{0:T(128)S(1)}, f32[24]{0:T(128)}, u32[]{:S(2)}) copy-start(f32[24]{0:T(128)} %param.41) | copy-start | bytes 292
  2.7 6.1 %copy-start.35 = (f32[24]{0:T(128)S(1)}, f32[24]{0:T(128)}, u32[]{:S(2)}) copy-start(f32[24]{0:T(128)} %param.43) | copy-start | bytes 292
  2.8 6.1 %copy-start.36 = (f32[96]{0:T(128)S(1)}, f32[96]{0:T(128)}, u32[]{:S(2)}) copy-start(f32[96]{0:T(128)} %param.37) | copy-start | bytes 1156
  2.8 6.8 %copy-start.19 = (f32[24,768]{1,0:T(8,128)S(1)}, f32[24,768]{1,0:T(8,128)}, u32[]{:S(2)}) copy-start(f32[24,768]{1,0:T(8,128)} %param.42) | copy-start | bytes 221188
  2.8 6.8 %copy-start.20 = (f32[24,768]{1,0:T(8,128)S(1)}, f32[24,768]{1,0:T(8,128)}, u32[]{:S(2)}) copy-start(f32[24,768]{1,0:T(8,128)} %param.32) | copy-start | bytes 221188
  2.8 6.8 %copy-start.11 = (f32[24,3072]{1,0:T(8,128)S(1)}, f32[24,3072]{1,0:T(8,128)}, u32[]{:S(2)}) copy-start(f32[24,3072]{1,0:T(8,128)} %param.36) | copy-start | bytes 884740
  2.8 6.9 %copy-start.12 = (f32[96,768]{1,0:T(8,128)S(1)}, f32[96,768]{1,0:T(8,128)}, u32[]{:S(2)}) copy-start(f32[96,768]{1,0:T(8,128)} %param.38) | copy-start | bytes 884740
  4.0 184.7 %collective-permute-start.3 = (bf16[1,256,768]{2,1,0:T(8,128)(2,1)}, bf16[1,256,768]{2,1,0:T(8,128)(2,1)S(1)}, u32[]{:S(2)}, u32[]{:S(2)}) collective-permute-start(bf16[1,256,768]{2,1,0:T(8,128)(2,1)} %get-tuple-element.141), channel_id=1, source_target_pairs={{0,1},{1,2},{2,3},{3,0},{4,5},{5,6},{6,7},{7,4},{8,9},{9,10},{10,1... | collective-permute-start | bytes 1179656 | tf_op jit(solution)/shard_map/ppermute | solution.py:1435
  4.5 185.9 %collective-permute-start.4 = (bf16[1,256,768]{2,1,0:T(8,128)(2,1)}, bf16[1,256,768]{2,1,0:T(8,128)(2,1)S(1)}, u32[]{:S(2)}, u32[]{:S(2)}) collective-permute-start(bf16[1,256,768]{2,1,0:T(8,128)(2,1)} %get-tuple-element.143), channel_id=1, source_target_pairs={{0,2},{1,3},{2,0},{3,1},{4,6},{5,7},{6,4},{7,5},{8,10},{9,11},{10,... | collective-permute-start | bytes 1179656 | tf_op jit(solution)/shard_map/ppermute | solution.py:1435
  7.0 184.2 %collective-permute-start.5 = (bf16[1,256,768]{2,1,0:T(8,128)(2,1)}, bf16[1,256,768]{2,1,0:T(8,128)(2,1)S(1)}, u32[]{:S(2)}, u32[]{:S(2)}) collective-permute-start(bf16[1,256,768]{2,1,0:T(8,128)(2,1)} %get-tuple-element.140), channel_id=1, source_target_pairs={{0,3},{1,0},{2,1},{3,2},{4,7},{5,4},{6,5},{7,6},{8,11},{9,8},{10,9... | collective-permute-start | bytes 1179656 | tf_op jit(solution)/shard_map/ppermute | solution.py:1435
  8.6 2.5 copy-start.15
  11.0 90.5 %copy-start.37 = (f32[3]{0:T(128)S(1)}, f32[3]{0:T(128)}, u32[]{:S(2)}) copy-start(f32[3]{0:T(128)} %param.45) | copy-start | bytes 40
  103.3 40.8 %copy-start.5 = (s32[4]{0:T(128)}, s32[4]{0:T(128)S(1)}, u32[]{:S(2)}) copy-start(s32[4]{0:T(128)S(1)} %get-tuple-element.157.lens_ref.refs_0_) | copy-start | bytes 52
  103.3 40.8 %copy-start.4 = (f32[16,768]{1,0:T(8,128)}, f32[16,768]{1,0:T(8,128)S(1)}, u32[]{:S(2)}) copy-start(f32[16,768]{1,0:T(8,128)S(1)} %pad.18.vec_ref) | copy-start | bytes 147460
  144.1 1.2 copy-start
  145.3 1.2 copy-start.1
  146.4 1.2 copy-start.2
  147.6 0.6 copy-start.3
  182.1 1.4 copy-start.10
  184.6 191.5 %collective-permute-start = (bf16[1,256,768]{2,1,0:T(8,128)(2,1)}, bf16[1,256,768]{2,1,0:T(8,128)(2,1)}, u32[]{:S(2)}, u32[]{:S(2)}) collective-permute-start(bf16[1,256,768]{2,1,0:T(8,128)(2,1)} %get-tuple-element.146), channel_id=1, source_target_pairs={{0,1},{1,2},{2,3},{3,0},{4,5},{5,6},{6,7},{7,4},{8,9},{9,10},{10,1... | collective-permute-start | bytes 1179656 | tf_op jit(solution)/shard_map/ppermute | solution.py:1435
  185.2 197.9 %collective-permute-start.1 = (bf16[1,256,768]{2,1,0:T(8,128)(2,1)}, bf16[1,256,768]{2,1,0:T(8,128)(2,1)S(1)}, u32[]{:S(2)}, u32[]{:S(2)}) collective-permute-start(bf16[1,256,768]{2,1,0:T(8,128)(2,1)} %get-tuple-element.145), channel_id=1, source_target_pairs={{0,2},{1,3},{2,0},{3,1},{4,6},{5,7},{6,4},{7,5},{8,10},{9,11},{10,... | collective-permute-start | bytes 1179656 | tf_op jit(solution)/shard_map/ppermute | solution.py:1435
  188.7 195.6 %collective-permute-start.2 = (bf16[1,256,768]{2,1,0:T(8,128)(2,1)}, bf16[1,256,768]{2,1,0:T(8,128)(2,1)}, u32[]{:S(2)}, u32[]{:S(2)}) collective-permute-start(bf16[1,256,768]{2,1,0:T(8,128)(2,1)} %get-tuple-element.144), channel_id=1, source_target_pairs={{0,3},{1,0},{2,1},{3,2},{4,7},{5,4},{6,5},{7,6},{8,11},{9,8},{10,9... | collective-permute-start | bytes 1179656 | tf_op jit(solution)/shard_map/ppermute | solution.py:1435
  191.9 25.2 %copy-start.39 = (bf16[1024,768]{1,0:T(8,128)(2,1)S(1)}, bf16[1024,768]{1,0:T(8,128)(2,1)}, u32[]{:S(2)}) copy-start(bf16[1024,768]{1,0:T(8,128)(2,1)} %get-tuple-element.80) | copy-start | bytes 4718596
  217.1 9.7 %copy-start.40 = (bf16[1024,768]{1,0:T(8,128)(2,1)S(1)}, bf16[1024,768]{1,0:T(8,128)(2,1)}, u32[]{:S(2)}) copy-start(bf16[1024,768]{1,0:T(8,128)(2,1)} %get-tuple-element.83) | copy-start | bytes 4718596
  226.8 9.9 %copy-start.6 = (bf16[1024,768]{1,0:T(8,128)(2,1)S(1)}, bf16[1024,768]{1,0:T(8,128)(2,1)}, u32[]{:S(2)}) copy-start(bf16[1024,768]{1,0:T(8,128)(2,1)} %get-tuple-element.62.att_ref.refs_6_) | copy-start | bytes 4718596
  226.8 9.9 %copy-start.38 = (bf16[1024,768]{1,0:T(8,128)(2,1)S(1)}, bf16[1024,768]{1,0:T(8,128)(2,1)}, u32[]{:S(2)}) copy-start(bf16[1024,768]{1,0:T(8,128)(2,1)} %get-tuple-element.84) | copy-start | bytes 4718596
  374.5 10.8 %copy-start.7 = (bf16[4,256,768]{2,1,0:T(8,128)(2,1)S(1)}, bf16[4,256,768]{2,1,0:T(8,128)(2,1)}, u32[]{:S(2)}) copy-start(bf16[4,256,768]{2,1,0:T(8,128)(2,1)} %get-tuple-element.183) | copy-start | bytes 4718596
  385.3 1.7 copy-start.8
  385.4 1.6 copy-start.25
  385.4 2.3 copy-start.24
  385.4 2.9 copy-start.23
  385.4 3.5 copy-start.22
  385.4 4.1 %copy-start.14 = (f32[24,3072]{1,0:T(8,128)S(1)}, f32[24,3072]{1,0:T(8,128)}, u32[]{:S(2)}) copy-start(f32[24,3072]{1,0:T(8,128)} %get-tuple-element.193) | copy-start | bytes 884740
  385.4 4.9 %copy-start.13 = (f32[96,768]{1,0:T(8,128)S(1)}, f32[96,768]{1,0:T(8,128)}, u32[]{:S(2)}) copy-start(f32[96,768]{1,0:T(8,128)} %get-tuple-element.195) | copy-start | bytes 884740
  387.0 4.0 %copy-start.21 = (f32[24,768]{1,0:T(8,128)S(1)}, f32[24,768]{1,0:T(8,128)}, u32[]{:S(2)}) copy-start(f32[24,768]{1,0:T(8,128)} %get-tuple-element.199) | copy-start | bytes 221188

commit v3 on v2

--- a/solution.py
+++ b/solution.py
@@ -556,149 +556,6 @@
     return (1 - x if k >= 2 else x, 1 - c if k % 2 == 1 else c)
 
 
-def gather_kernel(orders, *refs):
-    count = len(orders)
-    rows_ref, shards = refs[0], refs[1 : 1 + count]
-    seq_ref, wholes = refs[1 + count], refs[2 + count : 2 + 2 * count]
-    local_sem, row_send, row_recv, send_sem, recv_sem = refs[2 + 2 * count :]
-    z, y, x, c = my_place()
-    meet(all_partners(z, y, x, c))
-    mine = x * 2 + c
-    sent = []
-    got_rows = []
-    for k in range(1, 4):
-        px, pc = group_partner(k, x, c)
-        copy = pltpu.make_async_remote_copy(
-            src_ref=rows_ref.at[px * 2 + pc],
-            dst_ref=seq_ref.at[mine],
-            send_sem=row_send.at[k - 1],
-            recv_sem=row_recv.at[k - 1],
-            device_id=device_at(z, y, px, pc),
-            device_id_type=MESH,
-        )
-        copy.start()
-        sent.append(copy)
-        got_rows.append(copy)
-    own = pltpu.make_async_copy(rows_ref.at[mine], seq_ref.at[mine], local_sem.at[count])
-    own.start()
-    local = [own]
-
-    def place(rel):
-        dz, fy, fx, fc = rel
-        zz = lax.rem(z + dz, ZS)
-        yy = 1 - y if fy else y
-        xx = 1 - x if fx else x
-        cc = 1 - c if fc else c
-        return ((zz * 2 + yy) * 2 + xx) * 2 + cc
-
-    def slot(rel):
-        dz, fy, fx, fc = rel
-        return ((dz * 2 + fy) * 2 + fx) * 2 + fc
-
-    def send(a, rel, there, device, number):
-        source = shards[a] if slot(rel) == 0 else wholes[a].at[place(rel)]
-        copy = pltpu.make_async_remote_copy(
-            src_ref=source,
-            dst_ref=wholes[a].at[place(rel)],
-            send_sem=send_sem.at[a, number],
-            recv_sem=recv_sem.at[a, slot(there)],
-            device_id=device,
-            device_id_type=MESH,
-        )
-        copy.start()
-        sent.append(copy)
-
-    def arrive(a, rel):
-        block = wholes[a].at[place(rel)]
-        pltpu.make_async_remote_copy(
-            src_ref=block,
-            dst_ref=block,
-            send_sem=send_sem.at[a, 0],
-            recv_sem=recv_sem.at[a, slot(rel)],
-            device_id=device_at(z, y, x, 1 - c),
-            device_id_type=MESH,
-        ).wait_recv()
-
-    numbers = [0] * count
-
-    def forward_to(a, rel, axis):
-        numbers[a] += 1
-        dz, fy, fx, fc = rel
-        if axis == "y":
-            send(a, rel, (dz, 1 - fy, fx, fc), device_at(z, 1 - y, x, c), numbers[a] - 1)
-        elif axis == "x":
-            send(a, rel, (dz, fy, 1 - fx, fc), device_at(z, y, 1 - x, c), numbers[a] - 1)
-        else:
-            send(a, rel, (dz, fy, fx, 1 - fc), device_at(z, y, x, 1 - c), numbers[a] - 1)
-
-    for a in range(count):
-        keep = pltpu.make_async_copy(
-            shards[a], wholes[a].at[place((0, 0, 0, 0))], local_sem.at[a]
-        )
-        keep.start()
-        local.append(keep)
-        for k in (2, 1, 3):
-            numbers[a] += 1
-            send(
-                a, (0, 0, 0, 0), ((ZS - k) % ZS, 0, 0, 0),
-                device_at(lax.rem(z + k, ZS), y, x, c), numbers[a] - 1,
-            )
-        for axis in (*orders[a], "c"):
-            forward_to(a, (0, 0, 0, 0), axis)
-    for a in range(count):
-        for dz in (1, 3, 2):
-            arrive(a, (dz, 0, 0, 0))
-            for axis in (*orders[a], "c"):
-                forward_to(a, (dz, 0, 0, 0), axis)
-    for a in range(count):
-        first, second = orders[a]
-        for dz in (0, 1, 3, 2):
-            rel = (dz, int(first == "y"), int(first == "x"), 0)
-            arrive(a, rel)
-            forward_to(a, rel, second)
-            forward_to(a, rel, "c")
-    for a in range(count):
-        first, second = orders[a]
-        for dz in (0, 1, 3, 2):
-            for turn in (0, 1):
-                fy = 1 if second == "y" else turn
-                fx = 1 if second == "x" else turn
-                arrive(a, (dz, fy, fx, 0))
-                forward_to(a, (dz, fy, fx, 0), "c")
-    for a in range(count):
-        for dz in range(ZS):
-            for fy in (0, 1):
-                for fx in (0, 1):
-                    arrive(a, (dz, fy, fx, 1))
-    for copy in got_rows:
-        copy.wait_recv()
-    for copy in sent:
-        copy.wait_send()
-    for copy in local:
-        copy.wait()
-
-
-def gather_all(rows, shards, orders, collective_id):
-    count = len(shards)
-    whole = 8 * ZS
-    return pl.pallas_call(
-        functools.partial(gather_kernel, orders),
-        out_shape=[jax.ShapeDtypeStruct(rows.shape, rows.dtype)]
-        + [jax.ShapeDtypeStruct((whole,) + s.shape, s.dtype) for s in shards],
-        in_specs=[ANY] * (1 + count),
-        out_specs=[ANY] * (1 + count),
-        scratch_shapes=[
-            pltpu.SemaphoreType.DMA((count + 1,)),
-            pltpu.SemaphoreType.DMA((3,)),
-            pltpu.SemaphoreType.DMA((3,)),
-            pltpu.SemaphoreType.DMA((count, whole)),
-            pltpu.SemaphoreType.DMA((count, whole)),
-        ],
-        compiler_params=pltpu.CompilerParams(collective_id=collective_id, has_side_effects=True),
-        name="gather_weights",
-    )(rows, *shards)
-
-
 def doc_ends(lens_ref):
     ends = []
     total = 0
@@ -715,17 +572,201 @@
     return number
 
 
-def attend_kernel(
-    lens_ref, x_ref, wq_ref, wk_ref, wv_ref, vec_ref, q_ref, k_ref, v_ref, att_ref, lse_ref, vt_ref
-):
-    x = x_ref[...]
+GATHER_PIECES = (
+    (1, 0, 1, "rows"), (0, 0, 2, "columns"), (0, 1, 2, "columns"), (3, 0, 2, "rows"), (3, 1, 2, "rows"), (2, 0, 1, "rows"),
+)
+GATHER_ORDERS = ("xy", "xy", "xy", "xy", "yx", "xy", "yx", "yx", "xy")
+GATHER_PLAN = {
+    -1: "b0 b1 b2 z0 b3 z1 b4 z2 z3 b5 f0 z4 b6 f1 s0 f2 e0",
+    0: "s1 s2 f3 f4 z5 b7",
+    1: "z6 e1 e2",
+    2: "b8",
+    3: "s3 z7",
+    4: "z8 e3",
+    6: "s4 f5 f6",
+    8: "f7 s5 f8 e4",
+    9: "e5",
+    10: "s6 s8",
+    11: "s7 e8 e6",
+    12: "e7",
+}
+DENSE_ARRAYS = 4
+
+
+def part_of(piece, block):
+    _, which, count, along = piece
+    rows, columns = block
+    if along == "rows":
+        return (which * (rows // count), rows // count), (0, columns)
+    return (0, rows), (which * (columns // count), columns // count)
+
+
+def attend_kernel(groups, *refs):
+    lens_ref, tokens_ref, table_ref, wq_ref, wk_ref, wv_ref = refs[:6]
+    shards = refs[6 : 6 + DENSE_ARRAYS]
+    refs = refs[6 + DENSE_ARRAYS :]
+    q_ref, k_ref, v_ref, att_ref, lse_ref, w_ref, vec_ref, rows_ref = refs[:8]
+    wholes = refs[8 : 8 + DENSE_ARRAYS]
+    refs = refs[8 + DENSE_ARRAYS :]
+    x_ref, vt_ref, qkv_shard, qkv_ref, tab_ref, tab_in_ref = refs[:6]
+    local_sem, row_send, row_recv, tab_send, tab_recv, send_sem, recv_sem = refs[6:13]
+    own = refs[13 : 13 + DENSE_ARRAYS]
     length, width = q_ref.shape
     chunk = 256
+    points = length // chunk
     heads = width // HEAD_DIM
-    queries = (nn(x, wq_ref[...]) + vec_ref[B_QUERY : B_QUERY + 1, :]).astype(BF)
-    q_ref[...] = queries
-    k_ref[...] = nn(x, wk_ref[...]).astype(BF)
-    values = (nn(x, wv_ref[...]) + vec_ref[B_VALUE : B_VALUE + 1, :]).astype(BF)
+    items = groups + len(GATHER_PIECES)
+    group = pl.program_id(0)
+    z, y, x, c = my_place()
+    mine = x * 2 + c
+
+    def row_copy(k):
+        px, pc = group_partner(k, x, c)
+        return pltpu.make_async_remote_copy(
+            src_ref=tokens_ref.at[px * 2 + pc],
+            dst_ref=x_ref.at[mine],
+            send_sem=row_send.at[k - 1],
+            recv_sem=row_recv.at[k - 1],
+            device_id=device_at(z, y, px, pc),
+            device_id_type=MESH,
+        )
+
+    def row_own():
+        return pltpu.make_async_copy(tokens_ref.at[mine], x_ref.at[mine], local_sem.at[0])
+
+    def rows_out():
+        return pltpu.make_async_copy(x_ref, rows_ref, local_sem.at[1])
+
+    def table_copy(level):
+        if level < 3:
+            source, device = tab_ref.at[0], device_at(lax.rem(z + level + 1, ZS), y, x, c)
+        else:
+            source = tab_ref.at[level - 2]
+            device = (device_at(z, y, 1 - x, c), device_at(z, 1 - y, x, c), device_at(z, y, x, 1 - c))[level - 3]
+        return pltpu.make_async_remote_copy(
+            src_ref=source,
+            dst_ref=tab_in_ref.at[level],
+            send_sem=tab_send.at[level],
+            recv_sem=tab_recv.at[level],
+            device_id=device,
+            device_id_type=MESH,
+        )
+
+    def array_of(a):
+        if a < groups:
+            return qkv_ref.at[a], qkv_shard.at[a], None
+        piece = GATHER_PIECES[a - groups]
+        return wholes[piece[0]], own[piece[0]], part_of(piece, own[piece[0]].shape)
+
+    def view(a, where):
+        ref, _, part = array_of(a)
+        if part is None:
+            return ref.at[where]
+        (r0, rows), (c0, columns) = part
+        return ref.at[where + (pl.ds(r0, rows), pl.ds(c0, columns))]
+
+    def own_block(a):
+        _, ref, part = array_of(a)
+        if part is None:
+            return ref
+        (r0, rows), (c0, columns) = part
+        return ref.at[pl.ds(r0, rows), pl.ds(c0, columns)]
+
+    everything = slice(None)
+
+    def along(a, axis):
+        return device_at(z, 1 - y, x, c) if GATHER_ORDERS[a][axis] == "y" else device_at(z, y, 1 - x, c)
+
+    def copy_of(a, number):
+        core = device_at(z, y, x, 1 - c)
+        first_other = (1 - y, x) if GATHER_ORDERS[a][0] == "y" else (y, 1 - x)
+        if number < 3:
+            source, target = own_block(a), view(a, (z, y, x, c))
+            device = device_at(lax.rem(z + number + 1, ZS), y, x, c)
+        elif number < 6:
+            source = target = view(a, (everything, y, x, c))
+            device = (along(a, 0), along(a, 1), core)[number - 3]
+        elif number < 8:
+            source = target = view(a, (everything, first_other[0], first_other[1], c))
+            device = along(a, 1) if number == 6 else core
+        else:
+            if GATHER_ORDERS[a][1] == "y":
+                source = target = view(a, (everything, 1 - y, everything, c))
+            else:
+                source = target = view(a, (everything, everything, 1 - x, c))
+            device = core
+        return pltpu.make_async_remote_copy(
+            src_ref=source,
+            dst_ref=target,
+            send_sem=send_sem.at[a, number],
+            recv_sem=recv_sem.at[a, number],
+            device_id=device,
+            device_id_type=MESH,
+        )
+
+    def keep(a):
+        return pltpu.make_async_copy(own_block(a), view(a, (z, y, x, c)), local_sem.at[2 + a])
+
+    def take_up(point):
+        for word in GATHER_PLAN.get(point, "").split():
+            kind, a = word[0], int(word[1:])
+            if kind == "b":
+                for number in (1, 0, 2):
+                    copy_of(a, number).start()
+                keep(a).start()
+            elif kind == "z":
+                for number in (0, 1, 2):
+                    copy_of(a, number).wait_recv()
+                keep(a).wait()
+                for number in (3, 4, 5):
+                    copy_of(a, number).start()
+            elif kind == "f":
+                copy_of(a, 3).wait_recv()
+                for number in (6, 7):
+                    copy_of(a, number).start()
+            elif kind == "s":
+                copy_of(a, 4).wait_recv()
+                copy_of(a, 6).wait_recv()
+                copy_of(a, 8).start()
+            else:
+                for number in (5, 7, 8):
+                    copy_of(a, number).wait_recv()
+
+    @pl.when(group == 0)
+    def _():
+        tab_ref[0] = table_ref[...]
+        for g in range(groups):
+            for j, ref in enumerate((wq_ref, wk_ref, wv_ref)):
+                qkv_shard[g, :, j * width : (j + 1) * width] = ref[:, g * width : (g + 1) * width].astype(BF)
+        for target, ref in zip(own, shards):
+            target[...] = ref[...].astype(BF)
+        meet(all_partners(z, y, x, c))
+        for level in (1, 0, 2):
+            table_copy(level).start()
+        for k in (3, 2, 1):
+            row_copy(k).start()
+        row_own().start()
+        take_up(-1)
+        for level in (0, 1, 2):
+            table_copy(level).wait_recv()
+        tab_ref[1] = (tab_ref[0] + tab_in_ref[0]) + (tab_in_ref[1] + tab_in_ref[2])
+        for level in (3, 4, 5):
+            table_copy(level).start()
+            table_copy(level).wait_recv()
+            tab_ref[level - 1] = tab_ref[level - 2] + tab_in_ref[level]
+        vec_ref[...] = tab_ref[4]
+        row_own().wait()
+        for k in (1, 2, 3):
+            row_copy(k).wait_recv()
+        rows_out().start()
+
+    tokens = x_ref[...].reshape(length, x_ref.shape[2])
+    weights = qkv_ref[group].astype(F32).reshape(x_ref.shape[2], 3 * width).astype(BF)
+    w_ref[...] = weights
+    bias = tab_ref[4, B_QUERY : B_QUERY + 2, pl.ds(pl.multiple_of(group * width, width), width)]
+    q_ref[...] = (nn(tokens, weights[:, :width]) + bias[0:1]).astype(BF)
+    k_ref[...] = nn(tokens, weights[:, width : 2 * width]).astype(BF)
+    values = (nn(tokens, weights[:, 2 * width :]) + bias[1:2]).astype(BF)
     v_ref[...] = values
     vt_ref[...] = values.astype(F32).T.astype(BF)
     ends = doc_ends(lens_ref)
@@ -733,15 +774,22 @@
     lane_head = lax.broadcasted_iota(jnp.int32, (1, width), 1) // HEAD_DIM
 
     def step(i, carry):
+        for point in range(groups * points):
+            if point in GATHER_PLAN:
+
+                @pl.when((group == point // points) & (i == point % points))
+                def _(point=point):
+                    take_up(point)
+
         at = pl.multiple_of(i * chunk, chunk)
         query_doc = doc_numbers(lax.broadcasted_iota(jnp.int32, (1, chunk), 1) + at, ends)
         scaled = q_ref[pl.ds(at, chunk), :] * jnp.asarray(0.125, BF)
         mixed = []
         for h in range(heads):
-            own = jnp.where(lane_head == h, scaled, jnp.zeros_like(scaled))
+            own_q = jnp.where(lane_head == h, scaled, jnp.zeros_like(scaled))
             blocks = []
             for s in range(0, length, chunk):
-                scores = nt(k_ref[s : s + chunk, :], own)
+                scores = nt(k_ref[s : s + chunk, :], own_q)
                 blocks.append(jnp.where(key_doc[s : s + chunk] == query_doc, scores, -1000000000.0))
             peak = functools.reduce(jnp.maximum, [jnp.max(b, axis=0, keepdims=True) for b in blocks])
             exps = [jnp.exp(b - peak) for b in blocks]
@@ -753,43 +801,123 @@
         att_ref[pl.ds(at, chunk), :] = jnp.concatenate(mixed, axis=0).T.astype(BF)
         return carry
 
-    lax.fori_loop(0, length // chunk, step, 0)
-
-
-def attend(lens, rows, w_qkv, vectors):
-    length, width = rows.shape
+    lax.fori_loop(0, points, step, 0)
+
+    @pl.when(group == groups - 1)
+    def _():
+        take_up(groups * points)
+        for a in range(items):
+            for number in range(9):
+                copy_of(a, number).wait_send()
+        for level in range(6):
+            table_copy(level).wait_send()
+        for k in range(1, 4):
+            row_copy(k).wait_send()
+        rows_out().wait()
+
+
+def attend(lens, tokens, table, qkv_shards, shards):
+    seqs, local_len, width = tokens.shape
+    length = seqs * local_len
     group = 256
     groups = width // group
-    whole = pl.BlockSpec((length, width), lambda g: (0, 0))
+    share = qkv_shards[0].shape[0]
+    hbm = pl.BlockSpec(memory_space=pl.ANY)
     part = pl.BlockSpec((length, group), lambda g: (0, g))
+    once = pl.Buffered(buffer_count=1)
+    items = groups + len(GATHER_PIECES)
+
+    def fixed(shape):
+        return pl.BlockSpec(shape, lambda g: (0,) * len(shape), pipeline_mode=once)
+
+    lead = (ZS, 2, 2, 2)
     return pl.pallas_call(
-        attend_kernel,
+        functools.partial(attend_kernel, groups),
         grid=(groups,),
         out_shape=[jax.ShapeDtypeStruct((length, width), BF)] * 4
-        + [jax.ShapeDtypeStruct((groups, 8, length), F32)],
-        in_specs=[
-            SMEM,
-            whole,
-            pl.BlockSpec((width, group), lambda g: (0, 3 * g)),
-            pl.BlockSpec((width, group), lambda g: (0, 3 * g + 1)),
-            pl.BlockSpec((width, group), lambda g: (0, 3 * g + 2)),
-            pl.BlockSpec((VEC_ROWS, group), lambda g: (0, g)),
-        ],
-        out_specs=[part] * 4 + [pl.BlockSpec((1, 8, length), lambda g: (g, 0, 0))],
-        scratch_shapes=[pltpu.VMEM((group, length), BF)],
-        compiler_params=pltpu.CompilerParams(vmem_limit_bytes=48 * 2**20),
-        cost_estimate=pl.CostEstimate(flops=10 * 10**9, bytes_accessed=16 * 10**6, transcendentals=12 * 2**20),
+        + [
+            jax.ShapeDtypeStruct((groups, 8, length), F32),
+            jax.ShapeDtypeStruct((width, 3 * width), BF),
+            jax.ShapeDtypeStruct((VEC_ROWS, width), F32),
+            jax.ShapeDtypeStruct(tokens.shape, BF),
+        ]
+        + [jax.ShapeDtypeStruct(lead + s.shape, BF) for s in shards],
+        in_specs=[SMEM, hbm, fixed(table.shape)]
+        + [fixed(s.shape) for s in qkv_shards]
+        + [fixed(s.shape) for s in shards],
+        out_specs=[part] * 4
+        + [
+            pl.BlockSpec((1, 8, length), lambda g: (g, 0, 0)),
+            pl.BlockSpec((width, 3 * group), lambda g: (0, g)),
+            pl.BlockSpec((VEC_ROWS, width), lambda g: (0, 0)),
+            hbm,
+        ]
+        + [hbm] * DENSE_ARRAYS,
+        scratch_shapes=[
+            pltpu.VMEM(tokens.shape, BF),
+            pltpu.VMEM((group, length), BF),
+            pltpu.VMEM((groups, share, 3 * group), BF),
+            pltpu.VMEM((groups,) + lead + (share, 3 * group), BF),
+            pltpu.VMEM((5, VEC_ROWS, width), F32),
+            pltpu.VMEM((6, VEC_ROWS, width), F32),
+            pltpu.SemaphoreType.DMA((2 + items,)),
+            pltpu.SemaphoreType.DMA((3,)),
+            pltpu.SemaphoreType.DMA((3,)),
+            pltpu.SemaphoreType.DMA((6,)),
+            pltpu.SemaphoreType.DMA((6,)),
+            pltpu.SemaphoreType.DMA((items, 9)),
+            pltpu.SemaphoreType.DMA((items, 9)),
+        ]
+        + [pltpu.VMEM(s.shape, BF) for s in shards],
+        compiler_params=pltpu.CompilerParams(
+            collective_id=1, has_side_effects=True, vmem_limit_bytes=48 * 2**20
+        ),
         name="attend",
-    )(lens, rows, w_qkv, w_qkv, w_qkv, vectors)
+    )(lens, tokens, table, *qkv_shards, *shards)
 
 
 DENSE = 4
-SCATTER_ORDERS = ("yx", "xy", "yx", "yx", "yx", "yx", "yx")
+DENSE_ITEMS = (
+    (2, 0, 1, "rows", "yx"), (3, 0, 1, "rows", "xy"),
+    (0, 0, 2, "columns", "yx"), (1, 0, 2, "rows", "xy"), (0, 1, 2, "columns", "yx"), (1, 1, 2, "rows", "xy"),
+)
+GROUP_ORDERS = ("yx", "xy", "yx")
+SCATTER_PLAN = {
+    -1: "b0",
+    0: "b1",
+    1: "c00 c01 b2 c10 c11",
+    2: "b3",
+    3: "c02 b4 c12 f0 f1 c03 c13 b5",
+    4: "s0 s1 b6",
+    5: "c04 c05 c14 c15",
+    6: "z0 z1",
+    7: "f2 f3",
+    8: "b7",
+    9: "c06 c07 c16 c17",
+    10: "f4 s2 s3",
+    11: "f5",
+    12: "b8 dx f6 f7 t0 s4 s5 z2 c08 c18 z3 t1 s7 s6 f8 t2 z7 s8 z4 z6 z5 t3 z8",
+}
+PIECES = len(DENSE_ITEMS)
+
+
+def order_of(a):
+    return DENSE_ITEMS[a][4] if a < PIECES else GROUP_ORDERS[a - PIECES]
+
+
+def cut_of(a, block):
+    _, which, count, along, _ = DENSE_ITEMS[a]
+    rows, columns = block
+    if along == "rows":
+        return (which * (rows // count), rows // count), (0, columns)
+    return (0, rows), (which * (columns // count), columns // count)
+
+
 TABLE_ROWS = 24
 
 
 def attend_back_kernel(groups, *refs):
-    items = DENSE + groups
+    items = PIECES + groups
     lens_ref, x_ref, w_ref, q_ref, k_ref, v_ref, att_ref, datt_ref, lse_ref, start_ref = refs[:10]
     small_a_ref, small_b_ref, bi_ref, logit_ref = refs[10:14]
     parts = refs[14 : 14 + DENSE]
@@ -799,7 +927,7 @@
     xt_ref, kt_ref, dot_ref, dq_ref, dk_ref, dv_ref, acc_ref, dx_ref, bias_ref, dw_ref, tab_ref, tab_in_ref = rest[:12]
     local_sem, row_send, row_recv, tab_send, tab_recv, send_sem, recv_sem = rest[12:19]
     rest = rest[19:]
-    keeps, rest = rest[:DENSE], rest[DENSE:]
+    keeps, rest = rest[:PIECES], rest[PIECES:]
     firsts, seconds, thirds, fourths = (rest[j * items : (j + 1) * items] for j in range(4))
 
     length, width = q_ref.shape
@@ -811,20 +939,23 @@
     mine = x * 2 + c
 
     def axes(a):
-        return (y, x) if SCATTER_ORDERS[a][0] == "y" else (x, y)
+        return (y, x) if order_of(a)[0] == "y" else (x, y)
 
     def device_along(axis):
         return device_at(z, 1 - y, x, c) if axis == "y" else device_at(z, y, 1 - x, c)
 
     def half(a, ref, place):
-        return ref.at[:, place] if SCATTER_ORDERS[a][0] == "y" else ref.at[:, :, place]
+        return ref.at[:, place] if order_of(a)[0] == "y" else ref.at[:, :, place]
 
     def whole_of(a, core):
-        ref = parts[a] if a < DENSE else dw_ref.at[a - DENSE]
-        return ref.at[:, :, :, core]
+        if a >= PIECES:
+            return dw_ref.at[a - PIECES].at[:, :, :, core]
+        array = DENSE_ITEMS[a][0]
+        (r0, rows), (c0, columns) = cut_of(a, parts[array].shape[-2:])
+        return parts[array].at[:, :, :, core, pl.ds(r0, rows), pl.ds(c0, columns)]
 
     def kept(a):
-        return keeps[a] if a < DENSE else whole_of(a, c)
+        return keeps[a] if a < PIECES else whole_of(a, c)
 
     def load(a, turn):
         place = 1 - axes(a)[0] if turn == 0 else axes(a)[0]
@@ -840,10 +971,10 @@
             device = device_at(z, y, x, 1 - c)
         elif number == 2:
             source, target = half(a, kept(a), 1 - at), seconds[a]
-            device = device_along(SCATTER_ORDERS[a][0])
+            device = device_along(order_of(a)[0])
         elif number == 3:
             source, target = half(a, kept(a), at).at[:, 1 - other], thirds[a]
-            device = device_along(SCATTER_ORDERS[a][1])
+            device = device_along(order_of(a)[1])
         else:
             there = lax.rem(z + number - 3, ZS)
             source, target = half(a, kept(a), at).at[:, other].at[there], fourths[a].at[number - 4]
@@ -867,13 +998,13 @@
                 where.append(lax.rem(i, size))
                 i = i // size
             where = tuple(reversed(where))
-            target[where] = (target[where].astype(F32) + source[where].astype(F32)).astype(target.dtype)
+            target[where] = target[where] + source[where]
             return carry
 
         lax.fori_loop(0, total, step, 0)
 
     def begin(a):
-        if a < DENSE:
+        if a < PIECES:
             load(a, 0).start()
             load(a, 1).start()
         copy_of(a, 0).start()
@@ -881,7 +1012,7 @@
 
     def after_core(a, turn):
         place = 1 - axes(a)[0] if turn == 0 else axes(a)[0]
-        if a < DENSE:
+        if a < PIECES:
             load(a, turn).wait()
         copy_of(a, turn).wait_recv()
         add_into(half(a, kept(a), place), half(a, firsts[a], place))
@@ -914,10 +1045,12 @@
             + fourths[a][1].astype(F32)
             + fourths[a][2].astype(F32)
         )
-        if a < DENSE:
-            dense_outs[a][...] = total
+        if a < PIECES:
+            out = dense_outs[DENSE_ITEMS[a][0]]
+            (r0, rows), (c0, columns) = cut_of(a, out.shape)
+            out[r0 : r0 + rows, c0 : c0 + columns] = total
         else:
-            s = (a - DENSE) * width
+            s = (a - PIECES) * width
             for j, out in enumerate((out_q, out_k, out_v)):
                 out[:, s : s + width] = total[:, j * width : (j + 1) * width]
 
@@ -941,7 +1074,7 @@
             source, target = dx_ref.at[mine], back_ref.at[mine]
         else:
             source, target = logit_ref, logits_ref.at[mine]
-        return pltpu.make_async_copy(source, target, local_sem.at[DENSE, which])
+        return pltpu.make_async_copy(source, target, local_sem.at[PIECES, which])
 
     def table_copy(level):
         if level < 3:
@@ -976,6 +1109,11 @@
             ).wait_recv()
 
     def table_level(level):
+        if level == 3:
+            for last in (3, 4, 5):
+                table_wait(last)
+            table_ref[...] = (tab_in_ref[3] + tab_in_ref[4]) + (tab_in_ref[5] + tab_in_ref[6])
+            return
         table_wait(level)
         tab_ref[level + 1] = tab_ref[level] + tab_in_ref[level]
         if level < 2:
@@ -985,23 +1123,30 @@
             for nxt in (4, 3, 5):
                 table_copy(nxt).start()
 
-    dense_items = tuple(range(DENSE))
-    plan = {
-        2: [functools.partial(after_core, 0, 0), functools.partial(after_core, 1, 0)],
-        3: [functools.partial(after_core, a, 0) for a in dense_items[2:]] + [functools.partial(after_core, 0, 1)],
-        4: [functools.partial(begin, DENSE)] + [functools.partial(after_core, a, 1) for a in dense_items[1:]],
-        5: [functools.partial(after_core, DENSE, 0), functools.partial(after_core, DENSE, 1)],
-        8: [functools.partial(begin, DENSE + 1), functools.partial(after_first, 0)],
-        9: [functools.partial(after_core, DENSE + 1, 0), functools.partial(after_core, DENSE + 1, 1), functools.partial(after_first, 1)],
-        10: [functools.partial(after_first, a) for a in dense_items[2:]],
-        11: [functools.partial(after_second, 0), functools.partial(after_second, 1)],
-    }
+    def take_up(point):
+        for word in SCATTER_PLAN.get(point, "").split():
+            kind, a = word[:-1], int(word[-1]) if word != "dx" else 0
+            if kind == "b":
+                begin(a)
+            elif kind == "c0" or kind == "c1":
+                after_core(a, int(kind[1]))
+            elif kind == "f":
+                after_first(a)
+            elif kind == "s":
+                after_second(a)
+            elif kind == "z":
+                finish(a)
+            elif kind == "t":
+                table_level(a)
+            else:
+                for k in (3, 2, 1):
+                    row_copy(0, k).start()
+                row_own(0).start()
 
     @pl.when(group == 0)
     def _():
         meet(all_partners(z, y, x, c))
-        for a in range(DENSE):
-            begin(a)
+        take_up(-1)
         for k in range(1, 4):
             row_copy(1, k).start()
         row_own(1).start()
@@ -1017,12 +1162,11 @@
     lane_head = lax.broadcasted_iota(jnp.int32, (1, width), 1) // HEAD_DIM
 
     def step(i, carry):
-        for point, actions in plan.items():
+        for point in range(groups * points):
 
             @pl.when((group == point // points) & (i == point % points))
-            def _(actions=actions):
-                for action in actions:
-                    action()
+            def _(point=point):
+                take_up(point)
 
         at = pl.multiple_of(i * chunk, chunk)
         query_doc = doc_numbers(lax.broadcasted_iota(jnp.int32, (1, chunk), 1) + at, ends)
@@ -1073,12 +1217,7 @@
 
     @pl.when(group == groups - 1)
     def _():
-        last = items - 1
-        begin(last)
         dx_ref[...] = acc_ref[...].reshape(dx_ref.shape).astype(BF)
-        for k in (3, 2, 1):
-            row_copy(0, k).start()
-        row_own(0).start()
         tab_ref[0, 0:CLASSES] = small_a_ref[0:CLASSES]
         for g in range(groups):
             tab_ref[0, B_QUERY : B_QUERY + 2, g * width : (g + 1) * width] = bias_ref[g, 0:2, :]
@@ -1092,29 +1231,7 @@
             tab_ref[0, 12 + j : 13 + j] = bi_ref[:, j * full : (j + 1) * full]
         tab_ref[0, 17:TABLE_ROWS] = jnp.zeros((TABLE_ROWS - 17, full), F32)
         table_copy(0).start()
-        after_first(DENSE)
-        after_core(last, 0)
-        after_core(last, 1)
-        table_level(0)
-        for a in dense_items[2:]:
-            after_second(a)
-        after_first(DENSE + 1)
-        table_level(1)
-        finish(0)
-        finish(1)
-        after_second(DENSE)
-        after_first(last)
-        table_level(2)
-        after_second(DENSE + 1)
-        for a in dense_items[2:]:
-            finish(a)
-        after_second(last)
-        finish(DENSE)
-        finish(DENSE + 1)
-        for level in (3, 4, 5):
-            table_wait(level)
-        table_ref[...] = (tab_in_ref[3] + tab_in_ref[4]) + (tab_in_ref[5] + tab_in_ref[6])
-        finish(last)
+        take_up(groups * points)
         for a in range(items):
             for number in range(7):
                 copy_of(a, number).wait_send()
@@ -1138,13 +1255,15 @@
     part = pl.BlockSpec((length, group), lambda g: (0, g))
     blocks = [p.shape[1:] for p in parts]
     split = [p.reshape((ZS, 2, 2, 2) + b) for p, b in zip(parts, blocks)]
-    blocks = blocks + [(share, 3 * group)] * groups
+    shapes = [r for r in blocks]
+    cuts = [cut_of(a, blocks[DENSE_ITEMS[a][0]]) for a in range(PIECES)]
+    blocks = [(r[1], q[1]) for r, q in cuts] + [(share, 3 * group)] * groups
     hbm = pl.BlockSpec(memory_space=pl.ANY)
 
     def fixed(shape):
         return pl.BlockSpec(shape, lambda g: (0,) * len(shape))
 
-    results = [b for b in blocks[:DENSE]] + [(share, width)] * 3
+    results = shapes + [(share, width)] * 3
     arriving = []
     for lead in ((ZS, 2, 2), (ZS, 2), (ZS,), (ZS - 1,)):
         arriving += [pltpu.VMEM(lead + b, BF) for b in blocks]
@@ -1182,7 +1301,7 @@
             pltpu.VMEM((groups, ZS, 2, 2, 2, share, 3 * group), BF),
             pltpu.VMEM((4, TABLE_ROWS, width), F32),
             pltpu.VMEM((3 + ZS, TABLE_ROWS, width), F32),
-            pltpu.SemaphoreType.DMA((DENSE + 1, 2)),
+            pltpu.SemaphoreType.DMA((PIECES + 1, 2)),
             pltpu.SemaphoreType.DMA((2, 3)),
             pltpu.SemaphoreType.DMA((2, 3)),
             pltpu.SemaphoreType.DMA((6,)),
@@ -1190,7 +1309,7 @@
             pltpu.SemaphoreType.DMA((items, 7)),
             pltpu.SemaphoreType.DMA((items, 7)),
         ]
-        + [pltpu.VMEM((ZS, 2, 2) + b, BF) for b in blocks[:DENSE]]
+        + [pltpu.VMEM((ZS, 2, 2) + b, BF) for b in blocks[:PIECES]]
         + arriving,
         compiler_params=pltpu.CompilerParams(
             collective_id=2, has_side_effects=True, vmem_limit_bytes=60 * 2**20
@@ -1290,7 +1409,7 @@
         )
 
 
-def dense(lens, labels, rows, att, w_mid, w_outer, vectors, b_inner, b_class_row):
+def dense(lens, labels, rows, att, w_inner, w_out, w_pool, w_outer, vectors, b_inner, b_class_row):
     length, width = rows.shape
     hidden = w_outer.shape[0]
     tile = 256
@@ -1301,7 +1420,6 @@
     def fixed(shape, column=0):
         return pl.BlockSpec(shape, lambda i: (0, column))
 
-    spots = hidden // width
     return pl.pallas_call(
         dense_kernel,
         grid=(steps,),
@@ -1319,7 +1437,7 @@
         ],
         in_specs=[
             SMEM, SMEM, part, part,
-            fixed((width, hidden)), fixed((width, width), spots), fixed((width, width), spots + 1),
+            fixed((width, hidden)), fixed((width, width)), fixed((width, width)),
             fixed((hidden, width)), fixed((VEC_ROWS, width)), fixed((1, hidden)), fixed((1, VEC_ROWS)),
         ],
         out_specs=[
@@ -1330,7 +1448,7 @@
         compiler_params=pltpu.CompilerParams(vmem_limit_bytes=60 * 2**20),
         cost_estimate=pl.CostEstimate(flops=11 * 10**9, bytes_accessed=40 * 10**6, transcendentals=3 * 2**20),
         name="dense",
-    )(lens, labels, rows, att, w_mid, w_mid, w_mid, w_outer, vectors, b_inner, b_class_row)
+    )(lens, labels, rows, att, w_inner, w_out, w_pool, w_outer, vectors, b_inner, b_class_row)
 
 
 def norm_back(grad, values, gain):
@@ -1389,7 +1507,7 @@
     small_ref[5:6, :] += shift1
 
 
-def dense_back(lens, cot, summed, pre, dact, w_mid, w_outer, vectors, first):
+def dense_back(lens, cot, summed, pre, dact, w_inner, w_out, w_outer, vectors, first):
     length, width = cot.shape
     hidden = w_outer.shape[0]
     tile = 256
@@ -1399,7 +1517,6 @@
     def fixed(shape, column=0):
         return pl.BlockSpec(shape, lambda i: (0, column))
 
-    spots = hidden // width
     return pl.pallas_call(
         dense_back_kernel,
         grid=(length // tile,),
@@ -1414,14 +1531,14 @@
         ],
         in_specs=[
             SMEM, part, part, part, wide,
-            fixed((width, hidden)), fixed((width, width), spots), fixed((hidden, width)),
+            fixed((width, hidden)), fixed((width, width)), fixed((hidden, width)),
             fixed((VEC_ROWS, width)), fixed((VEC_ROWS, width)),
         ],
         out_specs=[part, wide, part, part, part, fixed((8, width)), fixed((1, hidden))],
         compiler_params=pltpu.CompilerParams(vmem_limit_bytes=60 * 2**20),
         cost_estimate=pl.CostEstimate(flops=11 * 10**9, bytes_accessed=40 * 10**6, transcendentals=0),
         name="dense_back",
-    )(lens, cot, summed, pre, dact, w_mid, w_mid, w_outer, vectors, first)
+    )(lens, cot, summed, pre, dact, w_inner, w_out, w_outer, vectors, first)
 
 
 def exchange(blocks):
@@ -1452,49 +1569,41 @@
     share = width // devices
     hidden_share = b_inner.shape[0]
     hidden = hidden_share * devices
-    group = 256
-    qkv_shard = jnp.concatenate(
-        [w[:, s : s + group] for s in range(0, width, group) for w in (w_query, w_key, w_value)], axis=1
-    ).astype(BF)
-    mid_shard = jnp.concatenate([w_inner, w_out, w_pool], axis=1).astype(BF)
-    outer_shard = w_outer.astype(BF)
-    vec_shard = jnp.concatenate(
+    device = lax.axis_index("dp") * 4 + mine
+    columns = jnp.stack(
         [
-            w_class.T.reshape(-1), b_query, b_value, b_out, first_gain, first_shift, b_outer, second_gain, second_shift,
-            b_pool, b_inner,
+            *(w_class[:, j] for j in range(CLASSES)), b_query, b_value, b_out, first_gain, first_shift, b_outer, second_gain,
+            second_shift, b_pool,
         ]
     )
-    vec_len = vec_shard.shape[0]
-    vec_shard = jnp.pad(vec_shard, (0, 1024 - vec_len)).reshape(8, 128).astype(BF).astype(F32)
-
-    rows, w_qkv, vec_all, w_mid, w_outer_all = gather_all(
-        inputs, [qkv_shard, vec_shard, mid_shard, outer_shard], ["xy", "xy", "xy", "yx"], 1
+    table = lax.dynamic_update_slice(jnp.zeros((12, width), F32), columns, (0, device * share))
+    inner_rows = lax.dynamic_update_slice(jnp.zeros((hidden,), F32), b_inner, (device * hidden_share,)).reshape(4, width)
+    table = jnp.concatenate([table, inner_rows], axis=0).astype(BF).astype(F32)
+    q, k, v, att, lse, w_qkv, vectors, rows, full_inner, full_out, full_pool, full_outer = attend(
+        own_lens, inputs, table, [w_query, w_key, w_value], [w_inner, w_out, w_pool, w_outer]
     )
     rows = rows.reshape(length, width)
-    w_qkv = w_qkv.reshape(width, 3 * width)
-    w_mid = w_mid.reshape(width, hidden + 2 * width)
-    w_outer_all = w_outer_all.reshape(hidden, width)
-    flat_vec = vec_all.reshape(devices, 1024)
-    rows_used = B_POOL + 1
-    vectors = flat_vec[:, : rows_used * share].reshape(devices, rows_used, share).transpose(1, 0, 2).reshape(rows_used, width)
-    vectors = jnp.pad(vectors, ((0, VEC_ROWS - rows_used), (0, 0)))
-    b_inner_row = flat_vec[:, rows_used * share : vec_len].reshape(1, hidden)
+    full_inner = full_inner.reshape(width, hidden)
+    full_out = full_out.reshape(width, width)
+    full_pool = full_pool.reshape(width, width)
+    full_outer = full_outer.reshape(hidden, width)
+    b_inner_row = vectors[12:16].reshape(1, hidden)
     b_class_row = jnp.pad(b_class, (0, VEC_ROWS - CLASSES)).reshape(1, VEC_ROWS)
 
+    cotangent, _ = lax.optimization_barrier((cotangent, att))
     cot = exchange(cotangent).reshape(length, width)
-    q, k, v, att, lse = attend(own_lens, rows, w_qkv, vectors)
     pre, summed, low, act, dact, result, grad_pool, first, small_a, logits = dense(
-        own_lens, own_labels, rows, att, w_mid, w_outer_all, vectors, b_inner_row, b_class_row
+        own_lens, own_labels, rows, att, full_inner, full_out, full_pool, full_outer, vectors, b_inner_row, b_class_row
     )
     layer_out = exchange(result.reshape(seqs, local_len, width))
     outer, inner, branch, datt, grad_pre, small_b, grad_b_inner = dense_back(
-        own_lens, cot, summed, pre, dact, w_mid, w_outer_all, vectors, first
+        own_lens, cot, summed, pre, dact, full_inner, full_out, full_outer, vectors, first
     )
     grad_outer_w = tn(act, outer).astype(BF)
     grad_inner_w = tn(low, inner).astype(BF)
     grad_out_w = tn(att, branch).astype(BF)
     logit_block = jnp.pad(logits[:docs, :CLASSES], ((0, 8 - docs), (0, 128 - CLASSES)))
-    grad_inputs, all_logits, table, o_inner, o_outer, o_out, o_pool, o_query, o_key, o_value = attend_back(
+    grad_inputs, all_logits, totals, o_inner, o_outer, o_out, o_pool, o_query, o_key, o_value = attend_back(
         own_lens, rows, w_qkv, q, k, v, att, datt, lse, grad_pre, small_a, small_b, grad_b_inner, logit_block,
         [
             grad_inner_w.reshape(devices, share, hidden),
@@ -1503,9 +1612,8 @@
             grad_pool.reshape(devices, share, width),
         ],
     )
-    device = lax.axis_index("dp") * 4 + mine
-    columns = lax.dynamic_slice_in_dim(table[:12], device * share, share, 1)
-    own_b_inner = lax.dynamic_slice_in_dim(table[12:16].reshape(hidden), device * hidden_share, hidden_share, 0)
+    columns = lax.dynamic_slice_in_dim(totals[:12], device * share, share, 1)
+    own_b_inner = lax.dynamic_slice_in_dim(totals[12:16].reshape(hidden), device * hidden_share, hidden_share, 0)
     return (
         layer_out,
         all_logits[:, :docs, :CLASSES],
@@ -1528,7 +1636,7 @@
         o_pool,
         columns[B_POOL],
         columns[:CLASSES].T,
-        table[16, :CLASSES],
+        totals[16, :CLASSES],
     )
 
 

time: 392 us -> 336 us (0.86)
  Pallas kernels: 324 us -> 265 us
  local copies, waits for them, and re-layouts: 34.4 us -> 42 us
    pallas_call x1, Pallas kernels: 135 us -> 105 us  [attend_back(): pl.pallas_call(functools.partial(attend_back_kernel, groups), grid=(group...]
    pallas_call x2 -> x1, Pallas kernels: 129 us -> 101 us  [attend(): pl.pallas_call(functools.partial(attend_kernel, groups), grid=(groups,),...]
    unnamed x101 -> x77, local copies, waits for them, and re-layouts: 14.9 us -> 20.8 us
  transfers between devices with their start and end apart: 6 -> 6, of which waited for: 0 -> 0; matrix products, arithmetic and copies ran while one was open for 11% -> 12% of each run, Pallas kernels for 83% -> 49%
where the time goes in v3:
time: 336 us; the launch traced here: 335 us
  Pallas kernels  265 us (79%)
  local copies, waits for them, and re-layouts  42 us (12%)
  matrix products  21.7 us (6%)
  starting transfers between devices  4.97 us (1%)
    pallas_call x1, Pallas kernels, attend_back(): pl.pallas_call(functools.partial(attend_back_kernel, groups), grid=(group...  105 us
    pallas_call x1, Pallas kernels, attend(): pl.pallas_call(functools.partial(attend_kernel, groups), grid=(groups,),...  101 us
    pallas_call x1, Pallas kernels, dense(): pl.pallas_call(dense_kernel, grid=(steps,), out_shape=[jax.ShapeDtypeStru...  34 us
    pallas_call x1, Pallas kernels, dense_back(): pl.pallas_call(dense_back_kernel, grid=(length // tile,), out_shape=[jax....  24.9 us
    dot_general x3, matrix products, tn(): lax.dot_general(a, b, (((0,), (0,)), ((), ())), preferred_element_type=F32)  21.7 us
    unnamed x77, local copies, waits for them, and re-layouts  20.8 us
  transfers between devices with their start and end apart: 6, of which 0 were waited for; matrix products, arithmetic and copies ran while one was open for 12% of the time, Pallas kernels for 49%

profile of v3, /device:TPU:0, one launch (start us, length us, event | category | flops | bytes accessed | tf_op | source)
XLA Modules:
  0.0 334.6 jit_solution(9423103820819375678)
XLA Ops:
  0.7 0.9 dynamic_update_slice.31
  1.6 0.8 slice_bitcast_fusion.2
  2.4 1.5 stack.39
  4.1 1.0 copy-done.3
  5.0 1.0 copy-done.4
  6.0 0.9 copy-done.6
  6.9 0.9 copy-done.7
  7.8 0.9 copy-done.8
  8.7 0.9 copy-done.9
  9.5 0.9 copy-done.10
  10.4 101.3 %attend.1 = (bf16[1024,768]{1,0:T(8,128)(2,1)S(1)}, bf16[1024,768]{1,0:T(8,128)(2,1)}, bf16[1024,768]{1,0:T(8,128)(2,1)}, bf16[1024,768]{1,0:T(8,128)(2,1)}, f32...) custom-call(s32[4]{0:T(128)S(1)} %fusion.1.refs_0_.lens_ref, ...), custom_call_target="tpu_custom_call" | custom-call | tf_op jit(solution)/shard_map/attend/pallas_call | solution.py:834
  111.7 1.1 copy-done.2
  112.8 0.6 copy-done.5
  113.5 1.0 copy-done.13
  114.5 1.0 copy-done.14
  115.7 1.0 constant_dynamic-slice_fusion.1
  117.0 1.1 collective-permute-start.4
  118.1 1.2 collective-permute-start.5
  119.2 1.2 fusion.2.labels_ref
  121.6 34.0 %dense.1 = (f32[1024,768]{1,0:T(8,128)}, f32[1024,768]{1,0:T(8,128)}, bf16[1024,768]{1,0:T(8,128)(2,1)}, bf16[1024,3072]{1,0:T(8,128)(2,1)}, bf16[1024,3072]{1,0...) custom-call(s32[4]{0:T(128)} %copy-done.12, ...), custom_call_target="tpu_custom_call" | custom-call | flops 11000000512 | bytes 40000000 | tf_op jit(solution)/shard_map/dense/pallas_call | solution.py:1423
  155.7 1.3 copy-done.22
  157.0 1.1 constant_dynamic-slice_fusion.4
  158.0 1.0 collective-permute-start.1
  159.0 0.7 slice.61
  160.3 1.4 collective-permute-start.2
  161.8 1.0 constant_dynamic-update-slice_fusion.2
  162.8 1.0 constant_dynamic-update-slice_fusion.1
  163.8 1.0 constant_dynamic-update-slice_fusion
  164.9 1.1 copy-done.20
  166.0 24.9 %dense_back.1 = (bf16[1024,768]{1,0:T(8,128)(2,1)}, bf16[1024,3072]{1,0:T(8,128)(2,1)}, bf16[1024,768]{1,0:T(8,128)(2,1)}, bf16[1024,768]{1,0:T(8,128)(2,1)}, f3...) custom-call(s32[4]{0:T(128)} %copy-done.12, bf16[1024,768]{1,0:T(8,128)(2,1)} %bitcast.71, ...), custom_call_target="tpu_custom_call" | custom-call | flops 11000000512 | bytes 40000000 | tf_op jit(solution)/shard_map/dense_back/pallas_call | solution.py:1520
  190.9 9.3 %convolution_convert_fusion.1 = bf16[768,3072]{1,0:T(8,128)(2,1)} fusion(bf16[1024,768]{1,0:T(8,128)(2,1)} %get-tuple-element.86, bf16[1024,3072]{1,0:T(8,128)(2,1)} %get-tuple-element.87), kind=kOutput, calls=%fused_computation.1 | convolution fusion | flops 4834197504 | bytes 12582912 | tf_op jit(solution)/shard_map/dot_general | solution.py:527
  200.2 9.9 %convolution_convert_fusion = bf16[3072,768]{1,0:T(8,128)(2,1)} fusion(bf16[1024,3072]{1,0:T(8,128)(2,1)} %get-tuple-element.88, bf16[1024,768]{1,0:T(8,128)(2,1)S(1)} %copy-done.32), kind=kOutput, calls=%fused_computation | convolution fusion | flops 4834197504 | bytes 12582912 | tf_op jit(solution)/shard_map/dot_general | solution.py:527
  210.2 2.5 convolution_convert_fusion.2
  212.6 104.9 %attend_back.1 = (bf16[4,256,768]{2,1,0:T(8,128)(2,1)}, f32[4,8,128]{2,1,0:T(8,128)}, f32[24,768]{1,0:T(8,128)}, f32[24,3072]{1,0:T(8,128)}, f32[96,768]{1,0:T(8...) custom-call(s32[4]{0:T(128)} %copy-done.12, ...), custom_call_target="tpu_custom_call" | custom-call | tf_op jit(solution)/shard_map/attend_back/pallas_call | solution.py:1271
  317.5 0.9 slice.63
  319.1 1.0 constant_dynamic-update-slice_fusion.5
  320.1 0.7 fusion
  320.8 0.7 slice.69
  321.5 1.3 slice.62
  322.8 1.4 copy.45
  324.8 1.3 dynamic_slice.49
  326.1 1.2 slice_bitcast_fusion.1
  327.3 1.0 constant_dynamic-update-slice_fusion.3
  328.5 1.1 copy.65
  330.0 0.6 copy.66
  331.3 0.6 copy.68
  332.6 0.7 copy.70
  333.3 0.7 copy.71
  (79 shorter events, 6.2 us)
Async XLA Ops:
  0.7 1.7 copy-start
  2.4 113.2 %copy-start.12 = (s32[4]{0:T(128)}, s32[4]{0:T(128)S(1)}, u32[]{:S(2)}) copy-start(s32[4]{0:T(128)S(1)} %fusion.1.refs_0_.lens_ref) | copy-start | bytes 52
  4.1 1.0 copy-start.3
  5.0 1.0 copy-start.4
  6.0 0.9 copy-start.6
  6.9 0.9 copy-start.7
  7.8 0.9 copy-start.8
  8.7 0.9 copy-start.9
  9.5 0.9 copy-start.10
  10.4 105.2 %copy-start.21 = (bf16[4,256,768]{2,1,0:T(8,128)(2,1)S(1)}, bf16[4,256,768]{2,1,0:T(8,128)(2,1)}, u32[]{:S(2)}) copy-start(bf16[4,256,768]{2,1,0:T(8,128)(2,1)} %param.24) | copy-start | bytes 4718596
  111.7 1.1 copy-start.2
  112.8 0.6 copy-start.5
  113.5 1.0 copy-start.13
  114.5 1.0 copy-start.14
  115.5 4.9 %copy-start.11 = (f32[16,768]{1,0:T(8,128)}, f32[16,768]{1,0:T(8,128)S(1)}, u32[]{:S(2)}) copy-start(f32[16,768]{1,0:T(8,128)S(1)} %get-tuple-element.68.vec_ref) | copy-start | bytes 147460
  115.6 5.4 %copy-start.30 = (f32[3]{0:T(128)S(1)}, f32[3]{0:T(128)}, u32[]{:S(2)}) copy-start(f32[3]{0:T(128)} %param.45) | copy-start | bytes 40
  116.7 3.7 %copy-start.18 = (bf16[4,256,768]{2,1,0:T(8,128)(2,1)}, bf16[4,256,768]{2,1,0:T(8,128)(2,1)S(1)}, u32[]{:S(2)}) copy-start(bf16[4,256,768]{2,1,0:T(8,128)(2,1)S(1)} %get-tuple-element.127) | copy-start | bytes 4718596
  116.7 43.6 %collective-permute-start.3 = (bf16[1,256,768]{2,1,0:T(8,128)(2,1)}, bf16[1,256,768]{2,1,0:T(8,128)(2,1)}, u32[]{:S(2)}, u32[]{:S(2)}) collective-permute-start(bf16[1,256,768]{2,1,0:T(8,128)(2,1)} %get-tuple-element.126), channel_id=1, source_target_pairs={{0,1},{1,2},{2,3},{3,0},{4,5},{5,6},{6,7},{7,4},{8,9},{9,10},{10,1... | collective-permute-start | bytes 1179656 | tf_op jit(solution)/shard_map/ppermute | solution.py:1552
  117.0 45.8 %collective-permute-start.4 = (bf16[1,256,768]{2,1,0:T(8,128)(2,1)}, bf16[1,256,768]{2,1,0:T(8,128)(2,1)}, u32[]{:S(2)}, u32[]{:S(2)}) collective-permute-start(bf16[1,256,768]{2,1,0:T(8,128)(2,1)} %get-tuple-element.125), channel_id=1, source_target_pairs={{0,2},{1,3},{2,0},{3,1},{4,6},{5,7},{6,4},{7,5},{8,10},{9,11},{10,... | collective-permute-start | bytes 1179656 | tf_op jit(solution)/shard_map/ppermute | solution.py:1552
  118.1 45.8 %collective-permute-start.5 = (bf16[1,256,768]{2,1,0:T(8,128)(2,1)}, bf16[1,256,768]{2,1,0:T(8,128)(2,1)}, u32[]{:S(2)}, u32[]{:S(2)}) collective-permute-start(bf16[1,256,768]{2,1,0:T(8,128)(2,1)} %get-tuple-element.124), channel_id=1, source_target_pairs={{0,3},{1,0},{2,1},{3,2},{4,7},{5,4},{6,5},{7,6},{8,11},{9,8},{10,9... | collective-permute-start | bytes 1179656 | tf_op jit(solution)/shard_map/ppermute | solution.py:1552
  155.5 1.4 copy-start.22
  157.0 4.8 %copy-start.19 = (bf16[4,256,768]{2,1,0:T(8,128)(2,1)S(1)}, bf16[4,256,768]{2,1,0:T(8,128)(2,1)}, u32[]{:S(2)}) copy-start(bf16[4,256,768]{2,1,0:T(8,128)(2,1)} %copy-done.18) | copy-start | bytes 4718596
  158.0 161.1 %collective-permute-start = (bf16[1,256,768]{2,1,0:T(8,128)(2,1)}, bf16[1,256,768]{2,1,0:T(8,128)(2,1)}, u32[]{:S(2)}, u32[]{:S(2)}) collective-permute-start(bf16[1,256,768]{2,1,0:T(8,128)(2,1)} %get-tuple-element.130), channel_id=1, source_target_pairs={{0,1},{1,2},{2,3},{3,0},{4,5},{5,6},{6,7},{7,4},{8,9},{9,10},{10,1... | collective-permute-start | bytes 1179656 | tf_op jit(solution)/shard_map/ppermute | solution.py:1552
  158.0 168.1 %collective-permute-start.1 = (bf16[1,256,768]{2,1,0:T(8,128)(2,1)}, bf16[1,256,768]{2,1,0:T(8,128)(2,1)S(1)}, u32[]{:S(2)}, u32[]{:S(2)}) collective-permute-start(bf16[1,256,768]{2,1,0:T(8,128)(2,1)} %get-tuple-element.129), channel_id=1, source_target_pairs={{0,2},{1,3},{2,0},{3,1},{4,6},{5,7},{6,4},{7,5},{8,10},{9,11},{10,... | collective-permute-start | bytes 1179656 | tf_op jit(solution)/shard_map/ppermute | solution.py:1552
  160.3 167.0 %collective-permute-start.2 = (bf16[1,256,768]{2,1,0:T(8,128)(2,1)}, bf16[1,256,768]{2,1,0:T(8,128)(2,1)}, u32[]{:S(2)}, u32[]{:S(2)}) collective-permute-start(bf16[1,256,768]{2,1,0:T(8,128)(2,1)} %get-tuple-element.128), channel_id=1, source_target_pairs={{0,3},{1,0},{2,1},{3,2},{4,7},{5,4},{6,5},{7,6},{8,11},{9,8},{10,9... | collective-permute-start | bytes 1179656 | tf_op jit(solution)/shard_map/ppermute | solution.py:1552
  164.9 1.1 copy-start.20
  190.9 9.3 %copy-start.32 = (bf16[1024,768]{1,0:T(8,128)(2,1)S(1)}, bf16[1024,768]{1,0:T(8,128)(2,1)}, u32[]{:S(2)}) copy-start(bf16[1024,768]{1,0:T(8,128)(2,1)} %get-tuple-element.89) | copy-start | bytes 4718596
  200.2 9.9 %copy-start.15 = (bf16[1024,768]{1,0:T(8,128)(2,1)S(1)}, bf16[1024,768]{1,0:T(8,128)(2,1)}, u32[]{:S(2)}) copy-start(bf16[1024,768]{1,0:T(8,128)(2,1)} %get-tuple-element.63.att_ref.refs_6_) | copy-start | bytes 4718596
  200.2 9.9 %copy-start.31 = (bf16[1024,768]{1,0:T(8,128)(2,1)S(1)}, bf16[1024,768]{1,0:T(8,128)(2,1)}, u32[]{:S(2)}) copy-start(bf16[1024,768]{1,0:T(8,128)(2,1)} %get-tuple-element.90) | copy-start | bytes 4718596
  317.5 10.8 %copy-start.16 = (bf16[4,256,768]{2,1,0:T(8,128)(2,1)S(1)}, bf16[4,256,768]{2,1,0:T(8,128)(2,1)}, u32[]{:S(2)}) copy-start(bf16[4,256,768]{2,1,0:T(8,128)(2,1)} %get-tuple-element.168) | copy-start | bytes 4718596
  328.4 1.7 copy-start.17
  328.4 1.6 copy-start.29
  328.4 2.3 copy-start.28
  328.4 2.9 copy-start.27
  328.4 3.5 %copy-start.26 = (f32[24,768]{1,0:T(8,128)S(1)}, f32[24,768]{1,0:T(8,128)}, u32[]{:S(2)}) copy-start(f32[24,768]{1,0:T(8,128)} %get-tuple-element.174) | copy-start | bytes 221188
  328.4 4.1 %copy-start.24 = (f32[24,3072]{1,0:T(8,128)S(1)}, f32[24,3072]{1,0:T(8,128)}, u32[]{:S(2)}) copy-start(f32[24,3072]{1,0:T(8,128)} %get-tuple-element.178) | copy-start | bytes 884740
  328.4 4.9 %copy-start.23 = (f32[96,768]{1,0:T(8,128)S(1)}, f32[96,768]{1,0:T(8,128)}, u32[]{:S(2)}) copy-start(f32[96,768]{1,0:T(8,128)} %get-tuple-element.180) | copy-start | bytes 884740
  328.4 6.2 %copy-start.1 = (s32[4,4]{1,0:T(4,128)S(1)}, s32[4,4]{1,0:T(4,128)}, u32[]{:S(2)}) copy-start(s32[4,4]{1,0:T(4,128)} %param.25) | copy-start | bytes 196
  330.0 4.0 %copy-start.25 = (f32[24,768]{1,0:T(8,128)S(1)}, f32[24,768]{1,0:T(8,128)}, u32[]{:S(2)}) copy-start(f32[24,768]{1,0:T(8,128)} %get-tuple-element.184) | copy-start | bytes 221188

commit v4 on v3

--- a/solution.py
+++ b/solution.py
@@ -559,10 +559,14 @@
 def doc_ends(lens_ref):
     ends = []
     total = 0
-    for d in range(lens_ref.shape[0]):
-        total = total + lens_ref[d]
+    for d in range(lens_ref.shape[1]):
+        total = total + lens_ref[lax.axis_index("fsdp"), d]
         ends.append(total)
     return ends
+
+
+def doc_starts(lens_ref):
+    return [0] + doc_ends(lens_ref)[:-1]
 
 
 def doc_numbers(places, ends):
@@ -577,20 +581,21 @@
 )
 GATHER_ORDERS = ("xy", "xy", "xy", "xy", "yx", "xy", "yx", "yx", "xy")
 GATHER_PLAN = {
-    -1: "b0 b1 b2 z0 b3 z1 b4 z2 z3 b5 f0 z4 b6 f1 s0 f2 e0",
-    0: "s1 s2 f3 f4 z5 b7",
-    1: "z6 e1 e2",
-    2: "b8",
-    3: "s3 z7",
-    4: "z8 e3",
-    6: "s4 f5 f6",
-    8: "f7 s5 f8 e4",
-    9: "e5",
-    10: "s6 s8",
-    11: "s7 e8 e6",
-    12: "e7",
+    -1: ("b0", "b1", "b2", "z0", "b3", "z1", "b4", "z2", "z3", "b5", "f0", "z4", "b6", "f1", "s0", "f2", "e0"),
+    0: ("s1", "s2", "f3", "f4", "z5", "b7"),
+    1: ("z6", "e1", "e2"),
+    2: ("b8",),
+    3: ("s3", "z7"),
+    4: ("z8", "e3"),
+    6: ("s4", "f5", "f6"),
+    8: ("f7", "s5", "f8", "e4"),
+    9: ("e5",),
+    10: ("s6", "s8"),
+    11: ("s7", "e8", "e6"),
+    12: ("e7",),
 }
 DENSE_ARRAYS = 4
+VECTORS = 9
 
 
 def part_of(piece, block):
@@ -602,9 +607,10 @@
 
 
 def attend_kernel(groups, *refs):
-    lens_ref, tokens_ref, table_ref, wq_ref, wk_ref, wv_ref = refs[:6]
-    shards = refs[6 : 6 + DENSE_ARRAYS]
-    refs = refs[6 + DENSE_ARRAYS :]
+    lens_ref, tokens_ref, class_ref = refs[:3]
+    vectors, b_inner_ref, (wq_ref, wk_ref, wv_ref) = refs[3 : 3 + VECTORS], refs[3 + VECTORS], refs[4 + VECTORS : 7 + VECTORS]
+    refs = refs[7 + VECTORS :]
+    shards, refs = refs[:DENSE_ARRAYS], refs[DENSE_ARRAYS:]
     q_ref, k_ref, v_ref, att_ref, lse_ref, w_ref, vec_ref, rows_ref = refs[:8]
     wholes = refs[8 : 8 + DENSE_ARRAYS]
     refs = refs[8 + DENSE_ARRAYS :]
@@ -708,7 +714,7 @@
         return pltpu.make_async_copy(own_block(a), view(a, (z, y, x, c)), local_sem.at[2 + a])
 
     def take_up(point):
-        for word in GATHER_PLAN.get(point, "").split():
+        for word in GATHER_PLAN.get(point, ()):
             kind, a = word[0], int(word[1:])
             if kind == "b":
                 for number in (1, 0, 2):
@@ -734,7 +740,22 @@
 
     @pl.when(group == 0)
     def _():
-        tab_ref[0] = table_ref[...]
+        device = ((z * 2 + y) * 2 + x) * 2 + c
+        full = tab_ref.shape[2]
+
+        def spread(values, at):
+            n = values.shape[1]
+            here = lax.broadcasted_iota(jnp.int32, (n, full), 1) - at == lax.broadcasted_iota(jnp.int32, (n, full), 0)
+            return nn(values.astype(BF), jnp.where(here, 1.0, 0.0).astype(BF))
+
+        share = class_ref.shape[1]
+        tab_ref[0, 0:CLASSES] = spread(class_ref[...], device * share)
+        for j, ref in enumerate(vectors):
+            tab_ref[0, CLASSES + j : CLASSES + j + 1] = spread(ref[...], device * share)
+        per_row = full // b_inner_ref.shape[1]
+        inner_bias = spread(b_inner_ref[...], lax.rem(device, per_row) * b_inner_ref.shape[1])
+        for j in range(4):
+            tab_ref[0, 12 + j : 13 + j] = jnp.where(device // per_row == j, inner_bias, 0.0)
         for g in range(groups):
             for j, ref in enumerate((wq_ref, wk_ref, wv_ref)):
                 qkv_shard[g, :, j * width : (j + 1) * width] = ref[:, g * width : (g + 1) * width].astype(BF)
@@ -816,7 +837,7 @@
         rows_out().wait()
 
 
-def attend(lens, tokens, table, qkv_shards, shards):
+def attend(lens, tokens, class_shard, vectors, b_inner, qkv_shards, shards):
     seqs, local_len, width = tokens.shape
     length = seqs * local_len
     group = 256
@@ -842,7 +863,9 @@
             jax.ShapeDtypeStruct(tokens.shape, BF),
         ]
         + [jax.ShapeDtypeStruct(lead + s.shape, BF) for s in shards],
-        in_specs=[SMEM, hbm, fixed(table.shape)]
+        in_specs=[SMEM, hbm, fixed(class_shard.shape)]
+        + [fixed(v.shape) for v in vectors]
+        + [fixed(b_inner.shape)]
         + [fixed(s.shape) for s in qkv_shards]
         + [fixed(s.shape) for s in shards],
         out_specs=[part] * 4
@@ -870,10 +893,10 @@
         ]
         + [pltpu.VMEM(s.shape, BF) for s in shards],
         compiler_params=pltpu.CompilerParams(
-            collective_id=1, has_side_effects=True, vmem_limit_bytes=48 * 2**20
+            collective_id=1, has_side_effects=True, vmem_limit_bytes=60 * 2**20
         ),
         name="attend",
-    )(lens, tokens, table, *qkv_shards, *shards)
+    )(lens, tokens, class_shard, *vectors, b_inner, *qkv_shards, *shards)
 
 
 DENSE = 4
@@ -883,20 +906,20 @@
 )
 GROUP_ORDERS = ("yx", "xy", "yx")
 SCATTER_PLAN = {
-    -1: "b0",
-    0: "b1",
-    1: "c00 c01 b2 c10 c11",
-    2: "b3",
-    3: "c02 b4 c12 f0 f1 c03 c13 b5",
-    4: "s0 s1 b6",
-    5: "c04 c05 c14 c15",
-    6: "z0 z1",
-    7: "f2 f3",
-    8: "b7",
-    9: "c06 c07 c16 c17",
-    10: "f4 s2 s3",
-    11: "f5",
-    12: "b8 dx f6 f7 t0 s4 s5 z2 c08 c18 z3 t1 s7 s6 f8 t2 z7 s8 z4 z6 z5 t3 z8",
+    -1: ("b0",),
+    0: ("b1",),
+    1: ("c00", "c01", "b2", "c10", "c11"),
+    2: ("b3",),
+    3: ("c02", "b4", "c12", "f0", "f1", "c03", "c13", "b5"),
+    4: ("s0", "s1", "b6"),
+    5: ("c04", "c05", "c14", "c15"),
+    6: ("z0", "z1"),
+    7: ("f2", "f3"),
+    8: ("b7",),
+    9: ("c06", "c07", "c16", "c17"),
+    10: ("f4", "s2", "s3"),
+    11: ("f5",),
+    12: ("b8", "dx", "f6", "f7", "t0", "s4", "s5", "z2", "c08", "c18", "z3", "t1", "s7", "s6", "f8", "t2", "z7", "s8", "z4", "z6", "z5", "t3", "z8"),
 }
 PIECES = len(DENSE_ITEMS)
 
@@ -921,8 +944,8 @@
     lens_ref, x_ref, w_ref, q_ref, k_ref, v_ref, att_ref, datt_ref, lse_ref, start_ref = refs[:10]
     small_a_ref, small_b_ref, bi_ref, logit_ref = refs[10:14]
     parts = refs[14 : 14 + DENSE]
-    back_ref, logits_ref, table_ref = refs[18:21]
-    dense_outs, (out_q, out_k, out_v) = refs[21 : 21 + DENSE], refs[21 + DENSE : 24 + DENSE]
+    back_ref, logits_ref, small_ref = refs[18:21]
+    dense_outs, group_outs = refs[21 : 21 + DENSE], refs[21 + DENSE : 24 + DENSE]
     rest = refs[24 + DENSE :]
     xt_ref, kt_ref, dot_ref, dq_ref, dk_ref, dv_ref, acc_ref, dx_ref, bias_ref, dw_ref, tab_ref, tab_in_ref = rest[:12]
     local_sem, row_send, row_recv, tab_send, tab_recv, send_sem, recv_sem = rest[12:19]
@@ -1051,7 +1074,7 @@
             out[r0 : r0 + rows, c0 : c0 + columns] = total
         else:
             s = (a - PIECES) * width
-            for j, out in enumerate((out_q, out_k, out_v)):
+            for j, out in enumerate(group_outs):
                 out[:, s : s + width] = total[:, j * width : (j + 1) * width]
 
     def row_copy(which, k):
@@ -1112,7 +1135,28 @@
         if level == 3:
             for last in (3, 4, 5):
                 table_wait(last)
-            table_ref[...] = (tab_in_ref[3] + tab_in_ref[4]) + (tab_in_ref[5] + tab_in_ref[6])
+            table = (tab_in_ref[3] + tab_in_ref[4]) + (tab_in_ref[5] + tab_in_ref[6])
+            device = ((z * 2 + y) * 2 + x) * 2 + c
+            full = table.shape[1]
+            row = lax.broadcasted_iota(jnp.int32, (full, 128), 0)
+            lane = lax.broadcasted_iota(jnp.int32, (full, 128), 1)
+
+            def own_lanes(values, size, at):
+                chosen = jnp.where((row == at + lane) & (lane < size), 1.0, 0.0)
+                return lax.dot_general(
+                    values, chosen, (((1,), (0,)), ((), ())), preferred_element_type=F32, precision=lax.Precision.HIGHEST
+                )
+
+            per_row = full * 4 // (8 * ZS)
+            small_ref[0:TABLE_ROWS] = own_lanes(table, full // (8 * ZS), device * (full // (8 * ZS)))
+            inner_bias = own_lanes(table, per_row, lax.rem(device, full // per_row) * per_row)
+            for j in range(4):
+
+                @pl.when(device // (full // per_row) == j)
+                def _(j=j):
+                    small_ref[TABLE_ROWS : TABLE_ROWS + 1] = inner_bias[12 + j : 13 + j]
+
+            small_ref[TABLE_ROWS + 1 : TABLE_ROWS + 2] = table[16:17, 0:128]
             return
         table_wait(level)
         tab_ref[level + 1] = tab_ref[level] + tab_in_ref[level]
@@ -1124,7 +1168,7 @@
                 table_copy(nxt).start()
 
     def take_up(point):
-        for word in SCATTER_PLAN.get(point, "").split():
+        for word in SCATTER_PLAN.get(point, ()):
             kind, a = word[:-1], int(word[-1]) if word != "dx" else 0
             if kind == "b":
                 begin(a)
@@ -1263,7 +1307,7 @@
     def fixed(shape):
         return pl.BlockSpec(shape, lambda g: (0,) * len(shape))
 
-    results = shapes + [(share, width)] * 3
+    results = [(TABLE_ROWS + 8, 128)] + shapes + [(share, width)] * 3
     arriving = []
     for lead in ((ZS, 2, 2), (ZS, 2), (ZS,), (ZS - 1,)):
         arriving += [pltpu.VMEM(lead + b, BF) for b in blocks]
@@ -1274,7 +1318,6 @@
         out_shape=[
             jax.ShapeDtypeStruct((4, local_len, width), BF),
             jax.ShapeDtypeStruct((4,) + logit_block.shape, F32),
-            jax.ShapeDtypeStruct((TABLE_ROWS, width), F32),
         ]
         + [jax.ShapeDtypeStruct(r, F32) for r in results],
         in_specs=[
@@ -1287,7 +1330,7 @@
             fixed(small_a.shape), fixed(small_b.shape), fixed(grad_b_inner.shape), hbm,
         ]
         + [hbm] * DENSE,
-        out_specs=[hbm, hbm, fixed((TABLE_ROWS, width))] + [fixed(r) for r in results],
+        out_specs=[hbm, hbm] + [fixed(r) for r in results],
         scratch_shapes=[
             pltpu.VMEM((width, length), BF),
             pltpu.VMEM((group, length), BF),
@@ -1318,6 +1361,43 @@
     )(lens, rows, w_groups, q, k, v, att, datt, lse, grad_pre, small_a, small_b, grad_b_inner, logit_block, *split)
 
 
+def row_copies(source_ref, target_ref, send_sem, recv_sem):
+    z, y, x, c = my_place()
+    copies = []
+    for k in (3, 2, 1):
+        px, pc = group_partner(k, x, c)
+        copies.append(
+            pltpu.make_async_remote_copy(
+                src_ref=source_ref.at[px * 2 + pc],
+                dst_ref=target_ref.at[x * 2 + c],
+                send_sem=send_sem.at[k - 1],
+                recv_sem=recv_sem.at[k - 1],
+                device_id=device_at(z, y, px, pc),
+                device_id_type=MESH,
+            )
+        )
+    return copies, pltpu.make_async_copy(source_ref.at[x * 2 + c], target_ref.at[x * 2 + c], send_sem.at[3])
+
+
+def begin_rows(*refs):
+    z, y, x, c = my_place()
+    meet([device_at(z, y, *group_partner(k, x, c)) for k in range(1, 4)])
+    copies, own = row_copies(*refs)
+    for copy in copies:
+        copy.start()
+    own.start()
+
+
+def end_rows(*refs):
+    copies, own = row_copies(*refs)
+    for copy in copies:
+        copy.wait()
+    own.wait()
+
+
+ROW_SEMAPHORES = [pltpu.SemaphoreType.DMA((4,)), pltpu.SemaphoreType.DMA((3,))]
+
+
 def normal_parts(v):
     bell = jnp.exp(v * v * -0.5)
     t = 1.0 / (1.0 + jnp.abs(v) * 0.23164189)
@@ -1334,16 +1414,33 @@
 
 
 def dense_kernel(
-    lens_ref, labels_ref, x_ref, att_ref, w_inner_ref, w_out_ref, w_pool_ref, w_outer_ref, vec_ref, b_inner_ref, b_class_ref,
-    pre_ref, summed_ref, low_ref, act_ref, dact_ref, lo_ref, dpool_ref, first_ref, small_ref, logits_ref, picked_ref,
+    lens_ref, labels_ref, b_class_ref, cot_ref, x_ref, att_ref, w_inner_ref, w_out_ref, w_pool_ref, w_outer_ref, vec_ref,
+    pre_ref, summed_ref, low_ref, act_ref, dact_ref, lo_ref, dpool_ref, first_ref, small_ref, logits_ref, cot_rows_ref,
+    picked_ref, row_send, row_recv,
 ):
     step = pl.program_id(0)
+
+    @pl.when(step == 0)
+    def _():
+        begin_rows(cot_ref, cot_rows_ref, row_send, row_recv)
+
     rows = x_ref.shape[0]
     hidden = w_inner_ref.shape[1]
     chunk = 512
 
     def vec(row):
         return vec_ref[row : row + 1, :]
+
+    full = vec_ref.shape[1]
+
+    def bias_at(s):
+        pieces, stop = [], s + chunk
+        while s < stop:
+            row, at = s // full, s % full
+            size = min(stop - s, full - at)
+            pieces.append(vec_ref[12 + row : 13 + row, at : at + size])
+            s += size
+        return pieces[0] if len(pieces) == 1 else jnp.concatenate(pieces, axis=1)
 
     pre = x_ref[...].astype(F32) + (nn(att_ref[...], w_out_ref[...]) + vec(B_OUT))
     pre_ref[...] = pre
@@ -1352,7 +1449,7 @@
     low_ref[...] = low
     total = normed + vec(B_OUTER)
     for s in range(0, hidden, chunk):
-        inner = nn(low, w_inner_ref[:, s : s + chunk]) + b_inner_ref[:, s : s + chunk]
+        inner = nn(low, w_inner_ref[:, s : s + chunk]) + bias_at(s)
         phi, bell = normal_parts(inner)
         activated = (inner * phi).astype(BF)
         act_ref[:, s : s + chunk] = activated
@@ -1361,13 +1458,13 @@
     summed_ref[...] = total
     result = (centered_parts(total)[0] * vec(GAIN2) + vec(SHIFT2)).astype(BF)
     lo_ref[...] = result
-    ends = doc_ends(lens_ref)
-    docs = len(ends)
+    starts = doc_starts(lens_ref)
+    docs = len(starts)
     places = lax.broadcasted_iota(jnp.int32, (VEC_ROWS, rows), 1) + step * rows
     row_doc = lax.broadcasted_iota(jnp.int32, (VEC_ROWS, rows), 0)
     hit = jnp.zeros((VEC_ROWS, rows), jnp.bool_)
     for d in range(docs):
-        hit = hit | ((row_doc == d) & (places == ends[d] - lens_ref[d]))
+        hit = hit | ((row_doc == d) & (places == starts[d]))
     found = nn(jnp.where(hit, 1.0, 0.0).astype(BF), result)
 
     @pl.when(step == 0)
@@ -1384,17 +1481,20 @@
         pooled = jnp.tanh(nn(picked, w_pool_ref[...]) + vec(B_POOL))
         pooled_low = pooled.astype(BF)
         table = vec_ref[...].astype(BF)
-        logits = nt(pooled_low, table) + b_class_ref[...]
         column = lax.broadcasted_iota(jnp.int32, (VEC_ROWS, VEC_ROWS), 1)
         row = lax.broadcasted_iota(jnp.int32, (VEC_ROWS, VEC_ROWS), 0)
-        logits_ref[...] = logits
+        class_bias = jnp.zeros((VEC_ROWS, VEC_ROWS), F32)
+        for j in range(CLASSES):
+            class_bias = jnp.where(column == j, b_class_ref[j], class_bias)
+        logits = nt(pooled_low, table) + class_bias
+        logits_ref[...] = jnp.concatenate([logits[0:8], jnp.zeros((8, 128 - VEC_ROWS), F32)], axis=1)
         live = column < CLASSES
         shown = jnp.where(live, logits, -jnp.inf)
         exps = jnp.where(live, jnp.exp(shown - jnp.max(shown, axis=-1, keepdims=True)), 0.0)
         probs = exps / jnp.sum(exps, axis=-1, keepdims=True)
         label = jnp.zeros((VEC_ROWS, VEC_ROWS), jnp.int32)
         for d in range(docs):
-            label = jnp.where(row == d, labels_ref[d], label)
+            label = jnp.where(row == d, labels_ref[lax.axis_index("fsdp"), d], label)
         grad = jnp.where(live & (row < docs), probs - jnp.where(label == column, 1.0, 0.0), 0.0)
         grad_low = grad.astype(BF)
         grad_pool = (nn(grad_low, table) * (1.0 - pooled * pooled)).astype(BF)
@@ -1407,9 +1507,10 @@
         small_ref[17:18, :] = jnp.concatenate(
             [class_sum, jnp.zeros((1, width - VEC_ROWS), F32)], axis=1
         )
-
-
-def dense(lens, labels, rows, att, w_inner, w_out, w_pool, w_outer, vectors, b_inner, b_class_row):
+        end_rows(cot_ref, cot_rows_ref, row_send, row_recv)
+
+
+def dense(lens, labels, b_class, cot, rows, att, w_inner, w_out, w_pool, w_outer, vectors):
     length, width = rows.shape
     hidden = w_outer.shape[0]
     tile = 256
@@ -1433,22 +1534,25 @@
             jax.ShapeDtypeStruct((width, width), BF),
             jax.ShapeDtypeStruct((VEC_ROWS, width), F32),
             jax.ShapeDtypeStruct((24, width), F32),
-            jax.ShapeDtypeStruct((VEC_ROWS, VEC_ROWS), F32),
+            jax.ShapeDtypeStruct((8, 128), F32),
+            jax.ShapeDtypeStruct(cot.shape, BF),
         ],
         in_specs=[
-            SMEM, SMEM, part, part,
+            SMEM, SMEM, SMEM, ANY, part, part,
             fixed((width, hidden)), fixed((width, width)), fixed((width, width)),
-            fixed((hidden, width)), fixed((VEC_ROWS, width)), fixed((1, hidden)), fixed((1, VEC_ROWS)),
+            fixed((hidden, width)), fixed((VEC_ROWS, width)),
         ],
         out_specs=[
             part, part, part, wide, wide, part,
-            fixed((width, width)), fixed((VEC_ROWS, width)), fixed((24, width)), fixed((VEC_ROWS, VEC_ROWS)),
+            fixed((width, width)), fixed((VEC_ROWS, width)), fixed((24, width)), fixed((8, 128)), ANY,
         ],
-        scratch_shapes=[pltpu.VMEM((VEC_ROWS, width), F32)],
-        compiler_params=pltpu.CompilerParams(vmem_limit_bytes=60 * 2**20),
+        scratch_shapes=[pltpu.VMEM((VEC_ROWS, width), F32)] + ROW_SEMAPHORES,
+        compiler_params=pltpu.CompilerParams(
+            collective_id=3, has_side_effects=True, vmem_limit_bytes=60 * 2**20
+        ),
         cost_estimate=pl.CostEstimate(flops=11 * 10**9, bytes_accessed=40 * 10**6, transcendentals=3 * 2**20),
         name="dense",
-    )(lens, labels, rows, att, w_inner, w_out, w_pool, w_outer, vectors, b_inner, b_class_row)
+    )(lens, labels, b_class, cot, rows, att, w_inner, w_out, w_pool, w_outer, vectors)
 
 
 def norm_back(grad, values, gain):
@@ -1461,8 +1565,8 @@
 
 
 def dense_back_kernel(
-    lens_ref, cot_ref, summed_ref, pre_ref, dact_ref, w_inner_ref, w_out_ref, w_outer_ref, vec_ref, first_ref,
-    outer_ref, inner_ref, branch_ref, datt_ref, gpre_ref, small_ref, bi_ref,
+    lens_ref, result_ref, cot_ref, summed_ref, pre_ref, dact_ref, w_inner_ref, w_out_ref, w_outer_ref, vec_ref, first_ref,
+    outer_ref, inner_ref, branch_ref, datt_ref, gpre_ref, small_ref, bi_ref, back_ref, row_send, row_recv,
 ):
     step = pl.program_id(0)
     rows = cot_ref.shape[0]
@@ -1474,15 +1578,15 @@
 
     @pl.when(step == 0)
     def _():
+        begin_rows(result_ref, back_ref, row_send, row_recv)
         small_ref[...] = jnp.zeros_like(small_ref)
         bi_ref[...] = jnp.zeros_like(bi_ref)
 
     grad = cot_ref[...].astype(F32)
     places = lax.broadcasted_iota(jnp.int32, (rows, 1), 0) + step * rows
-    ends = doc_ends(lens_ref)
     placed = jnp.zeros(grad.shape, F32)
-    for d in range(len(ends)):
-        placed = jnp.where(places == ends[d] - lens_ref[d], first_ref[d : d + 1, :], placed)
+    for d, start in enumerate(doc_starts(lens_ref)):
+        placed = jnp.where(places == start, first_ref[d : d + 1, :], placed)
     grad = grad + placed
     grad_summed, gain2, shift2 = norm_back(grad, summed_ref[...], vec(GAIN2))
     outer = grad_summed.astype(BF)
@@ -1506,8 +1610,12 @@
     small_ref[4:5, :] += gain1
     small_ref[5:6, :] += shift1
 
-
-def dense_back(lens, cot, summed, pre, dact, w_inner, w_out, w_outer, vectors, first):
+    @pl.when(step == pl.num_programs(0) - 1)
+    def _():
+        end_rows(result_ref, back_ref, row_send, row_recv)
+
+
+def dense_back(lens, result, cot, summed, pre, dact, w_inner, w_out, w_outer, vectors, first):
     length, width = cot.shape
     hidden = w_outer.shape[0]
     tile = 256
@@ -1528,30 +1636,54 @@
             jax.ShapeDtypeStruct((length, width), F32),
             jax.ShapeDtypeStruct((8, width), F32),
             jax.ShapeDtypeStruct((1, hidden), F32),
+            jax.ShapeDtypeStruct(result.shape, BF),
         ],
         in_specs=[
-            SMEM, part, part, part, wide,
+            SMEM, ANY, part, part, part, wide,
             fixed((width, hidden)), fixed((width, width)), fixed((hidden, width)),
             fixed((VEC_ROWS, width)), fixed((VEC_ROWS, width)),
         ],
-        out_specs=[part, wide, part, part, part, fixed((8, width)), fixed((1, hidden))],
-        compiler_params=pltpu.CompilerParams(vmem_limit_bytes=60 * 2**20),
+        out_specs=[part, wide, part, part, part, fixed((8, width)), fixed((1, hidden)), ANY],
+        scratch_shapes=ROW_SEMAPHORES,
+        compiler_params=pltpu.CompilerParams(
+            collective_id=4, has_side_effects=True, vmem_limit_bytes=60 * 2**20
+        ),
         cost_estimate=pl.CostEstimate(flops=11 * 10**9, bytes_accessed=40 * 10**6, transcendentals=0),
         name="dense_back",
-    )(lens, cot, summed, pre, dact, w_inner, w_out, w_outer, vectors, first)
-
-
-def exchange(blocks):
-    count = blocks.shape[0]
-    mine = lax.axis_index("fsdp")
-    held = jnp.zeros_like(blocks)
-    own = lax.dynamic_index_in_dim(blocks, mine, 0, keepdims=True)
-    held = lax.dynamic_update_slice_in_dim(held, own, mine, 0)
-    for k in range(1, count):
-        leaving = lax.dynamic_index_in_dim(blocks, lax.rem(mine + k, count), 0, keepdims=True)
-        came = lax.ppermute(leaving, "fsdp", [(i, (i + k) % count) for i in range(count)])
-        held = lax.dynamic_update_slice_in_dim(held, came, lax.rem(mine - k + count, count), 0)
-    return held
+    )(lens, result, cot, summed, pre, dact, w_inner, w_out, w_outer, vectors, first)
+
+
+def results_kernel(large, small_ref, *refs):
+    sources, refs = refs[:large], refs[large:]
+    targets, columns, inner_ref, class_ref, sem, *held = refs[:large], refs[large : large + VECTORS], *refs[large + VECTORS :]
+    arriving = [pltpu.make_async_copy(s, h, sem.at[0, j]) for j, (s, h) in enumerate(zip(sources, held))]
+    leaving = [pltpu.make_async_copy(h, t, sem.at[1, j]) for j, (h, t) in enumerate(zip(held, targets))]
+    for copy in arriving:
+        copy.start()
+    for j, ref in enumerate(columns):
+        ref[...] = small_ref[B_QUERY + j : B_QUERY + j + 1, 0 : ref.shape[1]]
+    inner_ref[...] = small_ref[TABLE_ROWS : TABLE_ROWS + 1, 0 : inner_ref.shape[1]]
+    class_ref[...] = small_ref[TABLE_ROWS + 1 : TABLE_ROWS + 2, 0 : class_ref.shape[1]]
+    for came, goes in zip(arriving, leaving):
+        came.wait()
+        goes.start()
+    for goes in leaving:
+        goes.wait()
+
+
+def write_results(small, arrays, share, hidden_share):
+    shapes = [jax.ShapeDtypeStruct(a.shape, a.dtype) for a in arrays]
+    vectors = [(1, share)] * VECTORS + [(1, hidden_share), (1, CLASSES)]
+    inside = pl.BlockSpec(memory_space=pltpu.VMEM)
+    return pl.pallas_call(
+        functools.partial(results_kernel, len(arrays)),
+        out_shape=shapes + [jax.ShapeDtypeStruct(v, F32) for v in vectors],
+        in_specs=[inside] + [ANY] * len(arrays),
+        out_specs=[ANY] * len(arrays) + [inside] * len(vectors),
+        scratch_shapes=[pltpu.SemaphoreType.DMA((2, len(arrays)))] + [pltpu.VMEM(a.shape, a.dtype) for a in arrays],
+        compiler_params=pltpu.CompilerParams(vmem_limit_bytes=60 * 2**20),
+        name="results",
+    )(small, *arrays)
 
 
 def fast_body(
@@ -1561,50 +1693,32 @@
     seqs, local_len, width = inputs.shape
     length = seqs * local_len
     devices = 8 * ZS
-    mine = lax.axis_index("fsdp")
     docs = doc_lengths.shape[1]
-    own_lens = lax.dynamic_index_in_dim(doc_lengths, mine, 0, keepdims=False)
-    own_labels = lax.dynamic_index_in_dim(labels, mine, 0, keepdims=False)
-
     share = width // devices
     hidden_share = b_inner.shape[0]
     hidden = hidden_share * devices
-    device = lax.axis_index("dp") * 4 + mine
-    columns = jnp.stack(
-        [
-            *(w_class[:, j] for j in range(CLASSES)), b_query, b_value, b_out, first_gain, first_shift, b_outer, second_gain,
-            second_shift, b_pool,
-        ]
-    )
-    table = lax.dynamic_update_slice(jnp.zeros((12, width), F32), columns, (0, device * share))
-    inner_rows = lax.dynamic_update_slice(jnp.zeros((hidden,), F32), b_inner, (device * hidden_share,)).reshape(4, width)
-    table = jnp.concatenate([table, inner_rows], axis=0).astype(BF).astype(F32)
+    vector_shards = [b_query, b_value, b_out, first_gain, first_shift, b_outer, second_gain, second_shift, b_pool]
     q, k, v, att, lse, w_qkv, vectors, rows, full_inner, full_out, full_pool, full_outer = attend(
-        own_lens, inputs, table, [w_query, w_key, w_value], [w_inner, w_out, w_pool, w_outer]
+        doc_lengths, inputs, w_class.T, [member.reshape(1, share) for member in vector_shards], b_inner.reshape(1, hidden_share),
+        [w_query, w_key, w_value], [w_inner, w_out, w_pool, w_outer],
     )
     rows = rows.reshape(length, width)
     full_inner = full_inner.reshape(width, hidden)
     full_out = full_out.reshape(width, width)
     full_pool = full_pool.reshape(width, width)
     full_outer = full_outer.reshape(hidden, width)
-    b_inner_row = vectors[12:16].reshape(1, hidden)
-    b_class_row = jnp.pad(b_class, (0, VEC_ROWS - CLASSES)).reshape(1, VEC_ROWS)
-
-    cotangent, _ = lax.optimization_barrier((cotangent, att))
-    cot = exchange(cotangent).reshape(length, width)
-    pre, summed, low, act, dact, result, grad_pool, first, small_a, logits = dense(
-        own_lens, own_labels, rows, att, full_inner, full_out, full_pool, full_outer, vectors, b_inner_row, b_class_row
-    )
-    layer_out = exchange(result.reshape(seqs, local_len, width))
-    outer, inner, branch, datt, grad_pre, small_b, grad_b_inner = dense_back(
-        own_lens, cot, summed, pre, dact, full_inner, full_out, full_outer, vectors, first
+    pre, summed, low, act, dact, result, grad_pool, first, small_a, logit_block, cot = dense(
+        doc_lengths, labels, b_class, cotangent, rows, att, full_inner, full_out, full_pool, full_outer, vectors
+    )
+    outer, inner, branch, datt, grad_pre, small_b, grad_b_inner, layer_out = dense_back(
+        doc_lengths, result.reshape(seqs, local_len, width), cot.reshape(length, width), summed, pre, dact, full_inner, full_out,
+        full_outer, vectors, first,
     )
     grad_outer_w = tn(act, outer).astype(BF)
     grad_inner_w = tn(low, inner).astype(BF)
     grad_out_w = tn(att, branch).astype(BF)
-    logit_block = jnp.pad(logits[:docs, :CLASSES], ((0, 8 - docs), (0, 128 - CLASSES)))
-    grad_inputs, all_logits, totals, o_inner, o_outer, o_out, o_pool, o_query, o_key, o_value = attend_back(
-        own_lens, rows, w_qkv, q, k, v, att, datt, lse, grad_pre, small_a, small_b, grad_b_inner, logit_block,
+    grad_inputs, all_logits, small, *sums = attend_back(
+        doc_lengths, rows, w_qkv, q, k, v, att, datt, lse, grad_pre, small_a, small_b, grad_b_inner, logit_block,
         [
             grad_inner_w.reshape(devices, share, hidden),
             grad_outer_w.reshape(devices, hidden_share, width),
@@ -1612,31 +1726,35 @@
             grad_pool.reshape(devices, share, width),
         ],
     )
-    columns = lax.dynamic_slice_in_dim(totals[:12], device * share, share, 1)
-    own_b_inner = lax.dynamic_slice_in_dim(totals[12:16].reshape(hidden), device * hidden_share, hidden_share, 0)
+
+    done = write_results(small, [grad_inputs, layer_out, *sums], share, hidden_share)
+    grad_inputs, layer_out, o_inner, o_outer, o_out, o_pool, o_query, o_key, o_value = done[:9]
+    (
+        o_b_query, o_b_value, o_b_out, o_gain1, o_shift1, o_b_outer, o_gain2, o_shift2, o_b_pool, o_b_inner, o_b_class,
+    ) = (vector.reshape(-1) for vector in done[9:])
     return (
         layer_out,
         all_logits[:, :docs, :CLASSES],
         grad_inputs,
         o_query,
-        columns[B_QUERY],
+        o_b_query,
         o_key,
         o_value,
-        columns[B_VALUE],
+        o_b_value,
         o_out,
-        columns[B_OUT],
-        columns[GAIN1],
-        columns[SHIFT1],
+        o_b_out,
+        o_gain1,
+        o_shift1,
         o_inner,
-        own_b_inner,
+        o_b_inner,
         o_outer,
-        columns[B_OUTER],
-        columns[GAIN2],
-        columns[SHIFT2],
+        o_b_outer,
+        o_gain2,
+        o_shift2,
         o_pool,
-        columns[B_POOL],
-        columns[:CLASSES].T,
-        totals[16, :CLASSES],
+        o_b_pool,
+        small[:CLASSES, :share].T,
+        o_b_class,
     )
 
 

time: 336 us -> 300 us (0.89)
  local copies, waits for them, and re-layouts: 42 us -> 2.72 us
  Pallas kernels: 265 us -> 277 us
  starting transfers between devices: 4.97 us -> 0 us
    unnamed x77 -> x11, local copies, waits for them, and re-layouts: 20.8 us -> 1.46 us
    dynamic_update_slice x8 -> x0, local copies, waits for them, and re-layouts: 6.19 us -> none  [the longest x6 5.16 us: exchange(): lax.dynamic_update_slice_in_dim(held, came, lax.rem(mine - k + count, cou...]
    ppermute x6 -> x0, starting transfers between devices: 4.97 us -> none  [exchange(): lax.ppermute(leaving, 'fsdp', [(i, (i + k) % count) for i in range(count)])]
    pallas_call x0 -> x1, Pallas kernels: none -> 4.8 us  [write_results(): pl.pallas_call(functools.partial(results_kernel, len(arrays)), out_shape=...]
    dynamic_slice x3 -> x0, local copies, waits for them, and re-layouts: 3.39 us -> none  [the longest x2 2.11 us: exchange(): lax.dynamic_index_in_dim(blocks, lax.rem(mine + k, count), 0, keepdims=True)]
  transfers between devices with their start and end apart: 6 -> 0, of which waited for: 0 -> 0; matrix products, arithmetic and copies ran while one was open for 12% -> 0% of each run, Pallas kernels for 49% -> 0%
where the time goes in v4:
time: 300 us; the launch traced here: 299 us
  Pallas kernels  277 us (92%)
  matrix products  18.7 us (6%)
    pallas_call x1, Pallas kernels, attend_back(): pl.pallas_call(functools.partial(attend_back_kernel, groups), grid=(group...  107 us
    pallas_call x1, Pallas kernels, attend(): pl.pallas_call(functools.partial(attend_kernel, groups), grid=(groups,),...  103 us
    pallas_call x1, Pallas kernels, dense(): pl.pallas_call(dense_kernel, grid=(steps,), out_shape=[jax.ShapeDtypeStru...  35.1 us
    pallas_call x1, Pallas kernels, dense_back(): pl.pallas_call(dense_back_kernel, grid=(length // tile,), out_shape=[jax....  27.8 us
    dot_general x3, matrix products, tn(): lax.dot_general(a, b, (((0,), (0,)), ((), ())), preferred_element_type=F32)  18.7 us

profile of v4, /device:TPU:0, one launch (start us, length us, event | category | flops | bytes accessed | tf_op | source)
XLA Modules:
  0.0 299.2 jit_solution(4115317633901402283)
XLA Ops:
  0.7 102.5 %attend.1 = (bf16[1024,768]{1,0:T(8,128)(2,1)}, bf16[1024,768]{1,0:T(8,128)(2,1)}, bf16[1024,768]{1,0:T(8,128)(2,1)}, bf16[1024,768]{1,0:T(8,128)(2,1)}, f32[3,8...) custom-call(s32[4,4]{1,0:T(4,128)} %refs_0_.3, ...), custom_call_target="tpu_custom_call" | custom-call | tf_op jit(solution)/shard_map/attend/pallas_call | solution.py:855
  103.2 35.1 %dense.1 = (f32[1024,768]{1,0:T(8,128)}, f32[1024,768]{1,0:T(8,128)}, bf16[1024,768]{1,0:T(8,128)(2,1)}, bf16[1024,3072]{1,0:T(8,128)(2,1)}, bf16[1024,3072]{1,0...) custom-call(s32[4,4]{1,0:T(4,128)} %refs_0_.3, ...), custom_call_target="tpu_custom_call" | custom-call | flops 11000000512 | bytes 40000000 | tf_op jit(solution)/shard_map/dense/pallas_call | solution.py:1524
  138.4 27.8 %dense_back.1 = (bf16[1024,768]{1,0:T(8,128)(2,1)}, bf16[1024,3072]{1,0:T(8,128)(2,1)}, bf16[1024,768]{1,0:T(8,128)(2,1)}, bf16[1024,768]{1,0:T(8,128)(2,1)}, f3...) custom-call(s32[4,4]{1,0:T(4,128)} %refs_0_.3, ...), custom_call_target="tpu_custom_call" | custom-call | flops 11000000512 | bytes 40000000 | tf_op jit(solution)/shard_map/dense_back/pallas_call | solution.py:1628
  166.2 0.0 copy-start
  166.2 0.0 copy-start.3
  166.2 0.0 copy-start.4
  166.2 9.4 %convolution_convert_fusion = bf16[3072,768]{1,0:T(8,128)(2,1)} fusion(bf16[1024,3072]{1,0:T(8,128)(2,1)} %get-tuple-element.109, bf16[1024,768]{1,0:T(8,128)(2,1)} %get-tuple-element.110), kind=kOutput, calls=%fused_computation | convolution fusion | flops 4834197504 | bytes 12582912 | tf_op jit(solution)/shard_map/dot_general | solution.py:527
  175.6 0.0 copy-done
  175.6 0.0 copy-done.3
  175.6 0.0 copy-start.2
  175.6 2.5 convolution_convert_fusion.2
  178.1 0.0 copy-done.4
  178.1 0.7 copy-done.2
  178.8 6.9 %convolution_convert_fusion.1 = bf16[768,3072]{1,0:T(8,128)(2,1)} fusion(bf16[1024,768]{1,0:T(8,128)(2,1)S(1)} %copy-done.4, bf16[1024,3072]{1,0:T(8,128)(2,1)S(1)} %copy-done.2), kind=kOutput, calls=%fused_computation.1 | convolution fusion | flops 4834197504 | bytes 12582912 | tf_op jit(solution)/shard_map/dot_general | solution.py:527
  185.7 106.7 %attend_back.1 = (bf16[4,256,768]{2,1,0:T(8,128)(2,1)}, f32[4,8,128]{2,1,0:T(8,128)}, f32[32,128]{1,0:T(8,128)}, f32[24,3072]{1,0:T(8,128)}, f32[96,768]{1,0:T(8...) custom-call(s32[4,4]{1,0:T(4,128)} %refs_0_.3, ...), custom_call_target="tpu_custom_call" | custom-call | tf_op jit(solution)/shard_map/attend_back/pallas_call | solution.py:1315
  292.4 1.3 slice_bitcast_fusion
  293.7 0.0 copy-start.1
  293.7 4.8 %results.1 = (bf16[4,256,768]{2,1,0:T(8,128)(2,1)}, bf16[4,256,768]{2,1,0:T(8,128)(2,1)}, f32[24,3072]{1,0:T(8,128)}, f32[96,768]{1,0:T(8,128)}, f32[24,768]{1,0...) custom-call(f32[32,128]{1,0:T(8,128)} %get-tuple-element.113.small_r, ...), custom_call_target="tpu_custom_call" | custom-call | tf_op jit(solution)/shard_map/results/pallas_call | solution.py:1678
  298.5 0.0 copy-done.1
  298.5 0.7 copy.45
  (1 shorter events, 0.0 us)
Async XLA Ops:
  166.2 9.4 %copy-start = (bf16[1024,768]{1,0:T(8,128)(2,1)S(1)}, bf16[1024,768]{1,0:T(8,128)(2,1)}, u32[]{:S(2)}) copy-start(bf16[1024,768]{1,0:T(8,128)(2,1)} %get-tuple-element.88.att_ref.refs_6_) | copy-start | bytes 4718596
  166.2 9.4 %copy-start.3 = (bf16[1024,768]{1,0:T(8,128)(2,1)S(1)}, bf16[1024,768]{1,0:T(8,128)(2,1)}, u32[]{:S(2)}) copy-start(bf16[1024,768]{1,0:T(8,128)(2,1)} %get-tuple-element.111) | copy-start | bytes 4718596
  166.2 11.8 %copy-start.4 = (bf16[1024,768]{1,0:T(8,128)(2,1)S(1)}, bf16[1024,768]{1,0:T(8,128)(2,1)}, u32[]{:S(2)}) copy-start(bf16[1024,768]{1,0:T(8,128)(2,1)} %get-tuple-element.107) | copy-start | bytes 4718596
  175.6 3.2 %copy-start.2 = (bf16[1024,3072]{1,0:T(8,128)(2,1)S(1)}, bf16[1024,3072]{1,0:T(8,128)(2,1)}, u32[]{:S(2)}) copy-start(bf16[1024,3072]{1,0:T(8,128)(2,1)} %get-tuple-element.108) | copy-start | bytes 18874372
  293.7 4.8 %copy-start.1 = (f32[4,8,128]{2,1,0:T(8,128)S(1)}, f32[4,8,128]{2,1,0:T(8,128)}, u32[]{:S(2)}) copy-start(f32[4,8,128]{2,1,0:T(8,128)} %get-tuple-element.124) | copy-start | bytes 49156

commit v5 on v4

--- a/solution.py
+++ b/solution.py
@@ -513,6 +513,7 @@
 ZS = 4
 CLASS_ROWS, B_QUERY, B_VALUE, B_OUT, GAIN1, SHIFT1, B_OUTER, GAIN2, SHIFT2, B_POOL = (0, 3, 4, 5, 6, 7, 8, 9, 10, 11)
 VEC_ROWS = 16
+KB, K0, K1, KF, KS, KZ, KE, KT, KX = range(9)
 
 
 def nn(a, b):
@@ -576,25 +577,97 @@
     return number
 
 
-GATHER_PIECES = (
-    (1, 0, 1, "rows"), (0, 0, 2, "columns"), (0, 1, 2, "columns"), (3, 0, 2, "rows"), (3, 1, 2, "rows"), (2, 0, 1, "rows"),
-)
-GATHER_ORDERS = ("xy", "xy", "xy", "xy", "yx", "xy", "yx", "yx", "xy")
+def gather_tools(plan, orders, view, own_block, keep_sem, send_sem, recv_sem, other=None):
+    z, y, x, c = my_place()
+    everything = slice(None)
+
+    def along(a, axis):
+        return device_at(z, 1 - y, x, c) if orders[a][axis] == "y" else device_at(z, y, 1 - x, c)
+
+    def copy_of(a, number):
+        core = device_at(z, y, x, 1 - c)
+        first_other = (1 - y, x) if orders[a][0] == "y" else (y, 1 - x)
+        if number < 3:
+            source, target = own_block(a), view(a, (z, y, x, c))
+            device = device_at(lax.rem(z + number + 1, ZS), y, x, c)
+        elif number < 6:
+            source = target = view(a, (everything, y, x, c))
+            device = (along(a, 0), along(a, 1), core)[number - 3]
+        elif number < 8:
+            source = target = view(a, (everything, first_other[0], first_other[1], c))
+            device = along(a, 1) if number == 6 else core
+        else:
+            if orders[a][1] == "y":
+                source = target = view(a, (everything, 1 - y, everything, c))
+            else:
+                source = target = view(a, (everything, everything, 1 - x, c))
+            device = core
+        return pltpu.make_async_remote_copy(
+            src_ref=source,
+            dst_ref=target,
+            send_sem=send_sem.at[a, number],
+            recv_sem=recv_sem.at[a, number],
+            device_id=device,
+            device_id_type=MESH,
+        )
+
+    def keep(a):
+        return pltpu.make_async_copy(own_block(a), view(a, (z, y, x, c)), keep_sem.at[a])
+
+    def take_up(point):
+        for kind, a in plan.get(point, ()):
+            if kind == KB:
+                for number in (1, 0, 2):
+                    copy_of(a, number).start()
+                keep(a).start()
+            elif kind == KZ:
+                for number in (0, 1, 2):
+                    copy_of(a, number).wait_recv()
+                keep(a).wait()
+                for number in (3, 4, 5):
+                    copy_of(a, number).start()
+            elif kind == KF:
+                copy_of(a, 3).wait_recv()
+                for number in (6, 7):
+                    copy_of(a, number).start()
+            elif kind == KS:
+                copy_of(a, 4).wait_recv()
+                copy_of(a, 6).wait_recv()
+                copy_of(a, 8).start()
+            elif kind == KT:
+                other(a)
+            else:
+                for number in (5, 7, 8):
+                    copy_of(a, number).wait_recv()
+
+    def all_sent():
+        for a in range(len(orders)):
+            for number in range(9):
+                copy_of(a, number).wait_send()
+
+    return take_up, all_sent
+
+
+GATHER_PIECES = ((1, 0, 1, "rows"), (0, 0, 2, "columns"), (0, 1, 2, "columns"), (2, 0, 2, "rows"), (2, 1, 2, "rows"))
+GATHER_ORDERS = ("xy", "xy", "yx", "xy", "yx", "xy", "yx", "xy")
 GATHER_PLAN = {
-    -1: ("b0", "b1", "b2", "z0", "b3", "z1", "b4", "z2", "z3", "b5", "f0", "z4", "b6", "f1", "s0", "f2", "e0"),
-    0: ("s1", "s2", "f3", "f4", "z5", "b7"),
-    1: ("z6", "e1", "e2"),
-    2: ("b8",),
-    3: ("s3", "z7"),
-    4: ("z8", "e3"),
-    6: ("s4", "f5", "f6"),
-    8: ("f7", "s5", "f8", "e4"),
-    9: ("e5",),
-    10: ("s6", "s8"),
-    11: ("s7", "e8", "e6"),
-    12: ("e7",),
+    -1: (
+        (KB, 0), (KT, 0), (KZ, 0), (KB, 1), (KB, 2), (KT, 1), (KB, 3), (KB, 4), (KB, 5), (KF, 0), (KT, 2), (KS, 0), (KB, 6), (KZ, 1),
+        (KT, 3), (KZ, 2), (KZ, 3), (KE, 0),
+    ),
+    0: ((KB, 7),),
+    1: ((KF, 1), (KF, 2), (KF, 3), (KZ, 4)),
+    3: ((KS, 1), (KS, 2), (KZ, 5), (KS, 3), (KE, 1)),
+    4: ((KZ, 6), (KE, 2), (KE, 3), (KF, 4)),
+    5: ((KF, 5),),
+    7: ((KZ, 7),),
+    8: ((KS, 4), (KF, 6)),
+    9: ((KS, 5), (KE, 4), (KF, 7), (KE, 5)),
+    10: ((KS, 6),),
+    11: ((KS, 7), (KE, 6)),
+    12: ((KE, 7),),
 }
-DENSE_ARRAYS = 4
+DENSE_ARRAYS = 3
 VECTORS = 9
 
 
@@ -678,65 +751,22 @@
         (r0, rows), (c0, columns) = part
         return ref.at[pl.ds(r0, rows), pl.ds(c0, columns)]
 
-    everything = slice(None)
-
-    def along(a, axis):
-        return device_at(z, 1 - y, x, c) if GATHER_ORDERS[a][axis] == "y" else device_at(z, y, 1 - x, c)
-
-    def copy_of(a, number):
-        core = device_at(z, y, x, 1 - c)
-        first_other = (1 - y, x) if GATHER_ORDERS[a][0] == "y" else (y, 1 - x)
-        if number < 3:
-            source, target = own_block(a), view(a, (z, y, x, c))
-            device = device_at(lax.rem(z + number + 1, ZS), y, x, c)
-        elif number < 6:
-            source = target = view(a, (everything, y, x, c))
-            device = (along(a, 0), along(a, 1), core)[number - 3]
-        elif number < 8:
-            source = target = view(a, (everything, first_other[0], first_other[1], c))
-            device = along(a, 1) if number == 6 else core
+    def table_level(level):
+        if level == 0:
+            for k in (0, 1, 2):
+                table_copy(k).wait_recv()
+            tab_ref[1] = (tab_ref[0] + tab_in_ref[0]) + (tab_in_ref[1] + tab_in_ref[2])
         else:
-            if GATHER_ORDERS[a][1] == "y":
-                source = target = view(a, (everything, 1 - y, everything, c))
-            else:
-                source = target = view(a, (everything, everything, 1 - x, c))
-            device = core
-        return pltpu.make_async_remote_copy(
-            src_ref=source,
-            dst_ref=target,
-            send_sem=send_sem.at[a, number],
-            recv_sem=recv_sem.at[a, number],
-            device_id=device,
-            device_id_type=MESH,
-        )
-
-    def keep(a):
-        return pltpu.make_async_copy(own_block(a), view(a, (z, y, x, c)), local_sem.at[2 + a])
-
-    def take_up(point):
-        for word in GATHER_PLAN.get(point, ()):
-            kind, a = word[0], int(word[1:])
-            if kind == "b":
-                for number in (1, 0, 2):
-                    copy_of(a, number).start()
-                keep(a).start()
-            elif kind == "z":
-                for number in (0, 1, 2):
-                    copy_of(a, number).wait_recv()
-                keep(a).wait()
-                for number in (3, 4, 5):
-                    copy_of(a, number).start()
-            elif kind == "f":
-                copy_of(a, 3).wait_recv()
-                for number in (6, 7):
-                    copy_of(a, number).start()
-            elif kind == "s":
-                copy_of(a, 4).wait_recv()
-                copy_of(a, 6).wait_recv()
-                copy_of(a, 8).start()
-            else:
-                for number in (5, 7, 8):
-                    copy_of(a, number).wait_recv()
+            table_copy(level + 2).wait_recv()
+            tab_ref[level + 1] = tab_ref[level] + tab_in_ref[level + 2]
+        if level < 3:
+            table_copy(level + 3).start()
+        else:
+            vec_ref[...] = tab_ref[4]
+
+    take_up, all_sent = gather_tools(
+        GATHER_PLAN, GATHER_ORDERS, view, own_block, local_sem.at[pl.ds(2, items)], send_sem, recv_sem, table_level
+    )
 
     @pl.when(group == 0)
     def _():
@@ -768,14 +798,6 @@
             row_copy(k).start()
         row_own().start()
         take_up(-1)
-        for level in (0, 1, 2):
-            table_copy(level).wait_recv()
-        tab_ref[1] = (tab_ref[0] + tab_in_ref[0]) + (tab_in_ref[1] + tab_in_ref[2])
-        for level in (3, 4, 5):
-            table_copy(level).start()
-            table_copy(level).wait_recv()
-            tab_ref[level - 1] = tab_ref[level - 2] + tab_in_ref[level]
-        vec_ref[...] = tab_ref[4]
         row_own().wait()
         for k in (1, 2, 3):
             row_copy(k).wait_recv()
@@ -827,9 +849,7 @@
     @pl.when(group == groups - 1)
     def _():
         take_up(groups * points)
-        for a in range(items):
-            for number in range(9):
-                copy_of(a, number).wait_send()
+        all_sent()
         for level in range(6):
             table_copy(level).wait_send()
         for k in range(1, 4):
@@ -906,20 +926,20 @@
 )
 GROUP_ORDERS = ("yx", "xy", "yx")
 SCATTER_PLAN = {
-    -1: ("b0",),
-    0: ("b1",),
-    1: ("c00", "c01", "b2", "c10", "c11"),
-    2: ("b3",),
-    3: ("c02", "b4", "c12", "f0", "f1", "c03", "c13", "b5"),
-    4: ("s0", "s1", "b6"),
-    5: ("c04", "c05", "c14", "c15"),
-    6: ("z0", "z1"),
-    7: ("f2", "f3"),
-    8: ("b7",),
-    9: ("c06", "c07", "c16", "c17"),
-    10: ("f4", "s2", "s3"),
-    11: ("f5",),
-    12: ("b8", "dx", "f6", "f7", "t0", "s4", "s5", "z2", "c08", "c18", "z3", "t1", "s7", "s6", "f8", "t2", "z7", "s8", "z4", "z6", "z5", "t3", "z8"),
+    -1: ((KB, 0),),
+    0: ((KB, 1),),
+    1: ((K0, 0), (K0, 1), (KB, 2), (K1, 0), (K1, 1)),
+    2: ((KB, 3),),
+    3: ((K0, 2), (KB, 4), (K1, 2), (KF, 0), (KF, 1), (K0, 3), (K1, 3), (KB, 5)),
+    4: ((KS, 0), (KS, 1), (KB, 6)),
+    5: ((K0, 4), (K0, 5), (K1, 4), (K1, 5)),
+    6: ((KZ, 0), (KZ, 1)),
+    7: ((KF, 2), (KF, 3)),
+    8: ((KB, 7),),
+    9: ((K0, 6), (K0, 7), (K1, 6), (K1, 7)),
+    10: ((KF, 4), (KS, 2), (KS, 3)),
+    11: ((KF, 5),),
+    12: ((KB, 8), (KX, 0), (KF, 6), (KF, 7), (KT, 0), (KS, 4), (KS, 5), (KZ, 2), (K0, 8), (K1, 8), (KZ, 3), (KT, 1), (KS, 7), (KS, 6), (KF, 8), (KT, 2), (KZ, 7), (KS, 8), (KZ, 4), (KZ, 6), (KZ, 5), (KT, 3), (KZ, 8)),
 }
 PIECES = len(DENSE_ITEMS)
 
@@ -1168,19 +1188,18 @@
                 table_copy(nxt).start()
 
     def take_up(point):
-        for word in SCATTER_PLAN.get(point, ()):
-            kind, a = word[:-1], int(word[-1]) if word != "dx" else 0
-            if kind == "b":
+        for kind, a in SCATTER_PLAN.get(point, ()):
+            if kind == KB:
                 begin(a)
-            elif kind == "c0" or kind == "c1":
-                after_core(a, int(kind[1]))
-            elif kind == "f":
+            elif kind == K0 or kind == K1:
+                after_core(a, 0 if kind == K0 else 1)
+            elif kind == KF:
                 after_first(a)
-            elif kind == "s":
+            elif kind == KS:
                 after_second(a)
-            elif kind == "z":
+            elif kind == KZ:
                 finish(a)
-            elif kind == "t":
+            elif kind == KT:
                 table_level(a)
             else:
                 for k in (3, 2, 1):
@@ -1379,22 +1398,6 @@
     return copies, pltpu.make_async_copy(source_ref.at[x * 2 + c], target_ref.at[x * 2 + c], send_sem.at[3])
 
 
-def begin_rows(*refs):
-    z, y, x, c = my_place()
-    meet([device_at(z, y, *group_partner(k, x, c)) for k in range(1, 4)])
-    copies, own = row_copies(*refs)
-    for copy in copies:
-        copy.start()
-    own.start()
-
-
-def end_rows(*refs):
-    copies, own = row_copies(*refs)
-    for copy in copies:
-        copy.wait()
-    own.wait()
-
-
 ROW_SEMAPHORES = [pltpu.SemaphoreType.DMA((4,)), pltpu.SemaphoreType.DMA((3,))]
 
 
@@ -1413,72 +1416,150 @@
     return centered * inverse, inverse
 
 
-def dense_kernel(
-    lens_ref, labels_ref, b_class_ref, cot_ref, x_ref, att_ref, w_inner_ref, w_out_ref, w_pool_ref, w_outer_ref, vec_ref,
-    pre_ref, summed_ref, low_ref, act_ref, dact_ref, lo_ref, dpool_ref, first_ref, small_ref, logits_ref, cot_rows_ref,
-    picked_ref, row_send, row_recv,
-):
+def norm_back(grad, values, gain):
+    hat, inverse = centered_parts(values)
+    scaled = grad * gain
+    mean_scaled = jnp.mean(scaled, axis=-1, keepdims=True)
+    mean_cross = jnp.mean(scaled * hat, axis=-1, keepdims=True)
+    back = (scaled - mean_scaled - hat * mean_cross) * inverse
+    return back, jnp.sum(grad * hat, axis=0, keepdims=True), jnp.sum(grad, axis=0, keepdims=True)
+
+
+MIDDLE_ORDERS = ("xy",)
+MIDDLE_PLAN = {
+    0: ((KB, 0),),
+    2: ((KZ, 0),),
+    5: ((KF, 0),),
+    8: ((KS, 0),),
+    14: ((KE, 0),),
+}
+COTANGENT_POINT = 3
+
+
+def middle_kernel(tiles, *refs):
+    (
+        lens_ref, labels_ref, b_class_ref, cot_ref, x_ref, att_ref, w_inner_ref, w_out_ref, outer_hbm_ref, pool_shard_ref,
+        vec_ref,
+    ) = refs[:11]
+    (
+        low_ref, act_out_ref, outer_ref, inner_ref, branch_ref, datt_ref, gpre_ref, dpool_ref, small_a_ref, small_b_ref, bi_ref,
+        logits_ref, layer_out_ref,
+    ) = refs[11:24]
+    (
+        act_ref, dact_ref, pre_ref, summed_ref, result_ref, cot_rows_ref, first_ref, picked_ref, own_pool, w_outer_ref, pool_ref,
+        outer_sem, act_sem, keep_sem, send_sem, recv_sem, cot_send, cot_recv, lo_send, lo_recv,
+    ) = refs[24:]
     step = pl.program_id(0)
+    rows, full = x_ref.shape
+    chunks = act_ref.shape[1] // full
+
+    def view(a, where):
+        return pool_ref.at[where]
+
+    def own_block(a):
+        return own_pool
+
+    gather_up, all_sent = gather_tools(MIDDLE_PLAN, MIDDLE_ORDERS, view, own_block, keep_sem, send_sem, recv_sem)
+
+    def take_up(point):
+        if point in MIDDLE_PLAN or point == COTANGENT_POINT:
+
+            @pl.when(step == point // 2)
+            def _():
+                gather_up(point)
+                if point == COTANGENT_POINT:
+                    copies, own = row_copies(cot_ref, cot_rows_ref, cot_send, cot_recv)
+                    for copy in copies:
+                        copy.start()
+                    own.start()
+
+    def outer_copy():
+        return pltpu.make_async_copy(outer_hbm_ref, w_outer_ref, outer_sem.at[0])
+
+    def act_copy(tile):
+        where = pl.ds(tile * rows, rows)
+        return pltpu.make_async_copy(act_ref.at[where], act_out_ref.at[where], act_sem.at[tile])
+
+    def vec(row):
+        return vec_ref[row : row + 1, :]
 
     @pl.when(step == 0)
     def _():
-        begin_rows(cot_ref, cot_rows_ref, row_send, row_recv)
-
-    rows = x_ref.shape[0]
-    hidden = w_inner_ref.shape[1]
-    chunk = 512
-
-    def vec(row):
-        return vec_ref[row : row + 1, :]
-
-    full = vec_ref.shape[1]
-
-    def bias_at(s):
-        pieces, stop = [], s + chunk
-        while s < stop:
-            row, at = s // full, s % full
-            size = min(stop - s, full - at)
-            pieces.append(vec_ref[12 + row : 13 + row, at : at + size])
-            s += size
-        return pieces[0] if len(pieces) == 1 else jnp.concatenate(pieces, axis=1)
-
-    pre = x_ref[...].astype(F32) + (nn(att_ref[...], w_out_ref[...]) + vec(B_OUT))
-    pre_ref[...] = pre
-    normed = centered_parts(pre)[0] * vec(GAIN1) + vec(SHIFT1)
-    low = normed.astype(BF)
-    low_ref[...] = low
-    total = normed + vec(B_OUTER)
-    for s in range(0, hidden, chunk):
-        inner = nn(low, w_inner_ref[:, s : s + chunk]) + bias_at(s)
-        phi, bell = normal_parts(inner)
-        activated = (inner * phi).astype(BF)
-        act_ref[:, s : s + chunk] = activated
-        dact_ref[:, s : s + chunk] = (phi + inner * bell * 0.3989422804014327).astype(BF)
-        total = total + nn(activated, w_outer_ref[s : s + chunk, :])
-    summed_ref[...] = total
-    result = (centered_parts(total)[0] * vec(GAIN2) + vec(SHIFT2)).astype(BF)
-    lo_ref[...] = result
-    starts = doc_starts(lens_ref)
-    docs = len(starts)
-    places = lax.broadcasted_iota(jnp.int32, (VEC_ROWS, rows), 1) + step * rows
-    row_doc = lax.broadcasted_iota(jnp.int32, (VEC_ROWS, rows), 0)
-    hit = jnp.zeros((VEC_ROWS, rows), jnp.bool_)
-    for d in range(docs):
-        hit = hit | ((row_doc == d) & (places == starts[d]))
-    found = nn(jnp.where(hit, 1.0, 0.0).astype(BF), result)
-
-    @pl.when(step == 0)
+        outer_copy().start()
+        own_pool[...] = pool_shard_ref[...].astype(BF)
+        z, y, x, c = my_place()
+        meet(all_partners(z, y, x, c))
+
+    tile = lax.rem(step, tiles)
+    here = pl.ds(pl.multiple_of(tile * rows, rows), rows)
+    for point in range(0, 2 * tiles, 2):
+        take_up(point)
+
+    @pl.when(step < tiles)
     def _():
-        picked_ref[...] = found
-
-    @pl.when(step > 0)
+        pre = x_ref[...].astype(F32) + (nn(att_ref[...], w_out_ref[...]) + vec(B_OUT))
+        pre_ref[here, :] = pre
+        low = (centered_parts(pre)[0] * vec(GAIN1) + vec(SHIFT1)).astype(BF)
+        low_ref[...] = low
+        for j in range(chunks):
+            if j == chunks // 2:
+                for point in range(1, 2 * tiles, 2):
+                    take_up(point)
+            s = j * full
+            hidden = nn(low, w_inner_ref[:, s : s + full]) + vec(12 + j)
+            phi, bell = normal_parts(hidden)
+            act_ref[here, s : s + full] = (hidden * phi).astype(BF)
+            dact_ref[here, s : s + full] = (phi + hidden * bell * 0.3989422804014327).astype(BF)
+        for t in range(tiles):
+
+            @pl.when(step == t)
+            def _(t=t):
+                act_copy(t).start()
+
+    for point in range(2 * tiles, 4 * tiles, 2):
+        take_up(point)
+
+    def outer_part(j):
+        return w_outer_ref[j].reshape(full, full)
+
+    @pl.when(step == tiles)
     def _():
-        picked_ref[...] += found
-
-    @pl.when(step == pl.num_programs(0) - 1)
+        outer_copy().wait()
+
+    @pl.when((step >= tiles) & (step < 2 * tiles))
     def _():
+        total = centered_parts(pre_ref[here, :])[0] * vec(GAIN1) + vec(SHIFT1) + vec(B_OUTER)
+        for j in range(chunks):
+            total = total + nn(act_ref[here, j * full : (j + 1) * full], outer_part(j))
+        summed_ref[here, :] = total
+        result = (centered_parts(total)[0] * vec(GAIN2) + vec(SHIFT2)).astype(BF)
+        result_ref[tile] = result
+        starts = doc_starts(lens_ref)
+        places = lax.broadcasted_iota(jnp.int32, (VEC_ROWS, rows), 1) + tile * rows
+        row_doc = lax.broadcasted_iota(jnp.int32, (VEC_ROWS, rows), 0)
+        hit = jnp.zeros((VEC_ROWS, rows), jnp.bool_)
+        for d, start in enumerate(starts):
+            hit = hit | ((row_doc == d) & (places == start))
+        found = nn(jnp.where(hit, 1.0, 0.0).astype(BF), result)
+
+        @pl.when(tile == 0)
+        def _():
+            picked_ref[...] = found
+
+        @pl.when(tile > 0)
+        def _():
+            picked_ref[...] += found
+
+    @pl.when(step == 2 * tiles - 1)
+    def _():
+        copies, own = row_copies(result_ref, layer_out_ref, lo_send, lo_recv)
+        for copy in copies:
+            copy.start()
+        own.start()
+        w_pool = pool_ref[...].astype(F32).reshape(full, full).astype(BF)
+        docs = lens_ref.shape[1]
         picked = picked_ref[...].astype(BF)
-        pooled = jnp.tanh(nn(picked, w_pool_ref[...]) + vec(B_POOL))
+        pooled = jnp.tanh(nn(picked, w_pool) + vec(B_POOL))
         pooled_low = pooled.astype(BF)
         table = vec_ref[...].astype(BF)
         column = lax.broadcasted_iota(jnp.int32, (VEC_ROWS, VEC_ROWS), 1)
@@ -1499,158 +1580,124 @@
         grad_low = grad.astype(BF)
         grad_pool = (nn(grad_low, table) * (1.0 - pooled * pooled)).astype(BF)
         dpool_ref[...] = tn(picked, grad_pool).astype(BF)
-        first_ref[...] = nt(grad_pool, w_pool_ref[...])
-        small_ref[0:16, :] = tn(grad_low, pooled_low)
-        small_ref[16:17, :] = jnp.sum(grad_pool.astype(F32), axis=0, keepdims=True)
-        width = small_ref.shape[1]
+        first_ref[...] = nt(grad_pool, w_pool)
+        small_a_ref[0:16, :] = tn(grad_low, pooled_low)
+        small_a_ref[16:17, :] = jnp.sum(grad_pool.astype(F32), axis=0, keepdims=True)
         class_sum = jnp.sum(grad_low.astype(F32), axis=0, keepdims=True)
-        small_ref[17:18, :] = jnp.concatenate(
-            [class_sum, jnp.zeros((1, width - VEC_ROWS), F32)], axis=1
-        )
-        end_rows(cot_ref, cot_rows_ref, row_send, row_recv)
-
-
-def dense(lens, labels, b_class, cot, rows, att, w_inner, w_out, w_pool, w_outer, vectors):
+        small_a_ref[17:18, :] = jnp.concatenate([class_sum, jnp.zeros((1, full - VEC_ROWS), F32)], axis=1)
+        small_b_ref[...] = jnp.zeros_like(small_b_ref)
+        bi_ref[...] = jnp.zeros_like(bi_ref)
+        copies, own = row_copies(cot_ref, cot_rows_ref, cot_send, cot_recv)
+        for copy in copies:
+            copy.wait()
+        own.wait()
+
+    @pl.when(step >= 2 * tiles)
+    def _():
+        grad = cot_rows_ref[tile].astype(F32)
+        places = lax.broadcasted_iota(jnp.int32, (rows, 1), 0) + tile * rows
+        placed = jnp.zeros(grad.shape, F32)
+        for d, start in enumerate(doc_starts(lens_ref)):
+            placed = jnp.where(places == start, first_ref[d : d + 1, :], placed)
+        grad = grad + placed
+        grad_summed, gain2, shift2 = norm_back(grad, summed_ref[here, :], vec(GAIN2))
+        outer = grad_summed.astype(BF)
+        outer_ref[...] = outer
+        grad_normed = grad_summed
+        for j in range(chunks):
+            s = j * full
+            back = nt(outer, outer_part(j))
+            inner = (back * dact_ref[here, s : s + full].astype(F32)).astype(BF)
+            inner_ref[:, s : s + full] = inner
+            bi_ref[:, s : s + full] += jnp.sum(inner.astype(F32), axis=0, keepdims=True)
+            grad_normed = grad_normed + nt(inner, w_inner_ref[:, s : s + full])
+        grad_pre, gain1, shift1 = norm_back(grad_normed, pre_ref[here, :], vec(GAIN1))
+        gpre_ref[...] = grad_pre
+        branch = grad_pre.astype(BF)
+        branch_ref[...] = branch
+        datt_ref[...] = nt(branch, w_out_ref[...]).astype(BF)
+        small_b_ref[0:1, :] += jnp.sum(outer.astype(F32), axis=0, keepdims=True)
+        small_b_ref[1:2, :] += gain2
+        small_b_ref[2:3, :] += shift2
+        small_b_ref[3:4, :] += jnp.sum(branch.astype(F32), axis=0, keepdims=True)
+        small_b_ref[4:5, :] += gain1
+        small_b_ref[5:6, :] += shift1
+
+    @pl.when(step == 3 * tiles - 1)
+    def _():
+        all_sent()
+        for t in range(tiles):
+            act_copy(t).wait()
+        copies, own = row_copies(result_ref, layer_out_ref, lo_send, lo_recv)
+        for copy in copies:
+            copy.wait()
+        own.wait()
+
+
+def middle(lens, labels, b_class, cot, rows, att, w_inner, w_out, w_outer, pool_shard, vectors):
     length, width = rows.shape
-    hidden = w_outer.shape[0]
+    hidden = w_inner.shape[1]
     tile = 256
-    steps = length // tile
-    part = pl.BlockSpec((tile, width), lambda i: (i, 0))
-    wide = pl.BlockSpec((tile, hidden), lambda i: (i, 0))
-
-    def fixed(shape, column=0):
-        return pl.BlockSpec(shape, lambda i: (0, column))
-
+    tiles = length // tile
+    items = len(MIDDLE_ORDERS)
+    once = pl.Buffered(buffer_count=1)
+    early = pl.BlockSpec((tile, width), lambda i: (jnp.minimum(i, tiles - 1), 0))
+
+    def late(size):
+        return pl.BlockSpec((tile, size), lambda i: (jnp.maximum(i - 2 * tiles, 0), 0))
+
+    def fixed(shape):
+        return pl.BlockSpec(shape, lambda i: (0,) * len(shape), pipeline_mode=once)
+
+    lead = (ZS, 2, 2, 2)
     return pl.pallas_call(
-        dense_kernel,
-        grid=(steps,),
+        functools.partial(middle_kernel, tiles),
+        grid=(3 * tiles,),
         out_shape=[
-            jax.ShapeDtypeStruct((length, width), F32),
-            jax.ShapeDtypeStruct((length, width), F32),
             jax.ShapeDtypeStruct((length, width), BF),
             jax.ShapeDtypeStruct((length, hidden), BF),
-            jax.ShapeDtypeStruct((length, hidden), BF),
-            jax.ShapeDtypeStruct((length, width), BF),
-            jax.ShapeDtypeStruct((width, width), BF),
-            jax.ShapeDtypeStruct((VEC_ROWS, width), F32),
-            jax.ShapeDtypeStruct((24, width), F32),
-            jax.ShapeDtypeStruct((8, 128), F32),
-            jax.ShapeDtypeStruct(cot.shape, BF),
-        ],
-        in_specs=[
-            SMEM, SMEM, SMEM, ANY, part, part,
-            fixed((width, hidden)), fixed((width, width)), fixed((width, width)),
-            fixed((hidden, width)), fixed((VEC_ROWS, width)),
-        ],
-        out_specs=[
-            part, part, part, wide, wide, part,
-            fixed((width, width)), fixed((VEC_ROWS, width)), fixed((24, width)), fixed((8, 128)), ANY,
-        ],
-        scratch_shapes=[pltpu.VMEM((VEC_ROWS, width), F32)] + ROW_SEMAPHORES,
-        compiler_params=pltpu.CompilerParams(
-            collective_id=3, has_side_effects=True, vmem_limit_bytes=60 * 2**20
-        ),
-        cost_estimate=pl.CostEstimate(flops=11 * 10**9, bytes_accessed=40 * 10**6, transcendentals=3 * 2**20),
-        name="dense",
-    )(lens, labels, b_class, cot, rows, att, w_inner, w_out, w_pool, w_outer, vectors)
-
-
-def norm_back(grad, values, gain):
-    hat, inverse = centered_parts(values)
-    scaled = grad * gain
-    mean_scaled = jnp.mean(scaled, axis=-1, keepdims=True)
-    mean_cross = jnp.mean(scaled * hat, axis=-1, keepdims=True)
-    back = (scaled - mean_scaled - hat * mean_cross) * inverse
-    return back, jnp.sum(grad * hat, axis=0, keepdims=True), jnp.sum(grad, axis=0, keepdims=True)
-
-
-def dense_back_kernel(
-    lens_ref, result_ref, cot_ref, summed_ref, pre_ref, dact_ref, w_inner_ref, w_out_ref, w_outer_ref, vec_ref, first_ref,
-    outer_ref, inner_ref, branch_ref, datt_ref, gpre_ref, small_ref, bi_ref, back_ref, row_send, row_recv,
-):
-    step = pl.program_id(0)
-    rows = cot_ref.shape[0]
-    hidden = dact_ref.shape[1]
-    chunk = 512
-
-    def vec(row):
-        return vec_ref[row : row + 1, :]
-
-    @pl.when(step == 0)
-    def _():
-        begin_rows(result_ref, back_ref, row_send, row_recv)
-        small_ref[...] = jnp.zeros_like(small_ref)
-        bi_ref[...] = jnp.zeros_like(bi_ref)
-
-    grad = cot_ref[...].astype(F32)
-    places = lax.broadcasted_iota(jnp.int32, (rows, 1), 0) + step * rows
-    placed = jnp.zeros(grad.shape, F32)
-    for d, start in enumerate(doc_starts(lens_ref)):
-        placed = jnp.where(places == start, first_ref[d : d + 1, :], placed)
-    grad = grad + placed
-    grad_summed, gain2, shift2 = norm_back(grad, summed_ref[...], vec(GAIN2))
-    outer = grad_summed.astype(BF)
-    outer_ref[...] = outer
-    grad_normed = grad_summed
-    for s in range(0, hidden, chunk):
-        back = nt(outer, w_outer_ref[s : s + chunk, :])
-        inner = (back * dact_ref[:, s : s + chunk].astype(F32)).astype(BF)
-        inner_ref[:, s : s + chunk] = inner
-        bi_ref[:, s : s + chunk] += jnp.sum(inner.astype(F32), axis=0, keepdims=True)
-        grad_normed = grad_normed + nt(inner, w_inner_ref[:, s : s + chunk])
-    grad_pre, gain1, shift1 = norm_back(grad_normed, pre_ref[...], vec(GAIN1))
-    gpre_ref[...] = grad_pre
-    branch = grad_pre.astype(BF)
-    branch_ref[...] = branch
-    datt_ref[...] = nt(branch, w_out_ref[...]).astype(BF)
-    small_ref[0:1, :] += jnp.sum(outer.astype(F32), axis=0, keepdims=True)
-    small_ref[1:2, :] += gain2
-    small_ref[2:3, :] += shift2
-    small_ref[3:4, :] += jnp.sum(branch.astype(F32), axis=0, keepdims=True)
-    small_ref[4:5, :] += gain1
-    small_ref[5:6, :] += shift1
-
-    @pl.when(step == pl.num_programs(0) - 1)
-    def _():
-        end_rows(result_ref, back_ref, row_send, row_recv)
-
-
-def dense_back(lens, result, cot, summed, pre, dact, w_inner, w_out, w_outer, vectors, first):
-    length, width = cot.shape
-    hidden = w_outer.shape[0]
-    tile = 256
-    part = pl.BlockSpec((tile, width), lambda i: (i, 0))
-    wide = pl.BlockSpec((tile, hidden), lambda i: (i, 0))
-
-    def fixed(shape, column=0):
-        return pl.BlockSpec(shape, lambda i: (0, column))
-
-    return pl.pallas_call(
-        dense_back_kernel,
-        grid=(length // tile,),
-        out_shape=[
             jax.ShapeDtypeStruct((length, width), BF),
             jax.ShapeDtypeStruct((length, hidden), BF),
             jax.ShapeDtypeStruct((length, width), BF),
             jax.ShapeDtypeStruct((length, width), BF),
             jax.ShapeDtypeStruct((length, width), F32),
+            jax.ShapeDtypeStruct((width, width), BF),
+            jax.ShapeDtypeStruct((24, width), F32),
             jax.ShapeDtypeStruct((8, width), F32),
             jax.ShapeDtypeStruct((1, hidden), F32),
-            jax.ShapeDtypeStruct(result.shape, BF),
+            jax.ShapeDtypeStruct((8, 128), F32),
+            jax.ShapeDtypeStruct(cot.shape, BF),
         ],
         in_specs=[
-            SMEM, ANY, part, part, part, wide,
-            fixed((width, hidden)), fixed((width, width)), fixed((hidden, width)),
-            fixed((VEC_ROWS, width)), fixed((VEC_ROWS, width)),
+            SMEM, SMEM, SMEM, ANY, early, early, fixed((width, hidden)), fixed((width, width)), ANY,
+            fixed(pool_shard.shape), fixed((VEC_ROWS, width)),
         ],
-        out_specs=[part, wide, part, part, part, fixed((8, width)), fixed((1, hidden)), ANY],
-        scratch_shapes=ROW_SEMAPHORES,
-        compiler_params=pltpu.CompilerParams(
-            collective_id=4, has_side_effects=True, vmem_limit_bytes=60 * 2**20
-        ),
-        cost_estimate=pl.CostEstimate(flops=11 * 10**9, bytes_accessed=40 * 10**6, transcendentals=0),
-        name="dense_back",
-    )(lens, result, cot, summed, pre, dact, w_inner, w_out, w_outer, vectors, first)
+        out_specs=[
+            early, ANY, late(width), late(hidden), late(width), late(width), late(width), fixed((width, width)),
+            fixed((24, width)), fixed((8, width)), fixed((1, hidden)), fixed((8, 128)), ANY,
+        ],
+        scratch_shapes=[
+            pltpu.VMEM((length, hidden), BF),
+            pltpu.VMEM((length, hidden), BF),
+            pltpu.VMEM((length, width), F32),
+            pltpu.VMEM((length, width), F32),
+            pltpu.VMEM(cot.shape, BF),
+            pltpu.VMEM(cot.shape, BF),
+            pltpu.VMEM((VEC_ROWS, width), F32),
+            pltpu.VMEM((VEC_ROWS, width), F32),
+            pltpu.VMEM(pool_shard.shape, BF),
+            pltpu.VMEM(w_outer.shape, BF),
+            pltpu.VMEM(lead + pool_shard.shape, BF),
+            pltpu.SemaphoreType.DMA((1,)),
+            pltpu.SemaphoreType.DMA((tiles,)),
+            pltpu.SemaphoreType.DMA((items,)),
+            pltpu.SemaphoreType.DMA((items, 9)),
+            pltpu.SemaphoreType.DMA((items, 9)),
+        ]
+        + ROW_SEMAPHORES * 2,
+        compiler_params=pltpu.CompilerParams(collective_id=3, has_side_effects=True, vmem_limit_bytes=60 * 2**20),
+        name="middle",
+    )(lens, labels, b_class, cot, rows, att, w_inner, w_out, w_outer, pool_shard, vectors)
 
 
 def results_kernel(large, small_ref, *refs):
@@ -1698,21 +1745,15 @@
     hidden_share = b_inner.shape[0]
     hidden = hidden_share * devices
     vector_shards = [b_query, b_value, b_out, first_gain, first_shift, b_outer, second_gain, second_shift, b_pool]
-    q, k, v, att, lse, w_qkv, vectors, rows, full_inner, full_out, full_pool, full_outer = attend(
+    q, k, v, att, lse, w_qkv, vectors, rows, full_inner, full_out, full_outer = attend(
         doc_lengths, inputs, w_class.T, [member.reshape(1, share) for member in vector_shards], b_inner.reshape(1, hidden_share),
-        [w_query, w_key, w_value], [w_inner, w_out, w_pool, w_outer],
+        [w_query, w_key, w_value], [w_inner, w_out, w_outer],
     )
     rows = rows.reshape(length, width)
     full_inner = full_inner.reshape(width, hidden)
     full_out = full_out.reshape(width, width)
-    full_pool = full_pool.reshape(width, width)
-    full_outer = full_outer.reshape(hidden, width)
-    pre, summed, low, act, dact, result, grad_pool, first, small_a, logit_block, cot = dense(
-        doc_lengths, labels, b_class, cotangent, rows, att, full_inner, full_out, full_pool, full_outer, vectors
-    )
-    outer, inner, branch, datt, grad_pre, small_b, grad_b_inner, layer_out = dense_back(
-        doc_lengths, result.reshape(seqs, local_len, width), cot.reshape(length, width), summed, pre, dact, full_inner, full_out,
-        full_outer, vectors, first,
+    low, act, outer, inner, branch, datt, grad_pre, grad_pool, small_a, small_b, grad_b_inner, logit_block, layer_out = middle(
+        doc_lengths, labels, b_class, cotangent, rows, att, full_inner, full_out, full_outer, w_pool, vectors
     )
     grad_outer_w = tn(act, outer).astype(BF)
     grad_inner_w = tn(low, inner).astype(BF)

time: 300 us -> 284 us (0.947)
  Pallas kernels: 277 us -> 260 us
    pallas_call x2 -> x1, Pallas kernels: 63 us -> 54.7 us  [middle(): pl.pallas_call(functools.partial(middle_kernel, tiles), grid=(3 * tiles,)...]
    pallas_call x1, Pallas kernels: 103 us -> 94.7 us  [attend(): pl.pallas_call(functools.partial(attend_kernel, groups), grid=(groups,),...]
where the time goes in v5:
time: 284 us
  Pallas kernels  260 us (92%)
  matrix products  20.8 us (7%)
    pallas_call x1, Pallas kernels, attend_back(): pl.pallas_call(functools.partial(attend_back_kernel, groups), grid=(group...  106 us
    pallas_call x1, Pallas kernels, attend(): pl.pallas_call(functools.partial(attend_kernel, groups), grid=(groups,),...  94.7 us
    pallas_call x1, Pallas kernels, middle(): pl.pallas_call(functools.partial(middle_kernel, tiles), grid=(3 * tiles,)...  54.7 us
    dot_general x3, matrix products, tn(): lax.dot_general(a, b, (((0,), (0,)), ((), ())), preferred_element_type=F32)  20.8 us

profile of v5, /device:TPU:0, one launch (start us, length us, event | category | flops | bytes accessed | tf_op | source)
XLA Modules:
  0.0 283.6 jit_solution(16269304410019639634)
XLA Ops:
  0.7 94.7 %attend.1 = (bf16[1024,768]{1,0:T(8,128)(2,1)}, bf16[1024,768]{1,0:T(8,128)(2,1)}, bf16[1024,768]{1,0:T(8,128)(2,1)}, bf16[1024,768]{1,0:T(8,128)(2,1)}, f32[3,8...) custom-call(s32[4,4]{1,0:T(4,128)} %refs_0_.5, ...), custom_call_target="tpu_custom_call" | custom-call | tf_op jit(solution)/shard_map/attend/pallas_call | solution.py:875
  95.3 0.0 copy-start
  95.3 54.7 %middle.1 = (bf16[1024,768]{1,0:T(8,128)(2,1)}, bf16[1024,3072]{1,0:T(8,128)(2,1)}, bf16[1024,768]{1,0:T(8,128)(2,1)}, bf16[1024,3072]{1,0:T(8,128)(2,1)}, bf16[...) custom-call(s32[4,4]{1,0:T(4,128)} %refs_0_.5, ...), custom_call_target="tpu_custom_call" | custom-call | tf_op jit(solution)/shard_map/middle/pallas_call | solution.py:1653
  150.1 0.0 copy-done
  150.1 0.0 copy-start.3
  150.1 0.0 slice-start
  150.1 4.0 %convolution_convert_fusion.2 = bf16[768,768]{1,0:T(8,128)(2,1)} fusion(bf16[1024,768]{1,0:T(8,128)(2,1)S(1)} %copy-done, bf16[1024,768]{1,0:T(8,128)(2,1)} %get-tuple-element.97), kind=kOutput, calls=%fused_computation.2 | convolution fusion | flops 1208549376 | bytes 4325376 | tf_op jit(solution)/shard_map/dot_general | solution.py:528
  154.1 0.0 copy-done.3
  154.1 0.0 slice-start.1
  154.1 0.0 copy-start.2
  154.1 9.9 %convolution_convert_fusion.1 = bf16[768,3072]{1,0:T(8,128)(2,1)} fusion(bf16[1024,768]{1,0:T(8,128)(2,1)S(1)} %copy-done.3, bf16[1024,3072]{1,0:T(8,128)(2,1)} %get-tuple-element.94), kind=kOutput, calls=%fused_computation.1 | convolution fusion | flops 4834197504 | bytes 12582912 | tf_op jit(solution)/shard_map/dot_general | solution.py:528
  164.0 0.0 slice-done
  164.0 0.0 slice-done.1
  164.0 0.0 copy-done.2
  164.0 6.9 %convolution_convert_fusion = bf16[3072,768]{1,0:T(8,128)(2,1)} fusion(bf16[1024,3072]{1,0:T(8,128)(2,1)S(1)} %bitcast.57, bf16[1024,768]{1,0:T(8,128)(2,1)S(1)} %copy-done.2), kind=kOutput, calls=%fused_computation | convolution fusion | flops 4834197504 | bytes 12582912 | tf_op jit(solution)/shard_map/dot_general | solution.py:528
  170.9 105.8 %attend_back.1 = (bf16[4,256,768]{2,1,0:T(8,128)(2,1)}, f32[4,8,128]{2,1,0:T(8,128)}, f32[32,128]{1,0:T(8,128)}, f32[24,3072]{1,0:T(8,128)}, f32[96,768]{1,0:T(8...) custom-call(s32[4,4]{1,0:T(4,128)} %refs_0_.5, ...), custom_call_target="tpu_custom_call" | custom-call | tf_op jit(solution)/shard_map/attend_back/pallas_call | solution.py:1334
  276.8 1.3 slice_bitcast_fusion
  278.0 0.0 copy-start.1
  278.0 4.8 %results.1 = (bf16[4,256,768]{2,1,0:T(8,128)(2,1)}, bf16[4,256,768]{2,1,0:T(8,128)(2,1)}, f32[24,3072]{1,0:T(8,128)}, f32[96,768]{1,0:T(8,128)}, f32[24,768]{1,0...) custom-call(f32[32,128]{1,0:T(8,128)} %get-tuple-element.99.small_re, ...), custom_call_target="tpu_custom_call" | custom-call | tf_op jit(solution)/shard_map/results/pallas_call | solution.py:1725
  282.8 0.0 copy-done.1
  282.9 0.7 copy.45
  (2 shorter events, 0.0 us)
Async XLA Ops:
  95.3 54.7 %copy-start = (bf16[1024,768]{1,0:T(8,128)(2,1)S(1)}, bf16[1024,768]{1,0:T(8,128)(2,1)}, u32[]{:S(2)}) copy-start(bf16[1024,768]{1,0:T(8,128)(2,1)} %get-tuple-element.81.refs_5_.refs_6_) | copy-start | bytes 4718596
  150.1 4.0 %copy-start.3 = (bf16[1024,768]{1,0:T(8,128)(2,1)S(1)}, bf16[1024,768]{1,0:T(8,128)(2,1)}, u32[]{:S(2)}) copy-start(bf16[1024,768]{1,0:T(8,128)(2,1)} %get-tuple-element.93) | copy-start | bytes 4718596
  150.1 13.9 %slice-start = ((s8[6291456]{0:T(1024)(128)(4,1)}), s8[4194304]{0:T(1024)(128)(4,1)S(1)}, s32[]{:S(2)}) async-start(s8[6291456]{0:T(1024)(128)(4,1)} %bitcast.56), calls=%async_computation | async-start | bytes 8388608
  154.1 9.9 %slice-start.1 = ((s8[6291456]{0:T(1024)(128)(4,1)}), s8[2097152]{0:T(1024)(128)(4,1)S(1)}, s32[]{:S(2)}) async-start(s8[6291456]{0:T(1024)(128)(4,1)} %bitcast.56), calls=%async_computation.1 | async-start | bytes 4194304
  154.1 9.9 %copy-start.2 = (bf16[1024,768]{1,0:T(8,128)(2,1)S(1)}, bf16[1024,768]{1,0:T(8,128)(2,1)}, u32[]{:S(2)}) copy-start(bf16[1024,768]{1,0:T(8,128)(2,1)} %get-tuple-element.96) | copy-start | bytes 4718596
  278.0 4.8 %copy-start.1 = (f32[4,8,128]{2,1,0:T(8,128)S(1)}, f32[4,8,128]{2,1,0:T(8,128)}, u32[]{:S(2)}) copy-start(f32[4,8,128]{2,1,0:T(8,128)} %get-tuple-element.110) | copy-start | bytes 49156

commit v6 on v5

--- a/solution.py
+++ b/solution.py
@@ -513,7 +513,7 @@
 ZS = 4
 CLASS_ROWS, B_QUERY, B_VALUE, B_OUT, GAIN1, SHIFT1, B_OUTER, GAIN2, SHIFT2, B_POOL = (0, 3, 4, 5, 6, 7, 8, 9, 10, 11)
 VEC_ROWS = 16
-KB, K0, K1, KF, KS, KZ, KE, KT, KX = range(9)
+KB, K0, K1, KF, KS, KZ, KE, KT = range(8)
 
 
 def nn(a, b):
@@ -679,6 +679,18 @@
     return (0, rows), (which * (columns // count), columns // count)
 
 
+def key_marks(length, ends):
+    number = doc_numbers(lax.broadcasted_iota(jnp.int32, (length, 1), 0), ends)
+    lane = lax.broadcasted_iota(jnp.int32, (length, 128), 1)
+    return jnp.where(lane == number, 1.0, 0.0).astype(BF)
+
+
+def query_marks(at, count, ends):
+    number = doc_numbers(lax.broadcasted_iota(jnp.int32, (count, 1), 0) + at, ends)
+    lane = lax.broadcasted_iota(jnp.int32, (count, 128), 1)
+    return jnp.where(lane == number, 0.0, -1000000000.0).astype(BF)
+
+
 def attend_kernel(groups, *refs):
     lens_ref, tokens_ref, class_ref = refs[:3]
     vectors, b_inner_ref, (wq_ref, wk_ref, wv_ref) = refs[3 : 3 + VECTORS], refs[3 + VECTORS], refs[4 + VECTORS : 7 + VECTORS]
@@ -687,9 +699,9 @@
     q_ref, k_ref, v_ref, att_ref, lse_ref, w_ref, vec_ref, rows_ref = refs[:8]
     wholes = refs[8 : 8 + DENSE_ARRAYS]
     refs = refs[8 + DENSE_ARRAYS :]
-    x_ref, vt_ref, qkv_shard, qkv_ref, tab_ref, tab_in_ref = refs[:6]
-    local_sem, row_send, row_recv, tab_send, tab_recv, send_sem, recv_sem = refs[6:13]
-    own = refs[13 : 13 + DENSE_ARRAYS]
+    x_ref, vt_ref, marked_ref, qkv_shard, qkv_ref, tab_ref, tab_in_ref = refs[:7]
+    local_sem, row_send, row_recv, tab_send, tab_recv, send_sem, recv_sem = refs[7:14]
+    own = refs[14 : 14 + DENSE_ARRAYS]
     length, width = q_ref.shape
     chunk = 256
     points = length // chunk
@@ -808,13 +820,16 @@
     w_ref[...] = weights
     bias = tab_ref[4, B_QUERY : B_QUERY + 2, pl.ds(pl.multiple_of(group * width, width), width)]
     q_ref[...] = (nn(tokens, weights[:, :width]) + bias[0:1]).astype(BF)
-    k_ref[...] = nn(tokens, weights[:, width : 2 * width]).astype(BF)
+    keys = nn(tokens, weights[:, width : 2 * width]).astype(BF)
+    k_ref[...] = keys
     values = (nn(tokens, weights[:, 2 * width :]) + bias[1:2]).astype(BF)
     v_ref[...] = values
     vt_ref[...] = values.astype(F32).T.astype(BF)
     ends = doc_ends(lens_ref)
-    key_doc = doc_numbers(lax.broadcasted_iota(jnp.int32, (length, 1), 0), ends)
-    lane_head = lax.broadcasted_iota(jnp.int32, (1, width), 1) // HEAD_DIM
+    marks = key_marks(length, ends)
+    for pair in range(width // 128):
+        marked_ref[pair] = jnp.concatenate([keys[:, pair * 128 : (pair + 1) * 128], marks], axis=1)
+    lane_half = lax.broadcasted_iota(jnp.int32, (1, 128), 1) // HEAD_DIM
 
     def step(i, carry):
         for point in range(groups * points):
@@ -825,15 +840,13 @@
                     take_up(point)
 
         at = pl.multiple_of(i * chunk, chunk)
-        query_doc = doc_numbers(lax.broadcasted_iota(jnp.int32, (1, chunk), 1) + at, ends)
+        ours = query_marks(at, chunk, ends)
         scaled = q_ref[pl.ds(at, chunk), :] * jnp.asarray(0.125, BF)
         mixed = []
         for h in range(heads):
-            own_q = jnp.where(lane_head == h, scaled, jnp.zeros_like(scaled))
-            blocks = []
-            for s in range(0, length, chunk):
-                scores = nt(k_ref[s : s + chunk, :], own_q)
-                blocks.append(jnp.where(key_doc[s : s + chunk] == query_doc, scores, -1000000000.0))
+            two = scaled[:, h // 2 * 128 : (h // 2 + 1) * 128]
+            own_q = jnp.concatenate([jnp.where(lane_half == h % 2, two, jnp.zeros_like(two)), ours], axis=1)
+            blocks = [nt(marked_ref[h // 2, s : s + chunk, :], own_q) for s in range(0, length, chunk)]
             peak = functools.reduce(jnp.maximum, [jnp.max(b, axis=0, keepdims=True) for b in blocks])
             exps = [jnp.exp(b - peak) for b in blocks]
             total = functools.reduce(jnp.add, [jnp.sum(e, axis=0, keepdims=True) for e in exps])
@@ -899,6 +912,7 @@
         scratch_shapes=[
             pltpu.VMEM(tokens.shape, BF),
             pltpu.VMEM((group, length), BF),
+            pltpu.VMEM((group // 128, length, 256), BF),
             pltpu.VMEM((groups, share, 3 * group), BF),
             pltpu.VMEM((groups,) + lead + (share, 3 * group), BF),
             pltpu.VMEM((5, VEC_ROWS, width), F32),
@@ -921,25 +935,26 @@
 
 DENSE = 4
 DENSE_ITEMS = (
-    (2, 0, 1, "rows", "yx"), (3, 0, 1, "rows", "xy"),
     (0, 0, 2, "columns", "yx"), (1, 0, 2, "rows", "xy"), (0, 1, 2, "columns", "yx"), (1, 1, 2, "rows", "xy"),
+    (2, 0, 1, "rows", "yx"), (3, 0, 1, "rows", "yx"),
 )
 GROUP_ORDERS = ("yx", "xy", "yx")
 SCATTER_PLAN = {
     -1: ((KB, 0),),
     0: ((KB, 1),),
-    1: ((K0, 0), (K0, 1), (KB, 2), (K1, 0), (K1, 1)),
-    2: ((KB, 3),),
-    3: ((K0, 2), (KB, 4), (K1, 2), (KF, 0), (KF, 1), (K0, 3), (K1, 3), (KB, 5)),
-    4: ((KS, 0), (KS, 1), (KB, 6)),
-    5: ((K0, 4), (K0, 5), (K1, 4), (K1, 5)),
-    6: ((KZ, 0), (KZ, 1)),
-    7: ((KF, 2), (KF, 3)),
-    8: ((KB, 7),),
-    9: ((K0, 6), (K0, 7), (K1, 6), (K1, 7)),
-    10: ((KF, 4), (KS, 2), (KS, 3)),
-    11: ((KF, 5),),
-    12: ((KB, 8), (KX, 0), (KF, 6), (KF, 7), (KT, 0), (KS, 4), (KS, 5), (KZ, 2), (K0, 8), (K1, 8), (KZ, 3), (KT, 1), (KS, 7), (KS, 6), (KF, 8), (KT, 2), (KZ, 7), (KS, 8), (KZ, 4), (KZ, 6), (KZ, 5), (KT, 3), (KZ, 8)),
+    1: ((K0, 0), (K0, 1), (KB, 2), (K1, 0), (KB, 3), (K1, 1)),
+    2: ((KB, 4),),
+    3: ((K0, 2), (K0, 3), (KB, 5), (K1, 2), (K1, 3)),
+    4: ((KF, 0), (KF, 1), (KB, 6)),
+    6: ((K0, 4), (K1, 4)),
+    8: ((KF, 2), (KF, 3), (KS, 0), (KS, 1), (K0, 5), (KB, 7), (K1, 5)),
+    9: ((KF, 4), (K0, 7), (K1, 7)),
+    10: ((K0, 6), (K1, 6)),
+    11: ((KS, 2),),
+    12: (
+        (KS, 4), (KT, 0), (KF, 7), (KS, 3), (KZ, 0), (KZ, 1), (KF, 5), (K0, 8), (K1, 8), (KT, 1), (KF, 6), (KZ, 2), (KS, 7), (KZ, 4),
+        (KS, 5), (KF, 8), (KT, 2), (KS, 6), (KZ, 3), (KZ, 7), (KZ, 5), (KS, 8), (KZ, 6), (KT, 3), (KZ, 8),
+    ),
 }
 PIECES = len(DENSE_ITEMS)
 
@@ -967,9 +982,9 @@
     back_ref, logits_ref, small_ref = refs[18:21]
     dense_outs, group_outs = refs[21 : 21 + DENSE], refs[21 + DENSE : 24 + DENSE]
     rest = refs[24 + DENSE :]
-    xt_ref, kt_ref, dot_ref, dq_ref, dk_ref, dv_ref, acc_ref, dx_ref, bias_ref, dw_ref, tab_ref, tab_in_ref = rest[:12]
-    local_sem, row_send, row_recv, tab_send, tab_recv, send_sem, recv_sem = rest[12:19]
-    rest = rest[19:]
+    xt_ref, kt_ref, marked_ref, dot_ref, dq_ref, dk_ref, dv_ref, acc_ref, dx_ref, bias_ref, dw_ref, tab_ref, tab_in_ref = rest[:13]
+    local_sem, row_send, row_recv, tab_send, tab_recv, send_sem, recv_sem = rest[13:20]
+    rest = rest[20:]
     keeps, rest = rest[:PIECES], rest[PIECES:]
     firsts, seconds, thirds, fourths = (rest[j * items : (j + 1) * items] for j in range(4))
 
@@ -1199,12 +1214,8 @@
                 after_second(a)
             elif kind == KZ:
                 finish(a)
-            elif kind == KT:
+            else:
                 table_level(a)
-            else:
-                for k in (3, 2, 1):
-                    row_copy(0, k).start()
-                row_own(0).start()
 
     @pl.when(group == 0)
     def _():
@@ -1221,7 +1232,10 @@
     dk_ref[...] = jnp.zeros_like(dk_ref)
     dv_ref[...] = jnp.zeros_like(dv_ref)
     ends = doc_ends(lens_ref)
-    key_doc = doc_numbers(lax.broadcasted_iota(jnp.int32, (length, 1), 0), ends)
+    marks = key_marks(length, ends)
+    for pair in range(width // 128):
+        marked_ref[pair] = jnp.concatenate([k_ref[:, pair * 128 : (pair + 1) * 128], marks], axis=1)
+    lane_half = lax.broadcasted_iota(jnp.int32, (1, 128), 1) // HEAD_DIM
     lane_head = lax.broadcasted_iota(jnp.int32, (1, width), 1) // HEAD_DIM
 
     def step(i, carry):
@@ -1232,7 +1246,7 @@
                 take_up(point)
 
         at = pl.multiple_of(i * chunk, chunk)
-        query_doc = doc_numbers(lax.broadcasted_iota(jnp.int32, (1, chunk), 1) + at, ends)
+        ours = query_marks(at, chunk, ends)
         scaled = q_ref[pl.ds(at, chunk), :] * jnp.asarray(0.125, BF)
         given = datt_ref[pl.ds(at, chunk), :]
         own_q = [jnp.where(lane_head == h, scaled, jnp.zeros_like(scaled)) for h in range(heads)]
@@ -1244,10 +1258,11 @@
             dots = jnp.sum(
                 dot_ref[h * HEAD_DIM : (h + 1) * HEAD_DIM, pl.ds(at, chunk)], axis=0, keepdims=True
             )
+            two = scaled[:, h // 2 * 128 : (h // 2 + 1) * 128]
+            marked_q = jnp.concatenate([jnp.where(lane_half == h % 2, two, jnp.zeros_like(two)), ours], axis=1)
             for j in range(length // chunk):
                 s = j * chunk
-                scores = nt(k_ref[s : s + chunk, :], own_q[h])
-                scores = jnp.where(key_doc[s : s + chunk] == query_doc, scores, -1000000000.0)
+                scores = nt(marked_ref[h // 2, s : s + chunk, :], marked_q)
                 probs = jnp.exp(scores - lse)
                 grad_probs = nt(v_ref[s : s + chunk, :], own_d[h])
                 all_grads[j].append((probs * (grad_probs - dots)).astype(BF))
@@ -1273,14 +1288,30 @@
         dw_ref[group, :, :, :, :, :, j * width : (j + 1) * width] = nn(xt, grad).reshape(block + (width,)).astype(BF)
     bias_ref[group, 0:1, :] = jnp.sum(grads[0].astype(F32), axis=0, keepdims=True)
     bias_ref[group, 1:2, :] = jnp.sum(grads[2].astype(F32), axis=0, keepdims=True)
-    total = acc_ref[...]
-    for j, grad in enumerate(grads):
-        total = total + nt(grad, w_ref[:, j * width : (j + 1) * width])
-    acc_ref[...] = total
+
+    @pl.when(group < groups - 1)
+    def _():
+        total = acc_ref[...]
+        for j, grad in enumerate(grads):
+            total = total + nt(grad, w_ref[:, j * width : (j + 1) * width])
+        acc_ref[...] = total
 
     @pl.when(group == groups - 1)
     def _():
-        dx_ref[...] = acc_ref[...].reshape(dx_ref.shape).astype(BF)
+        begin(items - 1)
+        size = dx_ref.shape[1]
+        for k in (3, 2, 1, 0):
+            px, pc = group_partner(k, x, c)
+            block = px * 2 + pc
+            here = pl.ds(pl.multiple_of(block * size, size), size)
+            total = acc_ref[here, :]
+            for j, ref in enumerate((dq_ref, dk_ref, dv_ref)):
+                total = total + nt(ref[here, :].astype(BF), w_ref[:, j * width : (j + 1) * width])
+            dx_ref[block] = total.astype(BF)
+            if k == 0:
+                row_own(0).start()
+            else:
+                row_copy(0, k).start()
         tab_ref[0, 0:CLASSES] = small_a_ref[0:CLASSES]
         for g in range(groups):
             tab_ref[0, B_QUERY : B_QUERY + 2, g * width : (g + 1) * width] = bias_ref[g, 0:2, :]
@@ -1353,6 +1384,7 @@
         scratch_shapes=[
             pltpu.VMEM((width, length), BF),
             pltpu.VMEM((group, length), BF),
+            pltpu.VMEM((group // 128, length, 256), BF),
             pltpu.VMEM((group, length), F32),
             pltpu.VMEM((length, group), BF),
             pltpu.VMEM((length, group), F32),

time: 284 us -> 278 us (0.979)
  Pallas kernels: 260 us -> 254 us
    pallas_call x1, Pallas kernels: 106 us -> 100 us  [attend_back(): pl.pallas_call(functools.partial(attend_back_kernel, groups), grid=(group...]
where the time goes in v6:
time: 278 us
  Pallas kernels  254 us (91%)
  matrix products  20.8 us (7%)
    pallas_call x1, Pallas kernels, attend_back(): pl.pallas_call(functools.partial(attend_back_kernel, groups), grid=(group...  100 us
    pallas_call x1, Pallas kernels, attend(): pl.pallas_call(functools.partial(attend_kernel, groups), grid=(groups,),...  94.6 us
    pallas_call x1, Pallas kernels, middle(): pl.pallas_call(functools.partial(middle_kernel, tiles), grid=(3 * tiles,)...  54.6 us
    dot_general x3, matrix products, tn(): lax.dot_general(a, b, (((0,), (0,)), ((), ())), preferred_element_type=F32)  20.8 us

profile of v6, /device:TPU:0, one launch (start us, length us, event | category | flops | bytes accessed | tf_op | source)
XLA Modules:
  0.0 277.7 jit_solution(463980864655698586)
XLA Ops:
  0.7 94.6 %attend.1 = (bf16[1024,768]{1,0:T(8,128)(2,1)}, bf16[1024,768]{1,0:T(8,128)(2,1)}, bf16[1024,768]{1,0:T(8,128)(2,1)}, bf16[1024,768]{1,0:T(8,128)(2,1)}, f32[3,8...) custom-call(s32[4,4]{1,0:T(4,128)} %refs_0_.5, ...), custom_call_target="tpu_custom_call" | custom-call | tf_op jit(solution)/shard_map/attend/pallas_call | solution.py:888
  95.2 0.0 copy-start
  95.2 54.6 %middle.1 = (bf16[1024,768]{1,0:T(8,128)(2,1)}, bf16[1024,3072]{1,0:T(8,128)(2,1)}, bf16[1024,768]{1,0:T(8,128)(2,1)}, bf16[1024,3072]{1,0:T(8,128)(2,1)}, bf16[...) custom-call(s32[4,4]{1,0:T(4,128)} %refs_0_.5, ...), custom_call_target="tpu_custom_call" | custom-call | tf_op jit(solution)/shard_map/middle/pallas_call | solution.py:1685
  149.9 0.0 copy-done
  149.9 0.0 copy-start.3
  149.9 0.0 slice-start
  149.9 4.0 %convolution_convert_fusion.2 = bf16[768,768]{1,0:T(8,128)(2,1)} fusion(bf16[1024,768]{1,0:T(8,128)(2,1)S(1)} %copy-done, bf16[1024,768]{1,0:T(8,128)(2,1)} %get-tuple-element.97), kind=kOutput, calls=%fused_computation.2 | convolution fusion | flops 1208549376 | bytes 4325376 | tf_op jit(solution)/shard_map/dot_general | solution.py:528
  153.9 0.0 copy-done.3
  153.9 0.0 slice-start.1
  153.9 0.0 copy-start.2
  153.9 9.9 %convolution_convert_fusion.1 = bf16[768,3072]{1,0:T(8,128)(2,1)} fusion(bf16[1024,768]{1,0:T(8,128)(2,1)S(1)} %copy-done.3, bf16[1024,3072]{1,0:T(8,128)(2,1)} %get-tuple-element.94), kind=kOutput, calls=%fused_computation.1 | convolution fusion | flops 4834197504 | bytes 12582912 | tf_op jit(solution)/shard_map/dot_general | solution.py:528
  163.8 0.0 slice-done
  163.8 0.0 slice-done.1
  163.8 0.0 copy-done.2
  163.8 6.9 %convolution_convert_fusion = bf16[3072,768]{1,0:T(8,128)(2,1)} fusion(bf16[1024,3072]{1,0:T(8,128)(2,1)S(1)} %bitcast.57, bf16[1024,768]{1,0:T(8,128)(2,1)S(1)} %copy-done.2), kind=kOutput, calls=%fused_computation | convolution fusion | flops 4834197504 | bytes 12582912 | tf_op jit(solution)/shard_map/dot_general | solution.py:528
  170.7 100.1 %attend_back.1 = (bf16[4,256,768]{2,1,0:T(8,128)(2,1)}, f32[4,8,128]{2,1,0:T(8,128)}, f32[32,128]{1,0:T(8,128)}, f32[24,3072]{1,0:T(8,128)}, f32[96,768]{1,0:T(8...) custom-call(s32[4,4]{1,0:T(4,128)} %refs_0_.5, ...), custom_call_target="tpu_custom_call" | custom-call | tf_op jit(solution)/shard_map/attend_back/pallas_call | solution.py:1365
  270.9 1.3 slice_bitcast_fusion
  272.1 0.0 copy-start.1
  272.1 4.8 %results.1 = (bf16[4,256,768]{2,1,0:T(8,128)(2,1)}, bf16[4,256,768]{2,1,0:T(8,128)(2,1)}, f32[24,3072]{1,0:T(8,128)}, f32[96,768]{1,0:T(8,128)}, f32[24,768]{1,0...) custom-call(f32[32,128]{1,0:T(8,128)} %get-tuple-element.99.small_re, ...), custom_call_target="tpu_custom_call" | custom-call | tf_op jit(solution)/shard_map/results/pallas_call | solution.py:1757
  277.0 0.0 copy-done.1
  277.0 0.7 copy.45
  (2 shorter events, 0.0 us)
Async XLA Ops:
  95.2 54.6 %copy-start = (bf16[1024,768]{1,0:T(8,128)(2,1)S(1)}, bf16[1024,768]{1,0:T(8,128)(2,1)}, u32[]{:S(2)}) copy-start(bf16[1024,768]{1,0:T(8,128)(2,1)} %get-tuple-element.81.refs_5_.refs_6_) | copy-start | bytes 4718596
  149.9 4.0 %copy-start.3 = (bf16[1024,768]{1,0:T(8,128)(2,1)S(1)}, bf16[1024,768]{1,0:T(8,128)(2,1)}, u32[]{:S(2)}) copy-start(bf16[1024,768]{1,0:T(8,128)(2,1)} %get-tuple-element.93) | copy-start | bytes 4718596
  149.9 13.9 %slice-start = ((s8[6291456]{0:T(1024)(128)(4,1)}), s8[4194304]{0:T(1024)(128)(4,1)S(1)}, s32[]{:S(2)}) async-start(s8[6291456]{0:T(1024)(128)(4,1)} %bitcast.56), calls=%async_computation | async-start | bytes 8388608
  153.9 9.9 %slice-start.1 = ((s8[6291456]{0:T(1024)(128)(4,1)}), s8[2097152]{0:T(1024)(128)(4,1)S(1)}, s32[]{:S(2)}) async-start(s8[6291456]{0:T(1024)(128)(4,1)} %bitcast.56), calls=%async_computation.1 | async-start | bytes 4194304
  153.9 9.9 %copy-start.2 = (bf16[1024,768]{1,0:T(8,128)(2,1)S(1)}, bf16[1024,768]{1,0:T(8,128)(2,1)}, u32[]{:S(2)}) copy-start(bf16[1024,768]{1,0:T(8,128)(2,1)} %get-tuple-element.96) | copy-start | bytes 4718596
  272.1 4.8 %copy-start.1 = (f32[4,8,128]{2,1,0:T(8,128)S(1)}, f32[4,8,128]{2,1,0:T(8,128)}, u32[]{:S(2)}) copy-start(f32[4,8,128]{2,1,0:T(8,128)} %get-tuple-element.110) | copy-start | bytes 49156

commit v7 on v6

--- a/solution.py
+++ b/solution.py
@@ -1474,11 +1474,11 @@
         vec_ref,
     ) = refs[:11]
     (
-        low_ref, act_out_ref, outer_ref, inner_ref, branch_ref, datt_ref, gpre_ref, dpool_ref, small_a_ref, small_b_ref, bi_ref,
+        low_ref, act_out_ref, outer_ref, inner_ref, dout_ref, datt_ref, gpre_ref, dpool_ref, small_a_ref, small_b_ref, bi_ref,
         logits_ref, layer_out_ref,
     ) = refs[11:24]
     (
-        act_ref, dact_ref, pre_ref, summed_ref, result_ref, cot_rows_ref, first_ref, picked_ref, own_pool, w_outer_ref, pool_ref,
+        act_ref, dact_ref, pre_ref, summed_ref, dout_acc_ref, result_ref, cot_rows_ref, first_ref, picked_ref, own_pool, w_outer_ref, pool_ref,
         outer_sem, act_sem, keep_sem, send_sem, recv_sem, cot_send, cot_recv, lo_send, lo_recv,
     ) = refs[24:]
     step = pl.program_id(0)
@@ -1646,7 +1646,16 @@
         grad_pre, gain1, shift1 = norm_back(grad_normed, pre_ref[here, :], vec(GAIN1))
         gpre_ref[...] = grad_pre
         branch = grad_pre.astype(BF)
-        branch_ref[...] = branch
+        dout = tn(att_ref[...], branch)
+
+        @pl.when(tile == 0)
+        def _():
+            dout_acc_ref[...] = dout
+
+        @pl.when(tile > 0)
+        def _():
+            dout_acc_ref[...] += dout
+
         datt_ref[...] = nt(branch, w_out_ref[...]).astype(BF)
         small_b_ref[0:1, :] += jnp.sum(outer.astype(F32), axis=0, keepdims=True)
         small_b_ref[1:2, :] += gain2
@@ -1657,6 +1666,7 @@
 
     @pl.when(step == 3 * tiles - 1)
     def _():
+        dout_ref[...] = dout_acc_ref[...].astype(BF)
         all_sent()
         for t in range(tiles):
             act_copy(t).wait()
@@ -1674,6 +1684,8 @@
     items = len(MIDDLE_ORDERS)
     once = pl.Buffered(buffer_count=1)
     early = pl.BlockSpec((tile, width), lambda i: (jnp.minimum(i, tiles - 1), 0))
+
+    twice = pl.BlockSpec((tile, width), lambda i: (jnp.where(i < 2 * tiles, jnp.minimum(i, tiles - 1), i - 2 * tiles), 0))
 
     def late(size):
         return pl.BlockSpec((tile, size), lambda i: (jnp.maximum(i - 2 * tiles, 0), 0))
@@ -1690,7 +1702,7 @@
             jax.ShapeDtypeStruct((length, hidden), BF),
             jax.ShapeDtypeStruct((length, width), BF),
             jax.ShapeDtypeStruct((length, hidden), BF),
-            jax.ShapeDtypeStruct((length, width), BF),
+            jax.ShapeDtypeStruct((width, width), BF),
             jax.ShapeDtypeStruct((length, width), BF),
             jax.ShapeDtypeStruct((length, width), F32),
             jax.ShapeDtypeStruct((width, width), BF),
@@ -1701,11 +1713,11 @@
             jax.ShapeDtypeStruct(cot.shape, BF),
         ],
         in_specs=[
-            SMEM, SMEM, SMEM, ANY, early, early, fixed((width, hidden)), fixed((width, width)), ANY,
+            SMEM, SMEM, SMEM, ANY, early, twice, fixed((width, hidden)), fixed((width, width)), ANY,
             fixed(pool_shard.shape), fixed((VEC_ROWS, width)),
         ],
         out_specs=[
-            early, ANY, late(width), late(hidden), late(width), late(width), late(width), fixed((width, width)),
+            early, ANY, late(width), late(hidden), fixed((width, width)), late(width), late(width), fixed((width, width)),
             fixed((24, width)), fixed((8, width)), fixed((1, hidden)), fixed((8, 128)), ANY,
         ],
         scratch_shapes=[
@@ -1713,6 +1725,7 @@
             pltpu.VMEM((length, hidden), BF),
             pltpu.VMEM((length, width), F32),
             pltpu.VMEM((length, width), F32),
+            pltpu.VMEM((width, width), F32),
             pltpu.VMEM(cot.shape, BF),
             pltpu.VMEM(cot.shape, BF),
             pltpu.VMEM((VEC_ROWS, width), F32),
@@ -1784,12 +1797,11 @@
     rows = rows.reshape(length, width)
     full_inner = full_inner.reshape(width, hidden)
     full_out = full_out.reshape(width, width)
-    low, act, outer, inner, branch, datt, grad_pre, grad_pool, small_a, small_b, grad_b_inner, logit_block, layer_out = middle(
+    low, act, outer, inner, grad_out_w, datt, grad_pre, grad_pool, small_a, small_b, grad_b_inner, logit_block, layer_out = middle(
         doc_lengths, labels, b_class, cotangent, rows, att, full_inner, full_out, full_outer, w_pool, vectors
     )
     grad_outer_w = tn(act, outer).astype(BF)
     grad_inner_w = tn(low, inner).astype(BF)
-    grad_out_w = tn(att, branch).astype(BF)
     grad_inputs, all_logits, small, *sums = attend_back(
         doc_lengths, rows, w_qkv, q, k, v, att, datt, lse, grad_pre, small_a, small_b, grad_b_inner, logit_block,
         [

time: 278 us -> 278 us (level)
  matrix products: 20.8 us -> 16.4 us
  Pallas kernels: 254 us -> 258 us
    dot_general x3 -> x2, matrix products: 20.8 us -> 16.4 us  [tn(): lax.dot_general(a, b, (((0,), (0,)), ((), ())), preferred_element_type=F32)]
    pallas_call x1, Pallas kernels: 54.6 us -> 58.6 us  [middle(): pl.pallas_call(functools.partial(middle_kernel, tiles), grid=(3 * tiles,)...]
where the time goes in v7:
time: 278 us; the launch traced here: 277 us
  Pallas kernels  258 us (93%)
  matrix products  16.4 us (6%)
    pallas_call x1, Pallas kernels, attend_back(): pl.pallas_call(functools.partial(attend_back_kernel, groups), grid=(group...  100 us
    pallas_call x1, Pallas kernels, attend(): pl.pallas_call(functools.partial(attend_kernel, groups), grid=(groups,),...  94.6 us
    pallas_call x1, Pallas kernels, middle(): pl.pallas_call(functools.partial(middle_kernel, tiles), grid=(3 * tiles,)...  58.6 us
    dot_general x2, matrix products, tn(): lax.dot_general(a, b, (((0,), (0,)), ((), ())), preferred_element_type=F32)  16.4 us

profile of v7, /device:TPU:0, one launch (start us, length us, event | category | flops | bytes accessed | tf_op | source)
XLA Modules:
  0.0 277.3 jit_solution(15016247541074110655)
XLA Ops:
  0.7 94.6 %attend.1 = (bf16[1024,768]{1,0:T(8,128)(2,1)}, bf16[1024,768]{1,0:T(8,128)(2,1)}, bf16[1024,768]{1,0:T(8,128)(2,1)}, bf16[1024,768]{1,0:T(8,128)(2,1)}, f32[3,8...) custom-call(s32[4,4]{1,0:T(4,128)} %refs_0_.5, ...), custom_call_target="tpu_custom_call" | custom-call | tf_op jit(solution)/shard_map/attend/pallas_call | solution.py:888
  95.3 58.6 %middle.1 = (bf16[1024,768]{1,0:T(8,128)(2,1)}, bf16[1024,3072]{1,0:T(8,128)(2,1)}, bf16[1024,768]{1,0:T(8,128)(2,1)}, bf16[1024,3072]{1,0:T(8,128)(2,1)}, bf16[...) custom-call(s32[4,4]{1,0:T(4,128)} %refs_0_.5, ...), custom_call_target="tpu_custom_call" | custom-call | tf_op jit(solution)/shard_map/middle/pallas_call | solution.py:1697
  153.9 0.0 copy-start.1
  154.0 0.0 copy-start.2
  154.0 9.5 %convolution_convert_fusion.1 = bf16[768,3072]{1,0:T(8,128)(2,1)} fusion(bf16[1024,768]{1,0:T(8,128)(2,1)} %get-tuple-element.93, bf16[1024,3072]{1,0:T(8,128)(2,1)} %get-tuple-element.94), kind=kOutput, calls=%fused_computation.1 | convolution fusion | flops 4834197504 | bytes 12582912 | tf_op jit(solution)/shard_map/dot_general | solution.py:528
  163.5 0.0 copy-done.1
  163.5 0.0 copy-done.2
  163.5 6.9 %convolution_convert_fusion = bf16[3072,768]{1,0:T(8,128)(2,1)} fusion(bf16[1024,3072]{1,0:T(8,128)(2,1)S(1)} %copy-done.1, bf16[1024,768]{1,0:T(8,128)(2,1)S(1)} %copy-done.2), kind=kOutput, calls=%fused_computation | convolution fusion | flops 4834197504 | bytes 12582912 | tf_op jit(solution)/shard_map/dot_general | solution.py:528
  170.4 100.1 %attend_back.1 = (bf16[4,256,768]{2,1,0:T(8,128)(2,1)}, f32[4,8,128]{2,1,0:T(8,128)}, f32[32,128]{1,0:T(8,128)}, f32[24,3072]{1,0:T(8,128)}, f32[96,768]{1,0:T(8...) custom-call(s32[4,4]{1,0:T(4,128)} %refs_0_.5, ...), custom_call_target="tpu_custom_call" | custom-call | tf_op jit(solution)/shard_map/attend_back/pallas_call | solution.py:1365
  270.5 1.3 slice_bitcast_fusion
  271.8 0.0 copy-start
  271.8 4.8 %results.1 = (bf16[4,256,768]{2,1,0:T(8,128)(2,1)}, bf16[4,256,768]{2,1,0:T(8,128)(2,1)}, f32[24,3072]{1,0:T(8,128)}, f32[96,768]{1,0:T(8,128)}, f32[24,768]{1,0...) custom-call(f32[32,128]{1,0:T(8,128)} %get-tuple-element.99.small_re, ...), custom_call_target="tpu_custom_call" | custom-call | tf_op jit(solution)/shard_map/results/pallas_call | solution.py:1770
  276.6 0.0 copy-done
  276.6 0.7 copy.45
  (1 shorter events, 0.0 us)
Async XLA Ops:
  153.9 9.5 %copy-start.1 = (bf16[1024,3072]{1,0:T(8,128)(2,1)S(1)}, bf16[1024,3072]{1,0:T(8,128)(2,1)}, u32[]{:S(2)}) copy-start(bf16[1024,3072]{1,0:T(8,128)(2,1)} %get-tuple-element.95) | copy-start | bytes 18874372
  154.0 9.5 %copy-start.2 = (bf16[1024,768]{1,0:T(8,128)(2,1)S(1)}, bf16[1024,768]{1,0:T(8,128)(2,1)}, u32[]{:S(2)}) copy-start(bf16[1024,768]{1,0:T(8,128)(2,1)} %get-tuple-element.96) | copy-start | bytes 4718596
  271.8 4.8 %copy-start = (f32[4,8,128]{2,1,0:T(8,128)S(1)}, f32[4,8,128]{2,1,0:T(8,128)}, u32[]{:S(2)}) copy-start(f32[4,8,128]{2,1,0:T(8,128)} %get-tuple-element.110) | copy-start | bytes 49156

commit v8 on v7

--- a/solution.py
+++ b/solution.py
@@ -1059,7 +1059,7 @@
             target[where] = target[where] + source[where]
             return carry
 
-        lax.fori_loop(0, total, step, 0)
+        lax.fori_loop(0, total, step, 0, unroll=True)
 
     def begin(a):
         if a < PIECES:

time: 278 us -> 277 us (level)
  no operation moved by 1% of the time
where the time goes in v8:
time: 277 us
  Pallas kernels  258 us (93%)
  matrix products  16.4 us (6%)
    pallas_call x1, Pallas kernels, attend_back(): pl.pallas_call(functools.partial(attend_back_kernel, groups), grid=(group...  99.5 us
    pallas_call x1, Pallas kernels, attend(): pl.pallas_call(functools.partial(attend_kernel, groups), grid=(groups,),...  94.6 us
    pallas_call x1, Pallas kernels, middle(): pl.pallas_call(functools.partial(middle_kernel, tiles), grid=(3 * tiles,)...  58.6 us
    dot_general x2, matrix products, tn(): lax.dot_general(a, b, (((0,), (0,)), ((), ())), preferred_element_type=F32)  16.4 us

profile of v8, /device:TPU:0, one launch (start us, length us, event | category | flops | bytes accessed | tf_op | source)
XLA Modules:
  0.0 276.7 jit_solution(14801643850170784576)
XLA Ops:
  0.7 94.6 %attend.1 = (bf16[1024,768]{1,0:T(8,128)(2,1)}, bf16[1024,768]{1,0:T(8,128)(2,1)}, bf16[1024,768]{1,0:T(8,128)(2,1)}, bf16[1024,768]{1,0:T(8,128)(2,1)}, f32[3,8...) custom-call(s32[4,4]{1,0:T(4,128)} %refs_0_.5, ...), custom_call_target="tpu_custom_call" | custom-call | tf_op jit(solution)/shard_map/attend/pallas_call | solution.py:888
  95.3 58.6 %middle.1 = (bf16[1024,768]{1,0:T(8,128)(2,1)}, bf16[1024,3072]{1,0:T(8,128)(2,1)}, bf16[1024,768]{1,0:T(8,128)(2,1)}, bf16[1024,3072]{1,0:T(8,128)(2,1)}, bf16[...) custom-call(s32[4,4]{1,0:T(4,128)} %refs_0_.5, ...), custom_call_target="tpu_custom_call" | custom-call | tf_op jit(solution)/shard_map/middle/pallas_call | solution.py:1697
  153.9 0.0 copy-start.1
  154.0 0.0 copy-start.2
  154.0 9.5 %convolution_convert_fusion.1 = bf16[768,3072]{1,0:T(8,128)(2,1)} fusion(bf16[1024,768]{1,0:T(8,128)(2,1)} %get-tuple-element.93, bf16[1024,3072]{1,0:T(8,128)(2,1)} %get-tuple-element.94), kind=kOutput, calls=%fused_computation.1 | convolution fusion | flops 4834197504 | bytes 12582912 | tf_op jit(solution)/shard_map/dot_general | solution.py:528
  163.5 0.0 copy-done.1
  163.5 0.0 copy-done.2
  163.5 6.9 %convolution_convert_fusion = bf16[3072,768]{1,0:T(8,128)(2,1)} fusion(bf16[1024,3072]{1,0:T(8,128)(2,1)S(1)} %copy-done.1, bf16[1024,768]{1,0:T(8,128)(2,1)S(1)} %copy-done.2), kind=kOutput, calls=%fused_computation | convolution fusion | flops 4834197504 | bytes 12582912 | tf_op jit(solution)/shard_map/dot_general | solution.py:528
  170.4 99.5 %attend_back.1 = (bf16[4,256,768]{2,1,0:T(8,128)(2,1)}, f32[4,8,128]{2,1,0:T(8,128)}, f32[32,128]{1,0:T(8,128)}, f32[24,3072]{1,0:T(8,128)}, f32[96,768]{1,0:T(8...) custom-call(s32[4,4]{1,0:T(4,128)} %refs_0_.5, ...), custom_call_target="tpu_custom_call" | custom-call | tf_op jit(solution)/shard_map/attend_back/pallas_call | solution.py:1365
  269.9 1.3 slice_bitcast_fusion
  271.2 0.0 copy-start
  271.2 4.8 %results.1 = (bf16[4,256,768]{2,1,0:T(8,128)(2,1)}, bf16[4,256,768]{2,1,0:T(8,128)(2,1)}, f32[24,3072]{1,0:T(8,128)}, f32[96,768]{1,0:T(8,128)}, f32[24,768]{1,0...) custom-call(f32[32,128]{1,0:T(8,128)} %get-tuple-element.99.small_re, ...), custom_call_target="tpu_custom_call" | custom-call | tf_op jit(solution)/shard_map/results/pallas_call | solution.py:1770
  276.0 0.0 copy-done
  276.0 0.7 copy.45
  (1 shorter events, 0.0 us)
Async XLA Ops:
  153.9 9.5 %copy-start.1 = (bf16[1024,3072]{1,0:T(8,128)(2,1)S(1)}, bf16[1024,3072]{1,0:T(8,128)(2,1)}, u32[]{:S(2)}) copy-start(bf16[1024,3072]{1,0:T(8,128)(2,1)} %get-tuple-element.95) | copy-start | bytes 18874372
  154.0 9.5 %copy-start.2 = (bf16[1024,768]{1,0:T(8,128)(2,1)S(1)}, bf16[1024,768]{1,0:T(8,128)(2,1)}, u32[]{:S(2)}) copy-start(bf16[1024,768]{1,0:T(8,128)(2,1)} %get-tuple-element.96) | copy-start | bytes 4718596
  271.2 4.8 %copy-start = (f32[4,8,128]{2,1,0:T(8,128)S(1)}, f32[4,8,128]{2,1,0:T(8,128)}, u32[]{:S(2)}) copy-start(f32[4,8,128]{2,1,0:T(8,128)} %get-tuple-element.110) | copy-start | bytes 49156
